TPU v7x, 256 devices: a whole 4x4x8 slice. The times are simulated.
256 devices in a mesh: doc: 2 (over core), seq: 32 (over x, z), head: 4 (over y).
Axes of the slice: x: 4, y: 4, z: 8, core: 2. Of those that a mesh axis runs over, the one named last changes fastest.
Arguments:
- att_query: bfloat16 [65536, 2048], P(('doc', 'seq'), 'head'), parts along dimension 0, may hold values from -12 to 12
- att_key: bfloat16 [65536, 2048], P(('doc', 'seq'), 'head'), parts along dimension 0, may hold values from -12 to 12
- att_value: bfloat16 [65536, 2048], P(('doc', 'seq'), 'head'), parts along dimension 0, may hold values from -6 to 6
- delta_query: bfloat16 [65536, 2048], P(('doc', 'seq'), 'head'), parts along dimension 0, may hold values from -6 to 6
- delta_key: bfloat16 [65536, 2048], P(('doc', 'seq'), 'head'), parts along dimension 0, may hold values from -6 to 6
- out_gate: bfloat16 [65536, 2048], P(('doc', 'seq'), 'head'), parts along dimension 0, may hold values from -6 to 6
- log_decay: float32 [16, 65536], P('head', ('doc', 'seq')), parts along dimension 1, may hold values from -1 to 0
- beta: float32 [16, 65536], P('head', ('doc', 'seq')), parts along dimension 1, may hold values from 0 to 1
- norm_gain: float32 [128], replicated, may hold values from 0.1 to 1.9
Outputs:
- layer_output: bfloat16 [65536, 2048], P(('doc', 'seq'), 'head'), parts along dimension 0
There are 2 independent parts, one for each index of `doc`. A program takes and returns all parts, laid end to end along the dimension named above; an argument that names none is the same for every part. Nothing has to cross between parts.
All inputs are finite; a program needn't handle non-finite values.
Results may differ from a plain program's by a relative error of at most 0.0057.
Values may be sent and summed in bfloat16 or wider, within the bound.
No kernel may reach another device: no remote copies, remote signals or barrier semaphores. Data moves between devices by JAX's collectives and lax.ppermute only.
A program may use at most 128 MiB of HBM per device.

v0:
```python
import math

import jax
import jax.numpy as jnp
from jax import lax
from jax.sharding import PartitionSpec as P

WINDOW = 1024
GROUP = 64


PRECISE = lax.Precision.HIGHEST


def passed_along(value, axis, steps):
    count = lax.axis_size(axis)
    leading, last = (max(0, -steps), min(count, count - steps))
    return lax.ppermute(value, axis, [(source, source + steps) for source in range(leading, last)])


def unit_rows(tensor):
    return tensor / jnp.sqrt(jnp.sum(tensor * tensor, axis=-1, keepdims=True) + 1e-06)


def rms_rows(tensor):
    return tensor / jnp.sqrt(jnp.mean(tensor * tensor, axis=-1, keepdims=True) + 1e-06)


def batched_product(left_side, right_side):
    return jnp.einsum("hij,hjk->hik", left_side, right_side, precision=PRECISE)


def window_attention(query_rows, key_ext, value_ext, first_place):
    local_row_count = query_rows.shape[0]
    block_rows = min(512, local_row_count)
    scale = 1.0 / math.sqrt(query_rows.shape[2])
    outputs = []
    for block_index in range(local_row_count // block_rows):
        first_row = block_index * block_rows
        query_block = query_rows[first_row : first_row + block_rows]
        key_block = key_ext[first_row : first_row + block_rows + WINDOW]
        value_block = value_ext[first_row : first_row + block_rows + WINDOW]
        offsets = (
            jnp.arange(block_rows)[:, None] + WINDOW - jnp.arange(block_rows + WINDOW)[None, :]
        )
        key_place = first_place + first_row - WINDOW + jnp.arange(block_rows + WINDOW)
        allowed = (offsets >= 0) & (offsets < WINDOW) & (key_place[None, :] >= 0)
        scores = (
            jnp.einsum("qhd,khd->hqk", query_block, key_block, preferred_element_type=jnp.float32)
            * scale
        )
        masked = jnp.where(allowed[None], scores, -1e30)
        summit = jnp.max(masked, axis=-1, keepdims=True)
        powered = jnp.where(allowed[None], jnp.exp(masked - summit), 0.0)
        denominator = jnp.sum(powered, axis=-1)
        weights = powered.astype(jnp.bfloat16)
        blended = jnp.einsum(
            "hqk,khd->qhd", weights, value_block, preferred_element_type=jnp.float32
        )
        blended = blended / jnp.transpose(denominator)[:, :, None]
        outputs.append(blended.astype(jnp.bfloat16))
    return jnp.concatenate(outputs, axis=0)


def group_kernel(key_rows, value_rows, logarithmic_forgetting, beta_rows):
    length = logarithmic_forgetting.shape[-1]
    key_width = key_rows.shape[-1]
    cumlog = jnp.cumsum(logarithmic_forgetting, axis=-1)
    log_gaps = cumlog[:, :, None] - cumlog[:, None, :]
    lower_mask = jnp.tril(jnp.ones((length, length), bool))
    strict_mask = jnp.tril(jnp.ones((length, length), bool), -1)
    decay_mask = jnp.where(lower_mask, jnp.exp(jnp.where(lower_mask, log_gaps, 0.0)), 0.0)
    intersection = jnp.einsum("htd,hjd->htj", key_rows, key_rows, precision=PRECISE)
    system = jnp.eye(length, dtype=jnp.float32) + jnp.where(
        strict_mask, beta_rows[:, :, None] * decay_mask * intersection, 0.0
    )
    right_side = jnp.concatenate(
        [(beta_rows * jnp.exp(cumlog))[..., None] * key_rows, beta_rows[..., None] * value_rows],
        axis=-1,
    )
    solved = jax.scipy.linalg.solve_triangular(system, right_side, lower=True, unit_diagonal=True)
    tail_decay = jnp.exp(cumlog[:, -1:] - cumlog)
    return (cumlog, decay_mask, solved[..., :key_width], solved[..., key_width:], tail_decay)


def body(
    att_query, att_key, att_value, delta_query, delta_key, out_gate, log_decay, beta, norm_gain
):
    local_row_count = att_query.shape[0]
    heads_here = log_decay.shape[0]
    head_size = norm_gain.shape[0]
    shape_three = (local_row_count, heads_here, head_size)
    tail_rows = jnp.stack([att_key, att_value])
    earlier = passed_along(tail_rows, "seq", 1)
    key_ext = jnp.concatenate([earlier[0], att_key], axis=0).reshape(
        WINDOW + local_row_count, heads_here, head_size
    )
    value_ext = jnp.concatenate([earlier[1], att_value], axis=0).reshape(
        WINDOW + local_row_count, heads_here, head_size
    )
    first_place = lax.axis_index("seq") * local_row_count
    attended = window_attention(att_query.reshape(shape_three), key_ext, value_ext, first_place)
    values = rms_rows(attended.astype(jnp.float32))
    unit_keys = unit_rows(delta_key.reshape(shape_three).astype(jnp.float32))
    unit_queries = unit_rows(delta_query.reshape(shape_three).astype(jnp.float32))
    group_count = local_row_count // GROUP

    def to_groups(tensor):
        return tensor.reshape(group_count, GROUP, heads_here, head_size).transpose(0, 2, 1, 3)

    key_groups = to_groups(unit_keys)
    value_groups = to_groups(values)
    query_groups = to_groups(unit_queries)
    log_groups = log_decay.reshape(heads_here, group_count, GROUP).transpose(1, 0, 2)
    beta_groups = beta.reshape(heads_here, group_count, GROUP).transpose(1, 0, 2)
    cumlog, decay_mask, weight_part, source_part, tail_decay = jax.vmap(group_kernel)(
        key_groups, value_groups, log_groups, beta_groups
    )
    identity_mat = jnp.broadcast_to(
        jnp.eye(head_size, dtype=jnp.float32), (heads_here, head_size, head_size)
    )
    group_decay = jnp.exp(cumlog[:, :, -1])[..., None, None] * identity_mat[None] - jnp.einsum(
        "nhcd,nhce->nhde", weight_part * tail_decay[..., None], key_groups, precision=PRECISE
    )
    group_source = jnp.einsum(
        "nhcv,nhce->nhve", source_part * tail_decay[..., None], key_groups, precision=PRECISE
    )

    def compose(carried, pair):
        decay_acc, source_acc = carried
        decay_new, source_new = pair
        return (
            (
                batched_product(decay_acc, decay_new),
                batched_product(source_acc, decay_new) + source_new,
            ),
            None,
        )

    zero_state = jnp.zeros((heads_here, head_size, head_size), jnp.float32)
    (span_decay, span_source), unused = lax.scan(
        compose, (identity_mat, zero_state), (group_decay, group_source)
    )

    def advance(step_index, incoming):
        return passed_along(batched_product(incoming, span_decay) + span_source, "seq", 1)

    incoming = lax.fori_loop(0, lax.axis_size("seq") - 1, advance, zero_state)

    def emit_group(carried, pieces):
        cum_row, mask_row, weight_row, source_row, tail_row, query_row, key_row = pieces
        new_values = source_row - jnp.einsum("hcd,hvd->hcv", weight_row, carried, precision=PRECISE)
        scores = jnp.einsum("htd,hjd->htj", query_row, key_row, precision=PRECISE) * mask_row
        readout = jnp.exp(cum_row)[..., None] * jnp.einsum(
            "hcd,hvd->hcv", query_row, carried, precision=PRECISE
        )
        readout = readout + jnp.einsum("htj,hjv->htv", scores, new_values, precision=PRECISE)
        carried = jnp.exp(cum_row[:, -1])[:, None, None] * carried + jnp.einsum(
            "hcv,hcd->hvd", new_values * tail_row[..., None], key_row, precision=PRECISE
        )
        return (carried, readout)

    final_state, readouts = lax.scan(
        emit_group,
        incoming,
        (cumlog, decay_mask, weight_part, source_part, tail_decay, query_groups, key_groups),
    )
    readouts = readouts.transpose(0, 2, 1, 3).reshape(shape_three)
    gates = jax.nn.silu(out_gate.reshape(shape_three).astype(jnp.float32))
    rescaled_output = rms_rows(readouts) * norm_gain * gates
    return rescaled_output.reshape(local_row_count, heads_here * head_size).astype(jnp.bfloat16)


def solution(mesh):
    return jax.shard_map(
        body,
        mesh=mesh,
        in_specs=(
            P(("doc", "seq"), "head"),
            P(("doc", "seq"), "head"),
            P(("doc", "seq"), "head"),
            P(("doc", "seq"), "head"),
            P(("doc", "seq"), "head"),
            P(("doc", "seq"), "head"),
            P("head", ("doc", "seq")),
            P("head", ("doc", "seq")),
            P(),
        ),
        out_specs=P(("doc", "seq"), "head"),
        check_vma=False,
    )
```

profile of v0, /device:TPU:18, one launch (start us, length us, event | category | flops | bytes accessed | tf_op | source)
XLA Modules:
  0.0 949.6 jit_solution(16166616895039469077)
XLA Ops:
  33.7 316.0 %custom-call.4 = f32[16,4,1,64,64]{3,4,2,1,0:T(8,128)} custom-call(f32[16,4,1,64,64]{4,3,2,1,0:T(8,128)} %add_bitcast_fusion), custom_call_target="InvertDiagBlocksLowerTriangular" | custom-call | tf_op jit(solution)/shard_map/vmap(jit(_solve_triangular))/vmap()/triangular_solve | solution.py:81
  367.6 11.0 %fusion.103 = (f32[4,512]{1,0:T(4,128)}, bf16[4,512,1536]{1,2,0:T(8,128)(2,1)}) fusion(pred[512,1536]{0,1:T(8,128)(4,1)S(1)} %get-tuple-element.295, bf16[1536,4,128]{0,2,1:T(8,128)(2,1)} %bitcast.214, bf16[512,4,128]{0,2,1:T(8,128)(2,1)} %bitcast.216), kind=kOutput, calls=%fused_computation.148 | convolution fusion | flops 824182272 | bytes 9183232 | tf_op jit(solution)/shard_map/sub | solution.py:54
  382.8 11.1 %fusion.102 = (f32[4,512]{1,0:T(4,128)}, bf16[4,512,1536]{1,2,0:T(8,128)(2,1)}) fusion(pred[512,1536]{0,1:T(8,128)(4,1)} %get-tuple-element.296, bf16[1536,4,128]{0,2,1:T(8,128)(2,1)} %bitcast.212, bf16[512,4,128]{0,2,1:T(8,128)(2,1)S(1)} %bitcast.215), kind=kOutput, calls=%fused_computation.147 | convolution fusion | flops 824182272 | bytes 9183232 | tf_op jit(solution)/shard_map/sub | solution.py:54
  412.7 9.0 fusion.55
  421.7 9.5 multiply_subtract_fusion
  431.2 52.4 %while.37 = (s32[]{:T(128)}, f32[4,128,128]{1,2,0:T(8,128)S(1)}, f32[4,128,128]{1,2,0:T(8,128)S(1)}, f32[16,4,128,128]{3,2,1,0:T(8,128)}, f32[16,4,128,128]{2,3,1,0:T(8,128)}, /*index=5*/s32[]{:T(128)}, s32[]{:T(128)}) while((s32[]{:T(128)}, f32[4,128,128]{1,2,0:T(8,128)S(1)}, f32[4,128,128]{1,2,0:T(8,128)S(1)}, ...), condition=%wide.region_8.9_spmd.clone, body=%wide.region_7.8_spmd.clone.sunk | while | flops 201457664 | bytes 2885207 | solution.py:141
  484.0 358.0 %while.35 = (s32[]{:T(128)}, f32[4,128,128]{2,1,0:T(8,128)S(1)}, f32[4,128,128]{2,1,0:T(8,128)S(1)}, f32[4,128,128]{2,1,0:T(8,128)S(1)}, s32[]{:T(128)}) while((s32[]{:T(128)}, f32[4,128,128]{2,1,0:T(8,128)S(1)}, f32[4,128,128]{2,1,0:T(8,128)S(1)}, f32[4,128,128]{2,1,0:T(8,128)S(1)}, s32[]{:T(128)}) %tuple.86), condition=%wide.region_10.11_spmd, body=%wide.region_9.10_spmd.sunk | while | flops 100728832 | bytes 2097253 | solution.py:148
  498.9 9.3 collective-permute-done
  510.6 8.4 collective-permute-done
  521.3 8.4 collective-permute-done
  532.1 8.4 collective-permute-done
  542.9 8.4 collective-permute-done
  553.7 9.0 collective-permute-done
  565.0 10.1 %collective-permute-done = f32[4,128,128]{2,1,0:T(8,128)S(1)} collective-permute-done((f32[4,128,128]{2,1,0:T(8,128)S(1)}, f32[4,128,128]{2,1,0:T(8,128)S(1)}, u32[]{:S(2)}, u32[]{:S(2)}) %collective-permute-start) | collective-permute-done | bytes 262176 | tf_op jit(solution)/shard_map/while/body/eval_jaxpr/ppermute | solution.py:18
  577.4 11.2 %collective-permute-done = f32[4,128,128]{2,1,0:T(8,128)S(1)} collective-permute-done((f32[4,128,128]{2,1,0:T(8,128)S(1)}, f32[4,128,128]{2,1,0:T(8,128)S(1)}, u32[]{:S(2)}, u32[]{:S(2)}) %collective-permute-start) | collective-permute-done | bytes 262176 | tf_op jit(solution)/shard_map/while/body/eval_jaxpr/ppermute | solution.py:18
  591.0 10.4 %collective-permute-done = f32[4,128,128]{2,1,0:T(8,128)S(1)} collective-permute-done((f32[4,128,128]{2,1,0:T(8,128)S(1)}, f32[4,128,128]{2,1,0:T(8,128)S(1)}, u32[]{:S(2)}, u32[]{:S(2)}) %collective-permute-start) | collective-permute-done | bytes 262176 | tf_op jit(solution)/shard_map/while/body/eval_jaxpr/ppermute | solution.py:18
  603.8 9.6 %collective-permute-done = f32[4,128,128]{2,1,0:T(8,128)S(1)} collective-permute-done((f32[4,128,128]{2,1,0:T(8,128)S(1)}, f32[4,128,128]{2,1,0:T(8,128)S(1)}, u32[]{:S(2)}, u32[]{:S(2)}) %collective-permute-start) | collective-permute-done | bytes 262176 | tf_op jit(solution)/shard_map/while/body/eval_jaxpr/ppermute | solution.py:18
  615.7 8.6 collective-permute-done
  637.4 8.4 collective-permute-done
  648.2 8.4 collective-permute-done
  659.0 8.5 collective-permute-done
  669.8 9.6 %collective-permute-done = f32[4,128,128]{2,1,0:T(8,128)S(1)} collective-permute-done((f32[4,128,128]{2,1,0:T(8,128)S(1)}, f32[4,128,128]{2,1,0:T(8,128)S(1)}, u32[]{:S(2)}, u32[]{:S(2)}) %collective-permute-start) | collective-permute-done | bytes 262176 | tf_op jit(solution)/shard_map/while/body/eval_jaxpr/ppermute | solution.py:18
  681.8 10.8 %collective-permute-done = f32[4,128,128]{2,1,0:T(8,128)S(1)} collective-permute-done((f32[4,128,128]{2,1,0:T(8,128)S(1)}, f32[4,128,128]{2,1,0:T(8,128)S(1)}, u32[]{:S(2)}, u32[]{:S(2)}) %collective-permute-start) | collective-permute-done | bytes 262176 | tf_op jit(solution)/shard_map/while/body/eval_jaxpr/ppermute | solution.py:18
  695.0 10.5 %collective-permute-done = f32[4,128,128]{2,1,0:T(8,128)S(1)} collective-permute-done((f32[4,128,128]{2,1,0:T(8,128)S(1)}, f32[4,128,128]{2,1,0:T(8,128)S(1)}, u32[]{:S(2)}, u32[]{:S(2)}) %collective-permute-start) | collective-permute-done | bytes 262176 | tf_op jit(solution)/shard_map/while/body/eval_jaxpr/ppermute | solution.py:18
  707.8 9.7 %collective-permute-done = f32[4,128,128]{2,1,0:T(8,128)S(1)} collective-permute-done((f32[4,128,128]{2,1,0:T(8,128)S(1)}, f32[4,128,128]{2,1,0:T(8,128)S(1)}, u32[]{:S(2)}, u32[]{:S(2)}) %collective-permute-start) | collective-permute-done | bytes 262176 | tf_op jit(solution)/shard_map/while/body/eval_jaxpr/ppermute | solution.py:18
  719.9 8.8 collective-permute-done
  731.0 8.4 collective-permute-done
  741.8 8.4 collective-permute-done
  774.1 9.5 %collective-permute-done = f32[4,128,128]{2,1,0:T(8,128)S(1)} collective-permute-done((f32[4,128,128]{2,1,0:T(8,128)S(1)}, f32[4,128,128]{2,1,0:T(8,128)S(1)}, u32[]{:S(2)}, u32[]{:S(2)}) %collective-permute-start) | collective-permute-done | bytes 262176 | tf_op jit(solution)/shard_map/while/body/eval_jaxpr/ppermute | solution.py:18
  786.0 10.7 %collective-permute-done = f32[4,128,128]{2,1,0:T(8,128)S(1)} collective-permute-done((f32[4,128,128]{2,1,0:T(8,128)S(1)}, f32[4,128,128]{2,1,0:T(8,128)S(1)}, u32[]{:S(2)}, u32[]{:S(2)}) %collective-permute-start) | collective-permute-done | bytes 262176 | tf_op jit(solution)/shard_map/while/body/eval_jaxpr/ppermute | solution.py:18
  799.0 10.6 %collective-permute-done = f32[4,128,128]{2,1,0:T(8,128)S(1)} collective-permute-done((f32[4,128,128]{2,1,0:T(8,128)S(1)}, f32[4,128,128]{2,1,0:T(8,128)S(1)}, u32[]{:S(2)}, u32[]{:S(2)}) %collective-permute-start) | collective-permute-done | bytes 262176 | tf_op jit(solution)/shard_map/while/body/eval_jaxpr/ppermute | solution.py:18
  842.0 100.0 %while.36 = (s32[]{:T(128)}, f32[4,128,128]{2,1,0:T(8,128)S(1)}, f32[16,4,64,128]{3,2,1,0:T(8,128)}, f32[16,4,64]{2,0,1:T(8,128)S(1)}, f32[16,4,64,128]{3,2,1,0:...) while((s32[]{:T(128)}, f32[4,128,128]{2,1,0:T(8,128)S(1)}, ...), condition=%wide.region_13.14_spmd, body=%wide.region_12.13_spmd.sunk | while | flops 201605120 | bytes 3162269 | solution.py:163
  (439 shorter events, 365.3 us)
Async XLA Ops:
  3.8 358.9 %collective-permute-start.1 = (bf16[2,1024,512]{1,2,0:T(8,128)(2,1)}, bf16[2,1024,512]{1,2,0:T(8,128)(2,1)}, u32[]{:S(2)}, u32[]{:S(2)}) collective-permute-start(bf16[2,1024,512]{1,2,0:T(8,128)(2,1)} %pad_maximum_fusion), channel_id=1, source_target_pairs={{0,4},{4,8},{8,12},{12,16},{16,20},{20,24},{24,28},{28,32},{32,36}... | collective-permute-start | bytes 6291464 | tf_op jit(solution)/shard_map/ppermute | solution.py:18
  484.4 12.1 %collective-permute-start = (f32[4,128,128]{2,1,0:T(8,128)S(1)}, f32[4,128,128]{2,1,0:T(8,128)S(1)}, u32[]{:S(2)}, u32[]{:S(2)}) collective-permute-start(f32[4,128,128]{2,1,0:T(8,128)S(1)} %convolution_add_fusion.4), channel_id=1, source_target_pairs={{0,4},{4,8},{8,12},{12,16},{16,20},{20,24},{24,28},{28,32},{32,36}... | collective-permute-start | bytes 786440 | tf_op jit(solution)/shard_map/while/body/eval_jaxpr/ppermute | solution.py:18
  496.9 11.3 %collective-permute-start = (f32[4,128,128]{2,1,0:T(8,128)S(1)}, f32[4,128,128]{2,1,0:T(8,128)S(1)}, u32[]{:S(2)}, u32[]{:S(2)}) collective-permute-start(f32[4,128,128]{2,1,0:T(8,128)S(1)} %convolution_add_fusion.4), channel_id=1, source_target_pairs={{0,4},{4,8},{8,12},{12,16},{16,20},{20,24},{24,28},{28,32},{32,36}... | collective-permute-start | bytes 786440 | tf_op jit(solution)/shard_map/while/body/eval_jaxpr/ppermute | solution.py:18
  508.6 10.4 %collective-permute-start = (f32[4,128,128]{2,1,0:T(8,128)S(1)}, f32[4,128,128]{2,1,0:T(8,128)S(1)}, u32[]{:S(2)}, u32[]{:S(2)}) collective-permute-start(f32[4,128,128]{2,1,0:T(8,128)S(1)} %convolution_add_fusion.4), channel_id=1, source_target_pairs={{0,4},{4,8},{8,12},{12,16},{16,20},{20,24},{24,28},{28,32},{32,36}... | collective-permute-start | bytes 786440 | tf_op jit(solution)/shard_map/while/body/eval_jaxpr/ppermute | solution.py:18
  519.4 10.4 %collective-permute-start = (f32[4,128,128]{2,1,0:T(8,128)S(1)}, f32[4,128,128]{2,1,0:T(8,128)S(1)}, u32[]{:S(2)}, u32[]{:S(2)}) collective-permute-start(f32[4,128,128]{2,1,0:T(8,128)S(1)} %convolution_add_fusion.4), channel_id=1, source_target_pairs={{0,4},{4,8},{8,12},{12,16},{16,20},{20,24},{24,28},{28,32},{32,36}... | collective-permute-start | bytes 786440 | tf_op jit(solution)/shard_map/while/body/eval_jaxpr/ppermute | solution.py:18
  530.2 10.4 %collective-permute-start = (f32[4,128,128]{2,1,0:T(8,128)S(1)}, f32[4,128,128]{2,1,0:T(8,128)S(1)}, u32[]{:S(2)}, u32[]{:S(2)}) collective-permute-start(f32[4,128,128]{2,1,0:T(8,128)S(1)} %convolution_add_fusion.4), channel_id=1, source_target_pairs={{0,4},{4,8},{8,12},{12,16},{16,20},{20,24},{24,28},{28,32},{32,36}... | collective-permute-start | bytes 786440 | tf_op jit(solution)/shard_map/while/body/eval_jaxpr/ppermute | solution.py:18
  541.0 10.4 %collective-permute-start = (f32[4,128,128]{2,1,0:T(8,128)S(1)}, f32[4,128,128]{2,1,0:T(8,128)S(1)}, u32[]{:S(2)}, u32[]{:S(2)}) collective-permute-start(f32[4,128,128]{2,1,0:T(8,128)S(1)} %convolution_add_fusion.4), channel_id=1, source_target_pairs={{0,4},{4,8},{8,12},{12,16},{16,20},{20,24},{24,28},{28,32},{32,36}... | collective-permute-start | bytes 786440 | tf_op jit(solution)/shard_map/while/body/eval_jaxpr/ppermute | solution.py:18
  551.8 10.9 %collective-permute-start = (f32[4,128,128]{2,1,0:T(8,128)S(1)}, f32[4,128,128]{2,1,0:T(8,128)S(1)}, u32[]{:S(2)}, u32[]{:S(2)}) collective-permute-start(f32[4,128,128]{2,1,0:T(8,128)S(1)} %convolution_add_fusion.4), channel_id=1, source_target_pairs={{0,4},{4,8},{8,12},{12,16},{16,20},{20,24},{24,28},{28,32},{32,36}... | collective-permute-start | bytes 786440 | tf_op jit(solution)/shard_map/while/body/eval_jaxpr/ppermute | solution.py:18
  563.1 12.0 %collective-permute-start = (f32[4,128,128]{2,1,0:T(8,128)S(1)}, f32[4,128,128]{2,1,0:T(8,128)S(1)}, u32[]{:S(2)}, u32[]{:S(2)}) collective-permute-start(f32[4,128,128]{2,1,0:T(8,128)S(1)} %convolution_add_fusion.4), channel_id=1, source_target_pairs={{0,4},{4,8},{8,12},{12,16},{16,20},{20,24},{24,28},{28,32},{32,36}... | collective-permute-start | bytes 786440 | tf_op jit(solution)/shard_map/while/body/eval_jaxpr/ppermute | solution.py:18
  575.5 13.2 %collective-permute-start = (f32[4,128,128]{2,1,0:T(8,128)S(1)}, f32[4,128,128]{2,1,0:T(8,128)S(1)}, u32[]{:S(2)}, u32[]{:S(2)}) collective-permute-start(f32[4,128,128]{2,1,0:T(8,128)S(1)} %convolution_add_fusion.4), channel_id=1, source_target_pairs={{0,4},{4,8},{8,12},{12,16},{16,20},{20,24},{24,28},{28,32},{32,36}... | collective-permute-start | bytes 786440 | tf_op jit(solution)/shard_map/while/body/eval_jaxpr/ppermute | solution.py:18
  589.1 12.3 %collective-permute-start = (f32[4,128,128]{2,1,0:T(8,128)S(1)}, f32[4,128,128]{2,1,0:T(8,128)S(1)}, u32[]{:S(2)}, u32[]{:S(2)}) collective-permute-start(f32[4,128,128]{2,1,0:T(8,128)S(1)} %convolution_add_fusion.4), channel_id=1, source_target_pairs={{0,4},{4,8},{8,12},{12,16},{16,20},{20,24},{24,28},{28,32},{32,36}... | collective-permute-start | bytes 786440 | tf_op jit(solution)/shard_map/while/body/eval_jaxpr/ppermute | solution.py:18
  601.8 11.5 %collective-permute-start = (f32[4,128,128]{2,1,0:T(8,128)S(1)}, f32[4,128,128]{2,1,0:T(8,128)S(1)}, u32[]{:S(2)}, u32[]{:S(2)}) collective-permute-start(f32[4,128,128]{2,1,0:T(8,128)S(1)} %convolution_add_fusion.4), channel_id=1, source_target_pairs={{0,4},{4,8},{8,12},{12,16},{16,20},{20,24},{24,28},{28,32},{32,36}... | collective-permute-start | bytes 786440 | tf_op jit(solution)/shard_map/while/body/eval_jaxpr/ppermute | solution.py:18
  613.7 10.6 %collective-permute-start = (f32[4,128,128]{2,1,0:T(8,128)S(1)}, f32[4,128,128]{2,1,0:T(8,128)S(1)}, u32[]{:S(2)}, u32[]{:S(2)}) collective-permute-start(f32[4,128,128]{2,1,0:T(8,128)S(1)} %convolution_add_fusion.4), channel_id=1, source_target_pairs={{0,4},{4,8},{8,12},{12,16},{16,20},{20,24},{24,28},{28,32},{32,36}... | collective-permute-start | bytes 786440 | tf_op jit(solution)/shard_map/while/body/eval_jaxpr/ppermute | solution.py:18
  624.7 10.4 %collective-permute-start = (f32[4,128,128]{2,1,0:T(8,128)S(1)}, f32[4,128,128]{2,1,0:T(8,128)S(1)}, u32[]{:S(2)}, u32[]{:S(2)}) collective-permute-start(f32[4,128,128]{2,1,0:T(8,128)S(1)} %convolution_add_fusion.4), channel_id=1, source_target_pairs={{0,4},{4,8},{8,12},{12,16},{16,20},{20,24},{24,28},{28,32},{32,36}... | collective-permute-start | bytes 786440 | tf_op jit(solution)/shard_map/while/body/eval_jaxpr/ppermute | solution.py:18
  635.5 10.4 %collective-permute-start = (f32[4,128,128]{2,1,0:T(8,128)S(1)}, f32[4,128,128]{2,1,0:T(8,128)S(1)}, u32[]{:S(2)}, u32[]{:S(2)}) collective-permute-start(f32[4,128,128]{2,1,0:T(8,128)S(1)} %convolution_add_fusion.4), channel_id=1, source_target_pairs={{0,4},{4,8},{8,12},{12,16},{16,20},{20,24},{24,28},{28,32},{32,36}... | collective-permute-start | bytes 786440 | tf_op jit(solution)/shard_map/while/body/eval_jaxpr/ppermute | solution.py:18
  646.3 10.4 %collective-permute-start = (f32[4,128,128]{2,1,0:T(8,128)S(1)}, f32[4,128,128]{2,1,0:T(8,128)S(1)}, u32[]{:S(2)}, u32[]{:S(2)}) collective-permute-start(f32[4,128,128]{2,1,0:T(8,128)S(1)} %convolution_add_fusion.4), channel_id=1, source_target_pairs={{0,4},{4,8},{8,12},{12,16},{16,20},{20,24},{24,28},{28,32},{32,36}... | collective-permute-start | bytes 786440 | tf_op jit(solution)/shard_map/while/body/eval_jaxpr/ppermute | solution.py:18
  657.0 10.5 %collective-permute-start = (f32[4,128,128]{2,1,0:T(8,128)S(1)}, f32[4,128,128]{2,1,0:T(8,128)S(1)}, u32[]{:S(2)}, u32[]{:S(2)}) collective-permute-start(f32[4,128,128]{2,1,0:T(8,128)S(1)} %convolution_add_fusion.4), channel_id=1, source_target_pairs={{0,4},{4,8},{8,12},{12,16},{16,20},{20,24},{24,28},{28,32},{32,36}... | collective-permute-start | bytes 786440 | tf_op jit(solution)/shard_map/while/body/eval_jaxpr/ppermute | solution.py:18
  667.9 11.5 %collective-permute-start = (f32[4,128,128]{2,1,0:T(8,128)S(1)}, f32[4,128,128]{2,1,0:T(8,128)S(1)}, u32[]{:S(2)}, u32[]{:S(2)}) collective-permute-start(f32[4,128,128]{2,1,0:T(8,128)S(1)} %convolution_add_fusion.4), channel_id=1, source_target_pairs={{0,4},{4,8},{8,12},{12,16},{16,20},{20,24},{24,28},{28,32},{32,36}... | collective-permute-start | bytes 786440 | tf_op jit(solution)/shard_map/while/body/eval_jaxpr/ppermute | solution.py:18
  679.9 12.8 %collective-permute-start = (f32[4,128,128]{2,1,0:T(8,128)S(1)}, f32[4,128,128]{2,1,0:T(8,128)S(1)}, u32[]{:S(2)}, u32[]{:S(2)}) collective-permute-start(f32[4,128,128]{2,1,0:T(8,128)S(1)} %convolution_add_fusion.4), channel_id=1, source_target_pairs={{0,4},{4,8},{8,12},{12,16},{16,20},{20,24},{24,28},{28,32},{32,36}... | collective-permute-start | bytes 786440 | tf_op jit(solution)/shard_map/while/body/eval_jaxpr/ppermute | solution.py:18
  693.0 12.4 %collective-permute-start = (f32[4,128,128]{2,1,0:T(8,128)S(1)}, f32[4,128,128]{2,1,0:T(8,128)S(1)}, u32[]{:S(2)}, u32[]{:S(2)}) collective-permute-start(f32[4,128,128]{2,1,0:T(8,128)S(1)} %convolution_add_fusion.4), channel_id=1, source_target_pairs={{0,4},{4,8},{8,12},{12,16},{16,20},{20,24},{24,28},{28,32},{32,36}... | collective-permute-start | bytes 786440 | tf_op jit(solution)/shard_map/while/body/eval_jaxpr/ppermute | solution.py:18
  705.9 11.6 %collective-permute-start = (f32[4,128,128]{2,1,0:T(8,128)S(1)}, f32[4,128,128]{2,1,0:T(8,128)S(1)}, u32[]{:S(2)}, u32[]{:S(2)}) collective-permute-start(f32[4,128,128]{2,1,0:T(8,128)S(1)} %convolution_add_fusion.4), channel_id=1, source_target_pairs={{0,4},{4,8},{8,12},{12,16},{16,20},{20,24},{24,28},{28,32},{32,36}... | collective-permute-start | bytes 786440 | tf_op jit(solution)/shard_map/while/body/eval_jaxpr/ppermute | solution.py:18
  717.9 10.7 %collective-permute-start = (f32[4,128,128]{2,1,0:T(8,128)S(1)}, f32[4,128,128]{2,1,0:T(8,128)S(1)}, u32[]{:S(2)}, u32[]{:S(2)}) collective-permute-start(f32[4,128,128]{2,1,0:T(8,128)S(1)} %convolution_add_fusion.4), channel_id=1, source_target_pairs={{0,4},{4,8},{8,12},{12,16},{16,20},{20,24},{24,28},{28,32},{32,36}... | collective-permute-start | bytes 786440 | tf_op jit(solution)/shard_map/while/body/eval_jaxpr/ppermute | solution.py:18
  729.0 10.4 %collective-permute-start = (f32[4,128,128]{2,1,0:T(8,128)S(1)}, f32[4,128,128]{2,1,0:T(8,128)S(1)}, u32[]{:S(2)}, u32[]{:S(2)}) collective-permute-start(f32[4,128,128]{2,1,0:T(8,128)S(1)} %convolution_add_fusion.4), channel_id=1, source_target_pairs={{0,4},{4,8},{8,12},{12,16},{16,20},{20,24},{24,28},{28,32},{32,36}... | collective-permute-start | bytes 786440 | tf_op jit(solution)/shard_map/while/body/eval_jaxpr/ppermute | solution.py:18
  739.8 10.4 %collective-permute-start = (f32[4,128,128]{2,1,0:T(8,128)S(1)}, f32[4,128,128]{2,1,0:T(8,128)S(1)}, u32[]{:S(2)}, u32[]{:S(2)}) collective-permute-start(f32[4,128,128]{2,1,0:T(8,128)S(1)} %convolution_add_fusion.4), channel_id=1, source_target_pairs={{0,4},{4,8},{8,12},{12,16},{16,20},{20,24},{24,28},{28,32},{32,36}... | collective-permute-start | bytes 786440 | tf_op jit(solution)/shard_map/while/body/eval_jaxpr/ppermute | solution.py:18
  750.6 10.4 %collective-permute-start = (f32[4,128,128]{2,1,0:T(8,128)S(1)}, f32[4,128,128]{2,1,0:T(8,128)S(1)}, u32[]{:S(2)}, u32[]{:S(2)}) collective-permute-start(f32[4,128,128]{2,1,0:T(8,128)S(1)} %convolution_add_fusion.4), channel_id=1, source_target_pairs={{0,4},{4,8},{8,12},{12,16},{16,20},{20,24},{24,28},{28,32},{32,36}... | collective-permute-start | bytes 786440 | tf_op jit(solution)/shard_map/while/body/eval_jaxpr/ppermute | solution.py:18
  761.4 10.4 %collective-permute-start = (f32[4,128,128]{2,1,0:T(8,128)S(1)}, f32[4,128,128]{2,1,0:T(8,128)S(1)}, u32[]{:S(2)}, u32[]{:S(2)}) collective-permute-start(f32[4,128,128]{2,1,0:T(8,128)S(1)} %convolution_add_fusion.4), channel_id=1, source_target_pairs={{0,4},{4,8},{8,12},{12,16},{16,20},{20,24},{24,28},{28,32},{32,36}... | collective-permute-start | bytes 786440 | tf_op jit(solution)/shard_map/while/body/eval_jaxpr/ppermute | solution.py:18
  772.2 11.5 %collective-permute-start = (f32[4,128,128]{2,1,0:T(8,128)S(1)}, f32[4,128,128]{2,1,0:T(8,128)S(1)}, u32[]{:S(2)}, u32[]{:S(2)}) collective-permute-start(f32[4,128,128]{2,1,0:T(8,128)S(1)} %convolution_add_fusion.4), channel_id=1, source_target_pairs={{0,4},{4,8},{8,12},{12,16},{16,20},{20,24},{24,28},{28,32},{32,36}... | collective-permute-start | bytes 786440 | tf_op jit(solution)/shard_map/while/body/eval_jaxpr/ppermute | solution.py:18
  784.0 12.7 %collective-permute-start = (f32[4,128,128]{2,1,0:T(8,128)S(1)}, f32[4,128,128]{2,1,0:T(8,128)S(1)}, u32[]{:S(2)}, u32[]{:S(2)}) collective-permute-start(f32[4,128,128]{2,1,0:T(8,128)S(1)} %convolution_add_fusion.4), channel_id=1, source_target_pairs={{0,4},{4,8},{8,12},{12,16},{16,20},{20,24},{24,28},{28,32},{32,36}... | collective-permute-start | bytes 786440 | tf_op jit(solution)/shard_map/while/body/eval_jaxpr/ppermute | solution.py:18
  797.1 12.6 %collective-permute-start = (f32[4,128,128]{2,1,0:T(8,128)S(1)}, f32[4,128,128]{2,1,0:T(8,128)S(1)}, u32[]{:S(2)}, u32[]{:S(2)}) collective-permute-start(f32[4,128,128]{2,1,0:T(8,128)S(1)} %convolution_add_fusion.4), channel_id=1, source_target_pairs={{0,4},{4,8},{8,12},{12,16},{16,20},{20,24},{24,28},{28,32},{32,36}... | collective-permute-start | bytes 786440 | tf_op jit(solution)/shard_map/while/body/eval_jaxpr/ppermute | solution.py:18
  810.1 10.4 %collective-permute-start = (f32[4,128,128]{2,1,0:T(8,128)S(1)}, f32[4,128,128]{2,1,0:T(8,128)S(1)}, u32[]{:S(2)}, u32[]{:S(2)}) collective-permute-start(f32[4,128,128]{2,1,0:T(8,128)S(1)} %convolution_add_fusion.4), channel_id=1, source_target_pairs={{0,4},{4,8},{8,12},{12,16},{16,20},{20,24},{24,28},{28,32},{32,36}... | collective-permute-start | bytes 786440 | tf_op jit(solution)/shard_map/while/body/eval_jaxpr/ppermute | solution.py:18
  820.8 10.4 %collective-permute-start = (f32[4,128,128]{2,1,0:T(8,128)S(1)}, f32[4,128,128]{2,1,0:T(8,128)S(1)}, u32[]{:S(2)}, u32[]{:S(2)}) collective-permute-start(f32[4,128,128]{2,1,0:T(8,128)S(1)} %convolution_add_fusion.4), channel_id=1, source_target_pairs={{0,4},{4,8},{8,12},{12,16},{16,20},{20,24},{24,28},{28,32},{32,36}... | collective-permute-start | bytes 786440 | tf_op jit(solution)/shard_map/while/body/eval_jaxpr/ppermute | solution.py:18
  831.6 10.4 %collective-permute-start = (f32[4,128,128]{2,1,0:T(8,128)S(1)}, f32[4,128,128]{2,1,0:T(8,128)S(1)}, u32[]{:S(2)}, u32[]{:S(2)}) collective-permute-start(f32[4,128,128]{2,1,0:T(8,128)S(1)} %convolution_add_fusion.4), channel_id=1, source_target_pairs={{0,4},{4,8},{8,12},{12,16},{16,20},{20,24},{24,28},{28,32},{32,36}... | collective-permute-start | bytes 786440 | tf_op jit(solution)/shard_map/while/body/eval_jaxpr/ppermute | solution.py:18
  (23 other events, 444.2 us)
where the time goes:
time: 960 us; the launch traced here: 950 us
  other arithmetic  350 us (36%)
  waiting for transfers between devices  284 us (30%)
  matrix products  203 us (21%)
  starting transfers between devices  65.3 us (7%)
  local copies, waits for them, and re-layouts  45.2 us (5%)
    another operation x2, other arithmetic, group_kernel(): jax.scipy.linalg.solve_triangular(system, right_side, lower=True, unit_di...  316 us
    ppermute x32, waiting for transfers between devices, passed_along(): lax.ppermute(value, axis, [(source, source + steps) for source in range(l...  284 us
    ppermute x32, starting transfers between devices, passed_along(): lax.ppermute(value, axis, [(source, source + steps) for source in range(l...  65.3 us
    dot_general x63, matrix products, batched_product(): return jnp.einsum('hij,hjk->hik', left_side, right_side, precision=PRECISE)  63.4 us
    dot_general x16, matrix products, emit_group(): jnp.einsum('hcd,hvd->hcv', weight_row, carried, precision=PRECISE)  25.4 us
    sub x2, matrix products, window_attention(): powered = jnp.where(allowed[None], jnp.exp(masked - summit), 0.0)  22.1 us
    dot_general x16, matrix products, emit_group(): jnp.einsum('hcd,hvd->hcv', query_row, carried, precision=PRECISE)  20.5 us
    dot_general x16, matrix products, emit_group(): jnp.einsum('htd,hjd->htj', query_row, key_row, precision=PRECISE) * mask_row  20 us
  transfers between devices with their start and end apart: 32, of which 31 were waited for; matrix products, arithmetic and copies ran while one was open for 37% of the time, Pallas kernels for 0%

commit v1 on v0

v1 whole, which is shorter than its diff:
```python
import functools
import math

import jax
import jax.numpy as jnp
from jax import lax
from jax.experimental import pallas as pl
from jax.experimental.pallas import tpu as pltpu
from jax.sharding import PartitionSpec as P

CHUNK = 128
DH = 128
WIRE = 144
VMEM = 60 * 2**20
NEG = -1e30
F32 = jnp.float32
BF16 = jnp.bfloat16
NN = (((1,), (0,)), ((), ()))
NT = (((1,), (1,)), ((), ()))


def dot(a, b, dims=NN):
    return lax.dot_general(a, b, dims, preferred_element_type=F32)


def shift_lanes(row, steps):
    lane = lax.broadcasted_iota(jnp.int32, row.shape, 1)
    return jnp.where(lane >= steps, pltpu.roll(row, steps, axis=1), 0.0)


def halves(value):
    high = value.astype(BF16)
    return high, (value - high.astype(F32)).astype(BF16)


def beside(*parts):
    return jnp.concatenate(parts, axis=1)


def below(*parts):
    return jnp.concatenate(parts, axis=0)


def split_three(g):
    high = g.astype(BF16)
    rest = g - high.astype(F32)
    mid = rest.astype(BF16)
    low = (rest - mid.astype(F32)).astype(BF16)
    return high, mid, low


def pack_gain(g):
    row = lax.broadcasted_iota(jnp.int32, (WIRE - DH, DH), 0)
    high, mid, low = split_three(g)
    block = jnp.where(
        row == 0,
        high.astype(F32),
        jnp.where(row == 1, mid.astype(F32), jnp.where(row == 2, low.astype(F32), 0.0)),
    )
    return block.astype(BF16)


def unpack_gain(block):
    rows = block.astype(F32)
    return rows[0:1] + rows[1:2] + rows[2:3]


def prep_kernel(
    heads, ld_ref, be_ref, k_ref, q_ref, m_ref, ke_ref, qe_ref, qf_ref, e_ref, g_ref, w_ref, f_scr, gp_scr
):
    c = pl.program_id(0)

    @pl.when(c == 0)
    def _():
        f_scr[...] = jnp.zeros_like(f_scr)
        gp_scr[...] = jnp.ones_like(gp_scr)

    rows = jnp.concatenate([ld_ref[...], be_ref[...]], axis=0)
    cum = rows
    for steps in (1, 2, 4, 8, 16, 32, 64):
        cum = cum + shift_lanes(cum, steps)
    row8 = lax.broadcasted_iota(jnp.int32, (2 * heads, CHUNK), 0)
    rows = jnp.where(row8 < heads, cum, rows)
    cols = jnp.transpose(rows)
    ti = lax.broadcasted_iota(jnp.int32, (CHUNK, CHUNK), 0)
    tj = lax.broadcasted_iota(jnp.int32, (CHUNK, CHUNK), 1)
    eye = jnp.where(ti == tj, 1.0, 0.0)
    keys = []
    inv_k = []
    colmat = jnp.zeros((CHUNK, CHUNK), F32)
    for h in range(heads):
        k = k_ref[:, h * DH : (h + 1) * DH]
        kf = k.astype(F32)
        rk = 1.0 / jnp.sqrt(jnp.sum(kf * kf, axis=1, keepdims=True) + 1e-6)
        keys.append((k, kf))
        inv_k.append(rk)
        colmat = jnp.where(tj == h, rk, colmat)
    rowmat = jnp.transpose(colmat)
    state = []
    for h in range(heads):
        k, kf = keys[h]
        rk_c = inv_k[h]
        rk_r = rowmat[h : h + 1]
        q = q_ref[:, h * DH : (h + 1) * DH]
        qf = q.astype(F32)
        rq_c = 1.0 / jnp.sqrt(jnp.sum(qf * qf, axis=1, keepdims=True) + 1e-6)
        g_c = cols[:, h : h + 1]
        g_r = rows[h : h + 1]
        b_c = cols[:, heads + h : heads + h + 1]
        b_r = rows[heads + h : heads + h + 1]
        decay = jnp.exp(jnp.where(ti >= tj, g_c - g_r, NEG)) * rk_r
        kk = dot(k, k, NT)
        qk = dot(q, k, NT)
        a = beside(*halves(decay * rq_c * qk))
        low = jnp.where(ti > tj, decay * (b_c * rk_c) * kk, 0.0)
        t = eye - jnp.where((ti >> 1) == (tj >> 1), low, 0.0)
        state.append((k, kf, rk_c, rk_r, qf, rq_c, g_c, g_r, b_r, a, low, t))
    ts = [s[-1] for s in state]
    for shift in range(1, 7):
        pair = (ti >> (shift + 1)) == (tj >> (shift + 1))
        cross = pair & (((ti >> shift) & 1) == 1) & (((tj >> shift) & 1) == 0)
        tb = [t.astype(BF16) for t in ts]
        lm = [below(*halves(jnp.where(cross, s[-2], 0.0))) for s in state]
        mid = [dot(beside(x, x), y).astype(BF16) for x, y in zip(tb, lm)]
        ts = [t - dot(x, y) for t, x, y in zip(ts, mid, tb)]
    for h in range(heads):
        k, kf, rk_c, rk_r, qf, rq_c, g_c, g_r, b_r, a, low, _ = state[h]
        t = ts[h]
        g_end = g_r[:, CHUNK - 1 : CHUNK]
        tail_c = jnp.exp(g_end - g_c)
        w = dot((t * (b_r * jnp.exp(g_r) * rk_r)).astype(BF16), k)
        wb = w.astype(BF16)
        tw = beside(t.astype(BF16), wb)
        both = dot(a, below(tw, tw))
        m_ref[0, h] = (both[:, :CHUNK] * b_r).astype(BF16)
        qe = (jnp.exp(g_c) * rq_c) * qf - both[:, CHUNK:]
        qeb = qe.astype(BF16)
        kt = jnp.transpose(kf).astype(BF16)
        ke = dot(beside(kt, kt), below(*halves((tail_c * rk_c) * t * b_r)))
        ke_ref[0, h] = beside(*halves(ke))
        e = -dot(kt, ((tail_c * rk_c) * w).astype(BF16))
        eb = e.astype(BF16)
        gc = jnp.broadcast_to(jnp.exp(g_end), (1, DH))
        gp = gp_scr[h : h + 1]
        f = f_scr[h]
        fb = f.astype(BF16)
        qe_ref[0, h] = qeb
        qf_ref[0, h] = (gp * qe + dot(qeb, fb)).astype(BF16)
        e_ref[0, h] = eb
        f_new = gc * f + gp * e + dot(eb, fb)
        gp_new = gp * gc
        f_scr[h] = f_new
        gp_scr[h : h + 1] = gp_new
        g_ref[0, h : h + 1] = gc

        @pl.when(c == pl.num_programs(0) - 1)
        def _():
            w_ref[h, :DH] = jnp.transpose(f_new).astype(BF16)
            w_ref[h, DH:] = pack_gain(gp_new)


def prep(log_decay, beta, delta_key, delta_query):
    heads, rows = log_decay.shape
    chunks = rows // CHUNK
    big = jax.ShapeDtypeStruct((chunks, heads, CHUNK, DH), BF16)
    big_spec = pl.BlockSpec((1, heads, CHUNK, DH), lambda c: (c, 0, 0, 0))
    row_spec = pl.BlockSpec((heads, CHUNK), lambda c: (0, c))
    tok_spec = pl.BlockSpec((CHUNK, heads * DH), lambda c: (c, 0))
    return pl.pallas_call(
        functools.partial(prep_kernel, heads),
        grid=(chunks,),
        in_specs=[row_spec, row_spec, tok_spec, tok_spec],
        out_specs=[big_spec, pl.BlockSpec((1, heads, CHUNK, 2 * DH), lambda c: (c, 0, 0, 0))]
        + [big_spec] * 3
        + [
            pl.BlockSpec((1, heads, DH), lambda c: (c, 0, 0)),
            pl.BlockSpec((heads, WIRE, DH), lambda c: (0, 0, 0)),
        ],
        out_shape=[big, jax.ShapeDtypeStruct((chunks, heads, CHUNK, 2 * DH), BF16)]
        + [big] * 3
        + [
            jax.ShapeDtypeStruct((chunks, heads, DH), F32),
            jax.ShapeDtypeStruct((heads, WIRE, DH), BF16),
        ],
        scratch_shapes=[pltpu.VMEM((heads, DH, DH), F32), pltpu.VMEM((heads, DH), F32)],
        compiler_params=pltpu.CompilerParams(vmem_limit_bytes=VMEM),
        cost_estimate=pl.CostEstimate(flops=1_000_000, bytes_accessed=1_000_000, transcendentals=0),
        name="delta_prep",
    )(log_decay, beta, delta_key, delta_query)


QB = 256


def attend_kernel(
    window,
    first_ref,
    q_ref,
    kp_ref,
    ko_ref,
    vp_ref,
    vo_ref,
    m_ref,
    ke_ref,
    qe_ref,
    e_ref,
    g_ref,
    r_ref,
    b_ref,
    kx,
    vx,
    x_scr,
):
    h = pl.program_id(0)
    i = pl.program_id(1)
    first = first_ref[0]

    @pl.when(i == 0)
    def _():
        kx[window:] = ko_ref[...]
        vx[window:, :DH] = vo_ref[...]
        vx[window:, DH:] = jnp.ones((vo_ref.shape[0], DH), BF16)
        vx[:window, :DH] = vp_ref[...]
        x_scr[...] = jnp.zeros_like(x_scr)

        @pl.when(first == 0)
        def _():
            kx[:window] = kp_ref[...]
            vx[:window, DH:] = jnp.ones((window, DH), BF16)

        @pl.when(first != 0)
        def _():
            kx[:window] = jnp.broadcast_to(ko_ref[0:1].astype(F32), (window, DH)).astype(BF16)
            vx[:window, DH:] = jnp.zeros((window, DH), BF16)

    start = pl.multiple_of(i * QB, QB)
    span = window + QB
    keys = kx[pl.ds(start, span)]
    vals = vx[pl.ds(start, span)]
    scale = 1.0 / math.sqrt(DH) * math.log2(math.e)
    s = dot(q_ref[...], keys, NT)
    ri = lax.broadcasted_iota(jnp.int32, (QB, QB), 0)
    rj = lax.broadcasted_iota(jnp.int32, (QB, QB), 1)
    s = jnp.concatenate(
        [
            jnp.where(rj > ri, s[:, :QB], NEG),
            s[:, QB:window],
            jnp.where(rj <= ri, s[:, window:], NEG),
        ],
        axis=1,
    )
    top = jnp.max(s, axis=1, keepdims=True)
    p = jnp.exp2((s - top) * scale).astype(BF16)
    pv = dot(p, vals)
    o = (pv[:, :DH] / pv[:, DH:]).astype(BF16).astype(F32)
    vh, vl = halves(o / jnp.sqrt(jnp.mean(o * o, axis=1, keepdims=True) + 1e-6))
    x = x_scr[...]
    for cc in range(QB // CHUNK):
        part = slice(cc * CHUNK, (cc + 1) * CHUNK)
        xh, xl = halves(x)
        m, qe, ke = m_ref[cc, 0], qe_ref[cc, 0], ke_ref[cc, 0]
        r_ref[part] = dot(beside(m, m), below(vh[part], vl[part])) + dot(beside(qe, qe), below(xh, xl))
        fresh = dot(ke, below(vh[part], vh[part])) + dot(ke[:, :DH], vl[part])
        x = g_ref[cc, pl.ds(h, 1)] * x + dot(e_ref[cc, 0], xh) + fresh
    x_scr[...] = x

    @pl.when(i == pl.num_programs(1) - 1)
    def _():
        b_ref[0] = jnp.transpose(x).astype(BF16)


def attend(first, att_query, k_prev, k_own, v_prev, v_own, m, ke, qe, e, g):
    rows, width = att_query.shape
    heads = width // DH
    window = k_prev.shape[0]
    per = QB // CHUNK
    col = lambda h, i: (0, h)
    big = pl.BlockSpec((per, 1, CHUNK, DH), lambda h, i: (i, h, 0, 0))
    return pl.pallas_call(
        functools.partial(attend_kernel, window),
        grid=(heads, rows // QB),
        in_specs=[
            pl.BlockSpec(memory_space=pltpu.SMEM),
            pl.BlockSpec((QB, DH), lambda h, i: (i, h)),
            pl.BlockSpec((window, DH), col),
            pl.BlockSpec((rows, DH), col),
            pl.BlockSpec((window, DH), col),
            pl.BlockSpec((rows, DH), col),
            big,
            pl.BlockSpec((per, 1, CHUNK, 2 * DH), lambda h, i: (i, h, 0, 0)),
            big,
            big,
            pl.BlockSpec((per, heads, DH), lambda h, i: (i, 0, 0)),
        ],
        out_specs=[
            pl.BlockSpec((QB, DH), lambda h, i: (i, h)),
            pl.BlockSpec((1, DH, DH), lambda h, i: (h, 0, 0)),
        ],
        out_shape=[
            jax.ShapeDtypeStruct((rows, width), F32),
            jax.ShapeDtypeStruct((heads, DH, DH), BF16),
        ],
        scratch_shapes=[
            pltpu.VMEM((window + rows, DH), BF16),
            pltpu.VMEM((window + rows, 2 * DH), BF16),
            pltpu.VMEM((DH, DH), F32),
        ],
        compiler_params=pltpu.CompilerParams(vmem_limit_bytes=VMEM),
        cost_estimate=pl.CostEstimate(
            flops=1_000_000_000_000, bytes_accessed=14_000_000, transcendentals=5_000_000
        ),
        name="window_attention",
    )(first, att_query, k_prev, k_own, v_prev, v_own, m, ke, qe, e, g)


def prefix_kernel(minor, majors, d_ref, p_ref):
    ti = lax.broadcasted_iota(jnp.int32, (DH, DH), 0)
    gs = [jnp.ones((1, DH), F32) for _ in range(majors)]
    fs = [jnp.zeros((DH, DH), F32) for _ in range(majors)]
    for z in range(minor + 1):
        for k in range(majors):
            p_ref[k, z, :DH] = fs[k].astype(BF16)
            p_ref[k, z, DH:] = pack_gain(gs[k])
        if z == minor:
            break
        for k in range(majors):
            d = d_ref[z, k, :DH]
            g = unpack_gain(d_ref[z, k, DH:])
            fs[k] = g * fs[k] + gs[k] * d.astype(F32) + dot(fs[k].astype(BF16), d)
            gs[k] = gs[k] * g


def prefix(d_all):
    minor, majors = d_all.shape[:2]
    return pl.pallas_call(
        functools.partial(prefix_kernel, minor, majors),
        in_specs=[pl.BlockSpec(memory_space=pltpu.VMEM)],
        out_specs=pl.BlockSpec(memory_space=pltpu.VMEM),
        out_shape=jax.ShapeDtypeStruct((majors, minor + 1, WIRE, DH), BF16),
        compiler_params=pltpu.CompilerParams(vmem_limit_bytes=VMEM),
        cost_estimate=pl.CostEstimate(flops=140_000_000, bytes_accessed=3_000_000, transcendentals=0),
        name="decay_prefix",
    )(d_all)


def chain_kernel(minor, majors, d_ref, p_ref, b_ref, s_ref):
    size = b_ref.shape[1]
    local = [[] for _ in range(majors)]
    acc = [jnp.zeros((size, DH), F32) for _ in range(majors)]
    for z in range(minor):
        for x in range(majors):
            local[x].append(acc[x])
            g = unpack_gain(d_ref[z, x, DH:])
            b = b_ref[x * minor + z].astype(F32)
            acc[x] = g * acc[x] + b + dot(acc[x].astype(BF16), d_ref[z, x, :DH])
    start = jnp.zeros((size, DH), F32)
    for x in range(majors):
        high = start.astype(BF16)
        for z in range(minor):
            g = unpack_gain(p_ref[x, z, DH:])
            out = g * start + local[x][z] + dot(high, p_ref[x, z, :DH])
            s_ref[x * minor + z] = out.astype(BF16)
        g = unpack_gain(p_ref[x, minor, DH:])
        start = g * start + acc[x] + dot(high, p_ref[x, minor, :DH])


def chain(d_all, p_all, b_rows):
    minor, majors = d_all.shape[:2]
    vm = pl.BlockSpec(memory_space=pltpu.VMEM)
    return pl.pallas_call(
        functools.partial(chain_kernel, minor, majors),
        in_specs=[vm, vm, vm],
        out_specs=vm,
        out_shape=jax.ShapeDtypeStruct(b_rows.shape, BF16),
        compiler_params=pltpu.CompilerParams(vmem_limit_bytes=VMEM),
        cost_estimate=pl.CostEstimate(flops=40_000_000, bytes_accessed=4_000_000, transcendentals=0),
        name="state_chain",
    )(d_all, p_all, b_rows)


def finish_kernel(heads, r_ref, qf_ref, s_ref, gate_ref, gain_ref, o_ref):
    gain = gain_ref[...]
    for h in range(heads):
        cols = slice(h * DH, (h + 1) * DH)
        r = r_ref[:, cols] + dot(qf_ref[0, h], s_ref[h], NT)
        gate = gate_ref[:, cols].astype(F32)
        r = r / jnp.sqrt(jnp.mean(r * r, axis=1, keepdims=True) + 1e-6)
        o_ref[:, cols] = (r * gain * (gate / (1.0 + jnp.exp(-gate)))).astype(BF16)


def finish(readout, qf, state, out_gate, gain):
    rows, width = readout.shape
    heads = width // DH
    tok = pl.BlockSpec((CHUNK, width), lambda c: (c, 0))
    return pl.pallas_call(
        functools.partial(finish_kernel, heads),
        grid=(rows // CHUNK,),
        in_specs=[
            tok,
            pl.BlockSpec((1, heads, CHUNK, DH), lambda c: (c, 0, 0, 0)),
            pl.BlockSpec((heads, DH, DH), lambda c: (0, 0, 0)),
            tok,
            pl.BlockSpec((1, DH), lambda c: (0, 0)),
        ],
        out_specs=tok,
        out_shape=jax.ShapeDtypeStruct((rows, width), BF16),
        compiler_params=pltpu.CompilerParams(vmem_limit_bytes=VMEM),
        cost_estimate=pl.CostEstimate(flops=140_000_000, bytes_accessed=6_000_000, transcendentals=600_000),
        name="gated_readout",
    )(readout, qf, state, out_gate, gain)


def body(att_query, att_key, att_value, delta_query, delta_key, out_gate, log_decay, beta, norm_gain):
    heads = log_decay.shape[0]
    count = lax.axis_size("seq")
    majors = heads
    minor = count // majors
    place = lax.axis_index("seq")
    onward = [(s, s + 1) for s in range(count - 1)]
    k_prev = lax.ppermute(att_key, "seq", onward)
    v_prev = lax.ppermute(att_value, "seq", onward)
    m, ke, qe, qf, e, g, wire = prep(log_decay, beta, delta_key, delta_query)
    columns = [[x * minor + z for x in range(majors)] for z in range(minor)]
    lines = [[x * minor + z for z in range(minor)] for x in range(majors)]
    pieces = lax.all_to_all(wire, "seq", 0, 0, axis_index_groups=columns)
    d_all = lax.all_gather(pieces, "seq", axis_index_groups=lines)
    p_all = prefix(d_all)
    first = jnp.reshape((place == 0).astype(jnp.int32), (1,))
    readout, b = attend(first, att_query, k_prev, att_key, v_prev, att_value, m, ke, qe, e, g)
    b, p_all = lax.optimization_barrier((b, p_all))
    b_rows = lax.all_to_all(b.reshape(count, heads * DH // count, DH), "seq", 0, 0)
    s_rows = chain(d_all, p_all, b_rows)
    state = lax.all_to_all(s_rows, "seq", 0, 0).reshape(heads, DH, DH)
    return finish(readout, qf, state, out_gate, norm_gain.reshape(1, DH))


def solution(mesh):
    tokens = P(("doc", "seq"), "head")
    gates = P("head", ("doc", "seq"))
    return jax.shard_map(
        body,
        mesh=mesh,
        in_specs=(tokens,) * 6 + (gates, gates, P()),
        out_specs=tokens,
        check_vma=False,
    )
```

time: 960 us -> 154 us (0.16)
  other arithmetic: 350 us -> 0 us
  waiting for transfers between devices: 284 us -> 14.9 us
  matrix products: 203 us -> 0 us
  Pallas kernels: 0 us -> 78.4 us
  starting transfers between devices: 65.3 us -> 12.5 us
  local copies, waits for them, and re-layouts: 45.2 us -> 1.98 us
  blocking collectives: 0 us -> 31.3 us
  between operations: 0.71 us -> 13.5 us
    another operation x4 -> x0, other arithmetic: 318 us -> none  [the longest x2 316 us: group_kernel(): jax.scipy.linalg.solve_triangular(system, right_side, lower=True, unit_di...]
    ppermute x32 -> x2, waiting for transfers between devices: 284 us -> 0.01 us  [the longest x1 0.01 us: body(): v_prev = lax.ppermute(att_value, 'seq', onward)]
    dot_general x148 -> x0, matrix products: 176 us -> none  [the longest x63 63.4 us: batched_product(): return jnp.einsum('hij,hjk->hik', left_side, right_side, precision=PRECISE)]
    pallas_call x0 -> x5, Pallas kernels: none -> 78.4 us  [the longest x1 36.4 us: prep(): pl.pallas_call(functools.partial(prep_kernel, heads), grid=(chunks,), in_...]
    ppermute x32 -> x2, starting transfers between devices: 65.3 us -> 7.64 us  [the longest x1 3.83 us: body(): v_prev = lax.ppermute(att_value, 'seq', onward)]
    all_to_all x0 -> x2, blocking collectives: none -> 31.3 us  [the longest x1 16.5 us: body(): lax.all_to_all(b.reshape(count, heads * DH // count, DH), 'seq', 0, 0)]
    sub x2 -> x0, matrix products: 22.1 us -> none  [window_attention(): powered = jnp.where(allowed[None], jnp.exp(masked - summit), 0.0)]
    dynamic_slice x48 -> x0, local copies, waits for them, and re-layouts: 16.4 us -> none  [body(): lax.scan(emit_group, incoming, (cumlog, decay_mask, weight_part, source_p...]
  transfers between devices with their start and end apart: 32 -> 4, of which waited for: 31 -> 2; matrix products, arithmetic and copies ran while one was open for 37% -> 0% of each run, Pallas kernels for 0% -> 42%
where the time goes in v1:
time: 154 us; the launch traced here: 153 us
  Pallas kernels  78.4 us (51%)
  blocking collectives  31.3 us (20%)
  waiting for transfers between devices  14.9 us (10%)
  between operations  13.5 us (9%)
  starting transfers between devices  12.5 us (8%)
  local copies, waits for them, and re-layouts  1.98 us (1%)
    pallas_call x1, Pallas kernels, prep(): pl.pallas_call(functools.partial(prep_kernel, heads), grid=(chunks,), in_...  36.4 us
    pallas_call x1, Pallas kernels, attend(): pl.pallas_call(functools.partial(attend_kernel, window), grid=(heads, row...  27.3 us
    all_to_all x1, blocking collectives, body(): lax.all_to_all(b.reshape(count, heads * DH // count, DH), 'seq', 0, 0)  16.5 us
    all_to_all x1, blocking collectives, body(): state = lax.all_to_all(s_rows, 'seq', 0, 0).reshape(heads, DH, DH)  14.8 us
    all_gather x1, waiting for transfers between devices, body(): d_all = lax.all_gather(pieces, 'seq', axis_index_groups=lines)  9.41 us
    pallas_call x1, Pallas kernels, finish(): pl.pallas_call(functools.partial(finish_kernel, heads), grid=(rows // CHU...  7.38 us
    all_to_all x1, waiting for transfers between devices, body(): pieces = lax.all_to_all(wire, 'seq', 0, 0, axis_index_groups=columns)  5.5 us
    all_to_all x1, starting transfers between devices, body(): pieces = lax.all_to_all(wire, 'seq', 0, 0, axis_index_groups=columns)  4.84 us
  transfers between devices with their start and end apart: 4, of which 2 were waited for; matrix products, arithmetic and copies ran while one was open for 0% of the time, Pallas kernels for 42%

profile of v1, /device:TPU:18, one launch (start us, length us, event | category | flops | bytes accessed | tf_op | source)
XLA Modules:
  0.0 152.6 jit_solution(14289934694493683327)
XLA Ops:
  6.5 3.8 %collective-permute-start = (bf16[1024,512]{1,0:T(8,128)(2,1)}, bf16[1024,512]{1,0:T(8,128)(2,1)S(1)}, u32[]{:S(2)}, u32[]{:S(2)}) collective-permute-start(bf16[1024,512]{1,0:T(8,128)(2,1)} %ko_ref.1), channel_id=1, source_target_pairs={{0,4},{4,8},{8,12},{12,16},{16,20},{20,24},{24,28},{28,32},{32,36}... | collective-permute-start | bytes 3145736 | tf_op jit(solution)/shard_map/ppermute | solution.py:420
  10.4 3.8 %collective-permute-start.1 = (bf16[1024,512]{1,0:T(8,128)(2,1)}, bf16[1024,512]{1,0:T(8,128)(2,1)S(1)}, u32[]{:S(2)}, u32[]{:S(2)}) collective-permute-start(bf16[1024,512]{1,0:T(8,128)(2,1)} %vo_ref.1), channel_id=1, source_target_pairs={{0,4},{4,8},{8,12},{12,16},{16,20},{20,24},{24,28},{28,32},{32,36}... | collective-permute-start | bytes 3145736 | tf_op jit(solution)/shard_map/ppermute | solution.py:421
  14.2 36.4 %delta_prep.1 = (bf16[8,4,128,128]{3,2,1,0:T(8,128)(2,1)}, bf16[8,4,128,256]{3,2,1,0:T(8,128)(2,1)}, bf16[8,4,128,128]{3,2,1,0:T(8,128)(2,1)}, bf16[8,4,128,128]...) custom-call(f32[4,1024]{1,0:T(4,128)} %ld_ref.1, ...), custom_call_target="tpu_custom_call" | custom-call | flops 1000000 | bytes 1000000 | tf_op jit(solution)/shard_map/delta_prep/pallas_call | solution.py:169
  50.6 4.8 %all-to-all-start = ((bf16[4,144,128]{2,1,0:T(8,128)(2,1)}), bf16[4,144,128]{2,1,0:T(8,128)(2,1)S(1)}, u32[]{:S(2)}, u32[]{:S(2)}) async-start(bf16[4,144,128]{2,1,0:T(8,128)(2,1)} %get-tuple-element.23), calls=%async_computation | async-start | bytes 294912 | tf_op jit(solution)/shard_map/all_to_all | solution.py:425
  55.5 0.0 all-gather.3.cloned.1.call-start
  55.5 5.5 %all-to-all-done = bf16[4,144,128]{2,1,0:T(8,128)(2,1)S(1)} async-done(((bf16[4,144,128]{2,1,0:T(8,128)(2,1)}), bf16[4,144,128]{2,1,0:T(8,128)(2,1)S(1)}, u32[]{:S(2)}, u32[]{:S(2)}) %all-to-all-start) | async-done | bytes 147488 | tf_op jit(solution)/shard_map/all_to_all | solution.py:425
  61.0 0.0 copy-start
  61.0 0.7 copy-done
  61.6 0.0 all-gather.3.cloned.1.call-update
  61.7 0.0 collective-permute-done.kp_ref
  61.7 0.0 copy-start.2
  61.7 0.0 collective-permute-done.1.vp_ref
  61.7 0.0 copy-start.3
  61.7 0.9 copy-done.2
  62.6 0.4 copy-done.3
  63.0 27.3 %window_attention.1 = (f32[1024,512]{1,0:T(8,128)}, bf16[4,128,128]{2,1,0:T(8,128)(2,1)}) custom-call(s32[1]{0:T(128)} %bitcast.first_ref, bf16[1024,512]{1,0:T(8,128)(2,1)} %q_ref.3, bf16[1024,512]{1,0:T(8,128)(2,1)} %copy-done.2, bf16[1024,512]{1,0:T(8,128)(2,1)} %ko_ref.1, bf16[1024,512]{1,0:T(8,128)(2,1)} %copy-done.3, bf16[1024,512]{1,0:T(8,128)(2,1)} %vo_ref.1, ...), custom_call_target="tpu_custom_call" | custom-call | flops 999999995904 | bytes 14000000 | tf_op jit(solution)/shard_map/window_attention/pallas_call | solution.py:279
  90.3 0.0 copy-start.1
  90.3 9.4 %all-gather.3.cloned.1.call-done = bf16[32,144,128]{2,1,0:T(8,128)(2,1)} async-done(((bf16[4,144,128]{2,1,0:T(8,128)(2,1)}), bf16[32,144,128]{2,1,0:T(8,128)(2,1)}) %all-gather.3.cloned.1.call-update) | async-done | bytes 1179664 | tf_op jit(solution)/shard_map/all_gather | solution.py:426
  99.7 3.4 %decay_prefix.1.p_ref = bf16[4,9,144,128]{3,2,1,0:T(8,128)(2,1)} custom-call(bf16[8,4,144,128]{3,2,1,0:T(8,128)(2,1)} %bitcast.5), custom_call_target="tpu_custom_call" | custom-call | flops 140000000 | bytes 3000000 | tf_op jit(solution)/shard_map/decay_prefix/pallas_call | solution.py:335
  103.1 0.0 copy-done.1
  103.1 16.5 %all_to_all.15.b_ref = bf16[32,16,128]{2,1,0:T(8,128)(2,1)} all-to-all(bf16[32,16,128]{2,1,0:T(8,128)(2,1)S(1)} %bitcast.8), channel_id=1, replica_groups=mesh['doc'=2,'seq'=32,'head'=4] {'seq'}, dimensions={0} | all-to-all | bytes 262144 | tf_op jit(solution)/shard_map/all_to_all | solution.py:431
  119.6 4.0 %state_chain.1 = bf16[32,16,128]{2,1,0:T(8,128)(2,1)} custom-call(bf16[8,4,144,128]{3,2,1,0:T(8,128)(2,1)} %bitcast.6, bf16[4,9,144,128]{3,2,1,0:T(8,128)(2,1)} %decay_prefix.1.p_ref, bf16[32,16,128]{2,1,0:T(8,128)(2,1)} %all_to_all.15.b_ref), custom_call_target="tpu_custom_call" | custom-call | flops 40000000 | bytes 4000000 | tf_op jit(solution)/shard_map/state_chain/pallas_call | solution.py:370
  123.5 14.8 %all_to_all.16 = bf16[32,16,128]{2,1,0:T(8,128)(2,1)} all-to-all(bf16[32,16,128]{2,1,0:T(8,128)(2,1)} %state_chain.1), channel_id=1, replica_groups=mesh['doc'=2,'seq'=32,'head'=4] {'seq'}, dimensions={0} | all-to-all | bytes 262144 | tf_op jit(solution)/shard_map/all_to_all | solution.py:433
  138.4 7.4 %gated_readout.1 = bf16[1024,512]{1,0:T(8,128)(2,1)} custom-call(f32[1024,512]{1,0:T(8,128)} %get-tuple-element.21.r_ref, bf16[8,4,128,128]{3,2,1,0:T(8,128)(2,1)} %get-tuple-element.22.qf_ref, bf16[4,128,128]{2,1,0:T(8,128)(2,1)} %bitcast.7, bf16[1024,512]{1,0:T(8,128)(2,1)} %gate_ref.1, f32[1,128]{1,0:T(1,128)} %bitcast.9), custom_call_target="tpu_custom_call" | custom-call | flops 140000000 | bytes 6000000 | tf_op jit(solution)/shard_map/gated_readout/pallas_call | solution.py:395
Async XLA Ops:
  6.5 55.1 %collective-permute-start = (bf16[1024,512]{1,0:T(8,128)(2,1)}, bf16[1024,512]{1,0:T(8,128)(2,1)S(1)}, u32[]{:S(2)}, u32[]{:S(2)}) collective-permute-start(bf16[1024,512]{1,0:T(8,128)(2,1)} %ko_ref.1), channel_id=1, source_target_pairs={{0,4},{4,8},{8,12},{12,16},{16,20},{20,24},{24,28},{28,32},{32,36}... | collective-permute-start | bytes 3145736 | tf_op jit(solution)/shard_map/ppermute | solution.py:420
  10.4 51.3 %collective-permute-start.1 = (bf16[1024,512]{1,0:T(8,128)(2,1)}, bf16[1024,512]{1,0:T(8,128)(2,1)S(1)}, u32[]{:S(2)}, u32[]{:S(2)}) collective-permute-start(bf16[1024,512]{1,0:T(8,128)(2,1)} %vo_ref.1), channel_id=1, source_target_pairs={{0,4},{4,8},{8,12},{12,16},{16,20},{20,24},{24,28},{28,32},{32,36}... | collective-permute-start | bytes 3145736 | tf_op jit(solution)/shard_map/ppermute | solution.py:421
  50.6 10.3 %all-to-all-start = ((bf16[4,144,128]{2,1,0:T(8,128)(2,1)}), bf16[4,144,128]{2,1,0:T(8,128)(2,1)S(1)}, u32[]{:S(2)}, u32[]{:S(2)}) async-start(bf16[4,144,128]{2,1,0:T(8,128)(2,1)} %get-tuple-element.23), calls=%async_computation | async-start | bytes 294912 | tf_op jit(solution)/shard_map/all_to_all | solution.py:425
  55.5 44.3 %all-gather.3.cloned.1.call-start = ((), (), s32[]{:S(2)}) async-start(), calls=%async_computation.3 | async-start | bytes 1327104 | tf_op jit(solution)/shard_map/all_gather | solution.py:426
  61.0 0.7 copy-start
  61.7 1.0 copy-start.2
  61.7 1.3 copy-start.3
  90.3 12.8 %copy-start.1 = (bf16[4,128,128]{2,1,0:T(8,128)(2,1)S(1)}, bf16[4,128,128]{2,1,0:T(8,128)(2,1)}, u32[]{:S(2)}) copy-start(bf16[4,128,128]{2,1,0:T(8,128)(2,1)} %get-tuple-element.26) | copy-start | bytes 393220
Sparse Core Ops, SparseCore 0:
  61.8 37.9 all-gather.2

commit v2 on v1

v2 whole, which is shorter than its diff:
```python
import functools
import math

import jax
import jax.numpy as jnp
from jax import lax
from jax.experimental import pallas as pl
from jax.experimental.pallas import tpu as pltpu
from jax.sharding import PartitionSpec as P

CHUNK = 128
DH = 128
WIRE = 144
VMEM = 60 * 2**20
MIDDLE = 58 * 2**20
SMALL = 8 * 2**20
NEG = -1e30
F32 = jnp.float32
BF16 = jnp.bfloat16
NN = (((1,), (0,)), ((), ()))
NT = (((1,), (1,)), ((), ()))


def dot(a, b, dims=NN):
    return lax.dot_general(a, b, dims, preferred_element_type=F32)


def shift_lanes(row, steps):
    lane = lax.broadcasted_iota(jnp.int32, row.shape, 1)
    return jnp.where(lane >= steps, pltpu.roll(row, steps, axis=1), 0.0)


def halves(value):
    high = value.astype(BF16)
    return high, (value - high.astype(F32)).astype(BF16)


def beside(*parts):
    return jnp.concatenate(parts, axis=1)


def below(*parts):
    return jnp.concatenate(parts, axis=0)


def split_three(g):
    high = g.astype(BF16)
    rest = g - high.astype(F32)
    mid = rest.astype(BF16)
    low = (rest - mid.astype(F32)).astype(BF16)
    return high, mid, low


def pack_gain(g):
    row = lax.broadcasted_iota(jnp.int32, (WIRE - DH, DH), 0)
    high, mid, low = split_three(g)
    block = jnp.where(
        row == 0,
        high.astype(F32),
        jnp.where(row == 1, mid.astype(F32), jnp.where(row == 2, low.astype(F32), 0.0)),
    )
    return block.astype(BF16)


def unpack_gain(block):
    rows = block.astype(F32)
    return rows[0:1] + rows[1:2] + rows[2:3]


def gate_rows(heads, ld, be):
    rows = below(ld, be)
    cum = rows
    for steps in (1, 2, 4, 8, 16, 32, 64):
        cum = cum + shift_lanes(cum, steps)
    row8 = lax.broadcasted_iota(jnp.int32, (2 * heads, CHUNK), 0)
    return jnp.where(row8 < heads, cum, rows)


def prep_kernel(
    heads, per, ld_ref, be_ref, k_ref, q_ref, m_ref, ke_ref, qe_ref, qf_ref, e_ref, g_ref, w_ref, f_scr, gp_scr
):
    step = pl.program_id(0)

    @pl.when(step == 0)
    def _():
        f_scr[...] = jnp.zeros_like(f_scr)
        gp_scr[...] = jnp.ones_like(gp_scr)

    ti = lax.broadcasted_iota(jnp.int32, (CHUNK, CHUNK), 0)
    tj = lax.broadcasted_iota(jnp.int32, (CHUNK, CHUNK), 1)
    eye = jnp.where(ti == tj, 1.0, 0.0)
    state = []
    ts = []
    for c in range(per):
        part = slice(c * CHUNK, (c + 1) * CHUNK)
        rows = gate_rows(heads, ld_ref[:, part], be_ref[:, part])
        cols = jnp.transpose(rows)
        keys = []
        colmat = jnp.zeros((CHUNK, CHUNK), F32)
        for h in range(heads):
            k = k_ref[part, h * DH : (h + 1) * DH]
            kf = k.astype(F32)
            rk = lax.rsqrt(jnp.sum(kf * kf, axis=1, keepdims=True) + 1e-6)
            keys.append((k, kf, rk))
            colmat = jnp.where(tj == h, rk, colmat)
        rowmat = jnp.transpose(colmat)
        for h in range(heads):
            k, kf, rk_c = keys[h]
            rk_r = rowmat[h : h + 1]
            q = q_ref[part, h * DH : (h + 1) * DH]
            qf = q.astype(F32)
            rq_c = lax.rsqrt(jnp.sum(qf * qf, axis=1, keepdims=True) + 1e-6)
            g_c = cols[:, h : h + 1]
            g_r = rows[h : h + 1]
            b_c = cols[:, heads + h : heads + h + 1]
            b_r = rows[heads + h : heads + h + 1]
            decay = jnp.exp(jnp.where(ti >= tj, g_c - g_r, NEG)) * rk_r
            kk = dot(k, k, NT)
            qk = dot(q, k, NT)
            a = beside(*halves(decay * rq_c * qk))
            low = jnp.where(ti > tj, decay * (b_c * rk_c) * kk, 0.0)
            ts.append(eye - jnp.where((ti >> 1) == (tj >> 1), low, 0.0))
            state.append((k, kf, rk_c, rk_r, qf, rq_c, g_c, g_r, b_r, a, low))
    for shift in range(1, 7):
        pair = (ti >> (shift + 1)) == (tj >> (shift + 1))
        cross = pair & (((ti >> shift) & 1) == 1) & (((tj >> shift) & 1) == 0)
        tb = [t.astype(BF16) for t in ts]
        lm = [below(*halves(jnp.where(cross, s[-1], 0.0))) for s in state]
        mid = [dot(beside(x, x), y).astype(BF16) for x, y in zip(tb, lm)]
        ts = [t - dot(x, y) for t, x, y in zip(ts, mid, tb)]
    for c in range(per):
        for h in range(heads):
            k, kf, rk_c, rk_r, qf, rq_c, g_c, g_r, b_r, a, low = state[c * heads + h]
            t = ts[c * heads + h]
            g_end = g_r[:, CHUNK - 1 : CHUNK]
            tail_c = jnp.exp(g_end - g_c) * rk_c
            w = dot((t * (b_r * jnp.exp(g_r) * rk_r)).astype(BF16), k)
            wb = w.astype(BF16)
            tw = beside(t.astype(BF16), wb)
            both = dot(a, below(tw, tw))
            m_ref[c, h] = (both[:, :CHUNK] * b_r).astype(BF16)
            qe = (jnp.exp(g_c) * rq_c) * qf - both[:, CHUNK:]
            qeb = qe.astype(BF16)
            kt = jnp.transpose(kf).astype(BF16)
            ke = dot(beside(kt, kt), below(*halves(tail_c * t * b_r)))
            ke_ref[c, h] = beside(*halves(ke))
            e = -dot(kt, (tail_c * w).astype(BF16))
            eb = e.astype(BF16)
            gc = jnp.broadcast_to(jnp.exp(g_end), (1, DH))
            gp = gp_scr[h : h + 1]
            f = f_scr[h]
            fb = f.astype(BF16)
            qe_ref[c, h] = qeb
            qf_ref[c, h] = beside(*halves(gp * qe + dot(qeb, fb)))
            e_ref[c, h] = eb
            f_scr[h] = gc * f + gp * e + dot(eb, fb)
            gp_scr[h : h + 1] = gp * gc
            g_ref[c, h : h + 1] = gc

    @pl.when(step == pl.num_programs(0) - 1)
    def _():
        for h in range(heads):
            matrix = jnp.transpose(f_scr[h]).astype(BF16)
            gain = pack_gain(gp_scr[h : h + 1])
            for copy in range(w_ref.shape[0] // heads):
                w_ref[h * (w_ref.shape[0] // heads) + copy, :DH] = matrix
                w_ref[h * (w_ref.shape[0] // heads) + copy, DH:] = gain


PER = 4


def prep(log_decay, beta, delta_key, delta_query, copies):
    heads, rows = log_decay.shape
    chunks = rows // CHUNK
    big = jax.ShapeDtypeStruct((chunks, heads, CHUNK, DH), BF16)
    wide = jax.ShapeDtypeStruct((chunks, heads, CHUNK, 2 * DH), BF16)
    big_spec = pl.BlockSpec((PER, heads, CHUNK, DH), lambda c: (c, 0, 0, 0))
    wide_spec = pl.BlockSpec((PER, heads, CHUNK, 2 * DH), lambda c: (c, 0, 0, 0))
    row_spec = pl.BlockSpec((heads, PER * CHUNK), lambda c: (0, c))
    tok_spec = pl.BlockSpec((PER * CHUNK, heads * DH), lambda c: (c, 0))
    return pl.pallas_call(
        functools.partial(prep_kernel, heads, PER),
        grid=(chunks // PER,),
        in_specs=[row_spec, row_spec, tok_spec, tok_spec],
        out_specs=[big_spec, wide_spec, big_spec, wide_spec, big_spec]
        + [
            pl.BlockSpec((PER, heads, DH), lambda c: (c, 0, 0)),
            pl.BlockSpec((heads * copies, WIRE, DH), lambda c: (0, 0, 0)),
        ],
        out_shape=[big, wide, big, wide, big]
        + [
            jax.ShapeDtypeStruct((chunks, heads, DH), F32),
            jax.ShapeDtypeStruct((heads * copies, WIRE, DH), BF16),
        ],
        scratch_shapes=[pltpu.VMEM((heads, DH, DH), F32), pltpu.VMEM((heads, DH), F32)],
        compiler_params=pltpu.CompilerParams(vmem_limit_bytes=VMEM),
        cost_estimate=pl.CostEstimate(flops=1_000_000, bytes_accessed=1_000_000, transcendentals=0),
        name="delta_prep",
    )(log_decay, beta, delta_key, delta_query)


QB = 256
SCALE = 1.0 / math.sqrt(DH) * math.log2(math.e)


def own_kernel(q_ref, k_ref, v_ref, o_ref, vx):
    rows = q_ref.shape[0]
    vx[:, :DH] = v_ref[...]
    vx[:, DH:] = jnp.ones((rows, DH), BF16)
    ri = lax.broadcasted_iota(jnp.int32, (QB, QB), 0)
    rj = lax.broadcasted_iota(jnp.int32, (QB, QB), 1)
    lane = lax.broadcasted_iota(jnp.int32, (QB, DH), 1)
    blocks = [slice(i * QB, (i + 1) * QB) for i in range(rows // QB)]
    scores = []
    for here in blocks:
        s = dot(q_ref[here], k_ref[: here.stop], NT)
        edge = jnp.where(rj <= ri, s[:, here], NEG)
        scores.append(beside(s[:, : here.start], edge) if here.start else edge)
    for here, s in zip(blocks, scores):
        top = jnp.max(s, axis=1, keepdims=True)
        pv = dot(jnp.exp2((s - top) * SCALE).astype(BF16), vx[: here.stop])
        o_ref[here, :DH] = pv[:, :DH]
        o_ref[here, DH:] = jnp.where(lane < DH // 2, pv[:, DH:], top)


def own_part(att_query, att_key, att_value):
    rows, width = att_query.shape
    heads = width // DH
    tok = pl.BlockSpec((rows, DH), lambda h: (0, h))
    return pl.pallas_call(
        own_kernel,
        grid=(heads,),
        in_specs=[tok, tok, tok],
        out_specs=pl.BlockSpec((rows, 2 * DH), lambda h: (0, h)),
        out_shape=jax.ShapeDtypeStruct((rows, 2 * width), F32),
        scratch_shapes=[pltpu.VMEM((rows, 2 * DH), BF16)],
        compiler_params=pltpu.CompilerParams(vmem_limit_bytes=VMEM),
        cost_estimate=pl.CostEstimate(flops=100_000_000_000, bytes_accessed=1_000_000, transcendentals=0),
        name="own_attention",
    )(att_query, att_key, att_value)


def attend_kernel(
    first_ref, q_ref, kp_ref, ko_ref, vp_ref, own_ref, m_ref, ke_ref, qe_ref, e_ref, g_ref, r_ref, b_ref, kx, vx
):
    h = pl.program_id(0)
    first = first_ref[0]
    window = kp_ref.shape[0]
    vx[:, :DH] = vp_ref[...]

    @pl.when(first == 0)
    def _():
        kx[...] = kp_ref[...]
        vx[:, DH:] = jnp.ones((window, DH), BF16)

    @pl.when(first != 0)
    def _():
        kx[...] = jnp.broadcast_to(ko_ref[0:1].astype(F32), (window, DH)).astype(BF16)
        vx[:, DH:] = jnp.zeros((window, DH), BF16)

    ri = lax.broadcasted_iota(jnp.int32, (QB, QB), 0)
    rj = lax.broadcasted_iota(jnp.int32, (QB, QB), 1)
    mean = jnp.full((DH, DH), 1.0 / DH, BF16)
    blocks = [slice(i * QB, (i + 1) * QB) for i in range(q_ref.shape[0] // QB)]
    scores = []
    for i, here in enumerate(blocks):
        s = dot(q_ref[here], kx[i * QB :], NT)
        edge = jnp.where(rj > ri, s[:, :QB], NEG)
        scores.append(beside(edge, s[:, QB:]) if s.shape[1] > QB else edge)
    sums = []
    for i, (here, s) in enumerate(zip(blocks, scores)):
        own_top = own_ref[here, 2 * DH - 1 :]
        top = jnp.maximum(jnp.max(s, axis=1, keepdims=True), own_top)
        pv = dot(jnp.exp2((s - top) * SCALE).astype(BF16), vx[i * QB :])
        sums.append((pv, jnp.exp2((own_top - top) * SCALE)))
    outs = []
    for here, (pv, fade) in zip(blocks, sums):
        total = pv[:, DH:] + fade * own_ref[here, DH : DH + 1]
        outs.append(((pv[:, :DH] + fade * own_ref[here, :DH]) / total).astype(BF16).astype(F32))
    squares = [dot(beside(*halves(o * o)), below(mean, mean)) for o in outs]
    values = [halves(o * lax.rsqrt(square + 1e-6)) for o, square in zip(outs, squares)]
    per = QB // CHUNK
    chunks = []
    for c in range(m_ref.shape[0]):
        part = slice((c % per) * CHUNK, (c % per + 1) * CHUNK)
        chunks.append((values[c // per][0][part], values[c // per][1][part]))
    fresh = []
    for c, (vh, vl) in enumerate(chunks):
        ke = ke_ref[c, 0]
        fresh.append(dot(ke, below(vh, vh)) + dot(ke[:, :DH], vl))
    x = jnp.zeros((DH, DH), F32)
    states = []
    for c in range(len(chunks)):
        xh, xl = halves(x)
        states.append(below(xh, xl))
        x = g_ref[c, pl.ds(h, 1)] * x + dot(e_ref[c, 0], xh) + fresh[c]
    for c, (vh, vl) in enumerate(chunks):
        m, qe = m_ref[c, 0], qe_ref[c, 0]
        r_ref[c * CHUNK : (c + 1) * CHUNK] = dot(beside(m, m), below(vh, vl)) + dot(beside(qe, qe), states[c])
    b_ref[0] = jnp.transpose(x).astype(BF16)


def attend(first, att_query, k_prev, k_own, v_prev, own, m, ke, qe, e, g):
    rows, width = att_query.shape
    heads = width // DH
    window = k_prev.shape[0]
    chunks = rows // CHUNK
    big = pl.BlockSpec((chunks, 1, CHUNK, DH), lambda h: (0, h, 0, 0))
    tok = pl.BlockSpec((rows, DH), lambda h: (0, h))
    return pl.pallas_call(
        attend_kernel,
        grid=(heads,),
        in_specs=[
            pl.BlockSpec(memory_space=pltpu.SMEM),
            tok,
            pl.BlockSpec((window, DH), lambda h: (0, h)),
            pl.BlockSpec((16, DH), lambda h: (0, h)),
            pl.BlockSpec((window, DH), lambda h: (0, h)),
            pl.BlockSpec((rows, 2 * DH), lambda h: (0, h)),
            big,
            pl.BlockSpec((chunks, 1, CHUNK, 2 * DH), lambda h: (0, h, 0, 0)),
            big,
            big,
            pl.BlockSpec((chunks, heads, DH), lambda h: (0, 0, 0)),
        ],
        out_specs=[tok, pl.BlockSpec((1, DH, DH), lambda h: (h, 0, 0))],
        out_shape=[
            jax.ShapeDtypeStruct((rows, width), F32),
            jax.ShapeDtypeStruct((heads, DH, DH), BF16),
        ],
        scratch_shapes=[pltpu.VMEM((window, DH), BF16), pltpu.VMEM((window, 2 * DH), BF16)],
        compiler_params=pltpu.CompilerParams(vmem_limit_bytes=MIDDLE),
        cost_estimate=pl.CostEstimate(flops=100_000_000_000, bytes_accessed=1_000_000, transcendentals=0),
        name="window_attention",
    )(first, att_query, k_prev, k_own, v_prev, own, m, ke, qe, e, g)


def vmem_call(kernel, outs, name, *args):
    vm = pl.BlockSpec(memory_space=pltpu.VMEM)
    return pl.pallas_call(
        kernel,
        in_specs=[vm] * len(args),
        out_specs=[vm] * len(outs),
        out_shape=[jax.ShapeDtypeStruct(*o) for o in outs],
        compiler_params=pltpu.CompilerParams(vmem_limit_bytes=SMALL),
        cost_estimate=pl.CostEstimate(flops=1_000_000, bytes_accessed=1_000_000, transcendentals=0),
        name=name,
    )(*args)


def follow(g, f, d_ref):
    d = d_ref[:DH]
    step = unpack_gain(d_ref[DH:])
    return g * step, step * f + g * d.astype(F32) + dot(f.astype(BF16), d)


def prefix_kernel(d_ref, p_ref, t_ref):
    g = jnp.ones((1, DH), F32)
    f = jnp.zeros((DH, DH), F32)
    count = d_ref.shape[0]
    for z in range(count):
        p_ref[z, :DH] = f.astype(BF16)
        p_ref[z, DH:] = pack_gain(g)
        g, f = follow(g, f, d_ref.at[z])
    t_ref[:DH] = f.astype(BF16)
    t_ref[DH:] = pack_gain(g)


def line_kernel(d_ref, b_ref, q_ref, t_ref):
    acc = b_ref[0].astype(F32)
    q_ref[0] = jnp.zeros_like(acc)
    for z in range(1, d_ref.shape[0]):
        q_ref[z] = acc
        g = unpack_gain(d_ref[z, DH:])
        acc = g * acc + b_ref[z].astype(F32) + dot(acc.astype(BF16), d_ref[z, :DH])
    t_ref[...] = acc


def place_kernel(majors, *refs):
    sums, fades = refs[: majors - 1], refs[majors - 1 : 2 * majors - 3]
    p_ref, q_ref, s_ref = refs[2 * majors - 3 :]
    base = sums[0][...]
    g = jnp.ones((1, DH), F32)
    f = jnp.zeros((DH, DH), F32)
    for k in range(1, majors - 1):
        d = fades[k - 1]
        step = unpack_gain(d[DH:])
        if k == 1:
            g, f = step, d[:DH].astype(F32)
        else:
            old = d[:DH]
            f, g = step * f + g * old.astype(F32) + dot(old, f.astype(BF16)), g * step
        value = sums[k][...]
        base = base + g * value + dot(value.astype(BF16), f.astype(BF16))
    high = base.astype(BF16)
    for z in range(p_ref.shape[0]):
        out = unpack_gain(p_ref[z, DH:]) * base + q_ref[z] + dot(high, p_ref[z, :DH])
        s_ref[z] = out.astype(BF16)


def finish_kernel(heads, r_ref, qf_ref, s_ref, gate_ref, gain_ref, o_ref):
    gain = gain_ref[...]
    mean = jnp.full((DH, DH), 1.0 / DH, BF16)
    tiles = [
        (slice(c * CHUNK, (c + 1) * CHUNK), slice(h * DH, (h + 1) * DH), c, h)
        for c in range(qf_ref.shape[0])
        for h in range(heads)
    ]
    reads = [r_ref[rows, cols] + dot(qf_ref[c, h], beside(s_ref[h], s_ref[h]), NT) for rows, cols, c, h in tiles]
    squares = [dot(beside(*halves(r * r)), below(mean, mean)) for r in reads]
    for (rows, cols, c, h), r, square in zip(tiles, reads, squares):
        gate = gate_ref[rows, cols].astype(F32)
        r = r * lax.rsqrt(square + 1e-6) * gain
        o_ref[rows, cols] = (r * (gate / (1.0 + jnp.exp(-gate)))).astype(BF16)


def finish(readout, qf, state, out_gate, gain):
    rows, width = readout.shape
    heads = width // DH
    tok = pl.BlockSpec((PER * CHUNK, width), lambda c: (c, 0))
    return pl.pallas_call(
        functools.partial(finish_kernel, heads),
        grid=(rows // (PER * CHUNK),),
        in_specs=[
            tok,
            pl.BlockSpec((PER, heads, CHUNK, 2 * DH), lambda c: (c, 0, 0, 0)),
            pl.BlockSpec((heads, DH, DH), lambda c: (0, 0, 0)),
            tok,
            pl.BlockSpec((1, DH), lambda c: (0, 0)),
        ],
        out_specs=tok,
        out_shape=jax.ShapeDtypeStruct((rows, width), BF16),
        compiler_params=pltpu.CompilerParams(vmem_limit_bytes=VMEM),
        cost_estimate=pl.CostEstimate(flops=140_000_000, bytes_accessed=6_000_000, transcendentals=600_000),
        name="gated_readout",
    )(readout, qf, state, out_gate, gain)


def body(att_query, att_key, att_value, delta_query, delta_key, out_gate, log_decay, beta, norm_gain):
    heads = log_decay.shape[0]
    count = lax.axis_size("seq")
    minor = 2 * heads
    majors = count // minor
    place = lax.axis_index("seq")
    onward = [(s, s + 1) for s in range(count - 1)]
    k_prev = lax.ppermute(att_key, "seq", onward)
    v_prev = lax.ppermute(att_value, "seq", onward)
    copies = minor // heads
    m, ke, qe, qf, e, g, wire = prep(log_decay, beta, delta_key, delta_query, copies)
    own = own_part(att_query, att_key, att_value)
    lines = [[x * minor + z for z in range(minor)] for x in range(majors)]
    d_line = lax.all_to_all(wire, "seq", 0, 0, axis_index_groups=lines)
    first = jnp.reshape((place == 0).astype(jnp.int32), (1,))
    readout, b = attend(first, att_query, k_prev, att_key, v_prev, own, m, ke, qe, e, g)
    d_line, b = lax.optimization_barrier((d_line, b))
    p_line, d_total = vmem_call(
        prefix_kernel, [(d_line.shape, BF16), (d_line.shape[1:], BF16)], "decay_prefix", d_line
    )

    def from_lines(value, back):
        hops = back * minor
        return lax.ppermute(value, "seq", [(s, s + hops) for s in range(count - hops)])

    fades = [from_lines(d_total, k) for k in range(1, majors - 1)]
    b, p_line = lax.optimization_barrier((b, p_line))
    size = DH // copies
    b_line = lax.all_to_all(b.reshape(minor, size, DH), "seq", 0, 0, axis_index_groups=lines)
    q_line, b_total = vmem_call(
        line_kernel, [(b_line.shape, F32), ((size, DH), F32)], "line_states", d_line, b_line
    )
    sums = [from_lines(b_total, k) for k in range(1, majors)]
    (s_line,) = vmem_call(
        functools.partial(place_kernel, majors), [(b_line.shape, BF16)], "block_states", *sums, *fades, p_line, q_line
    )
    state = lax.all_to_all(s_line, "seq", 0, 0, axis_index_groups=lines).reshape(heads, DH, DH)
    return finish(readout, qf, state, out_gate, norm_gain.reshape(1, DH))


def solution(mesh):
    tokens = P(("doc", "seq"), "head")
    gates = P("head", ("doc", "seq"))
    return jax.shard_map(
        body,
        mesh=mesh,
        in_specs=(tokens,) * 6 + (gates, gates, P()),
        out_specs=tokens,
        check_vma=False,
    )
```

time: 154 us -> 122 us (0.79)
  Pallas kernels: 78.4 us -> 53.9 us
  starting transfers between devices: 12.5 us -> 36.5 us
  blocking collectives: 31.3 us -> 12.1 us
  between operations: 13.5 us -> 0.12 us
  waiting for transfers between devices: 14.9 us -> 17.8 us
    pallas_call x5 -> x7, Pallas kernels: 78.4 us -> 53.9 us  [the longest x1 22.7 us: prep(): pl.pallas_call(functools.partial(prep_kernel, heads, PER), grid=(chunks /...]
    all_to_all x2 -> x1, blocking collectives: 31.3 us -> 12.1 us  [body(): lax.all_to_all(s_line, 'seq', 0, 0, axis_index_groups=lines)]
    ppermute x0 -> x5, starting transfers between devices: none -> 13.2 us  [from_lines(): lax.ppermute(value, 'seq', [(s, s + hops) for s in range(count - hops)])]
    all_to_all x1 -> x2, starting transfers between devices: 4.84 us -> 15.7 us  [the longest x1 9.04 us: body(): lax.all_to_all(b.reshape(minor, size, DH), 'seq', 0, 0, axis_index_groups...]
    ppermute x1, waiting for transfers between devices: 0.01 us -> 10.8 us  [body(): k_prev = lax.ppermute(att_key, 'seq', onward)]
    all_gather x1 -> x0, waiting for transfers between devices: 9.41 us -> none  [body(): d_all = lax.all_gather(pieces, 'seq', axis_index_groups=lines)]
    ppermute x0 -> x5, waiting for transfers between devices: none -> 3.85 us  [from_lines(): lax.ppermute(value, 'seq', [(s, s + hops) for s in range(count - hops)])]
    all_to_all x1 -> x2, waiting for transfers between devices: 5.5 us -> 3.12 us  [the longest x1 3.12 us: body(): lax.all_to_all(b.reshape(minor, size, DH), 'seq', 0, 0, axis_index_groups...]
  transfers between devices with their start and end apart: 4 -> 9, of which waited for: 2 -> 3; matrix products, arithmetic and copies ran while one was open for 0% -> 0% of each run, Pallas kernels for 42% -> 38%
where the time goes in v2:
time: 122 us; the launch traced here: 121 us
  Pallas kernels  53.9 us (44%)
  starting transfers between devices  36.5 us (30%)
  waiting for transfers between devices  17.8 us (15%)
  blocking collectives  12.1 us (10%)
    pallas_call x1, Pallas kernels, prep(): pl.pallas_call(functools.partial(prep_kernel, heads, PER), grid=(chunks /...  22.7 us
    pallas_call x1, Pallas kernels, attend(): pl.pallas_call(attend_kernel, grid=(heads,), in_specs=[pl.BlockSpec(memor...  14.9 us
    ppermute x5, starting transfers between devices, from_lines(): lax.ppermute(value, 'seq', [(s, s + hops) for s in range(count - hops)])  13.2 us
    all_to_all x1, blocking collectives, body(): lax.all_to_all(s_line, 'seq', 0, 0, axis_index_groups=lines)  12.1 us
    ppermute x1, waiting for transfers between devices, body(): k_prev = lax.ppermute(att_key, 'seq', onward)  10.8 us
    all_to_all x1, starting transfers between devices, body(): lax.all_to_all(b.reshape(minor, size, DH), 'seq', 0, 0, axis_index_groups...  9.04 us
    pallas_call x1, Pallas kernels, own_part(): pl.pallas_call(own_kernel, grid=(heads,), in_specs=[tok, tok, tok], out_s...  7.33 us
    all_to_all x1, starting transfers between devices, body(): d_line = lax.all_to_all(wire, 'seq', 0, 0, axis_index_groups=lines)  6.68 us
  transfers between devices with their start and end apart: 9, of which 3 were waited for; matrix products, arithmetic and copies ran while one was open for 0% of the time, Pallas kernels for 38%

profile of v2, /device:TPU:18, one launch (start us, length us, event | category | flops | bytes accessed | tf_op | source)
XLA Modules:
  0.0 121.4 jit_solution(3860275454186416622)
XLA Ops:
  0.0 3.8 %collective-permute-start.1 = (bf16[1024,512]{1,0:T(8,128)(2,1)}, bf16[1024,512]{1,0:T(8,128)(2,1)S(1)}, u32[]{:S(2)}, u32[]{:S(2)}) collective-permute-start(bf16[1024,512]{1,0:T(8,128)(2,1)} %v_ref.1), channel_id=1, source_target_pairs={{0,4},{4,8},{8,12},{12,16},{16,20},{20,24},{24,28},{28,32},{32,36}... | collective-permute-start | bytes 3145736 | tf_op jit(solution)/shard_map/ppermute | solution.py:448
  3.8 3.8 %collective-permute-start = (bf16[1024,512]{1,0:T(8,128)(2,1)}, bf16[1024,512]{1,0:T(8,128)(2,1)S(1)}, u32[]{:S(2)}, u32[]{:S(2)}) collective-permute-start(bf16[1024,512]{1,0:T(8,128)(2,1)} %ko_ref.1), channel_id=1, source_target_pairs={{0,4},{4,8},{8,12},{12,16},{16,20},{20,24},{24,28},{28,32},{32,36}... | collective-permute-start | bytes 3145736 | tf_op jit(solution)/shard_map/ppermute | solution.py:447
  7.7 22.7 %delta_prep.1 = (bf16[8,4,128,128]{3,2,1,0:T(8,128)(2,1)}, bf16[8,4,128,256]{3,2,1,0:T(8,128)(2,1)}, bf16[8,4,128,128]{3,2,1,0:T(8,128)(2,1)}, bf16[8,4,128,256]...) custom-call(f32[4,1024]{1,0:T(4,128)} %ld_ref.1, ...), custom_call_target="tpu_custom_call" | custom-call | flops 1000000 | bytes 1000000 | tf_op jit(solution)/shard_map/delta_prep/pallas_call | solution.py:182
  30.3 6.7 %all-to-all-start = ((bf16[8,144,128]{2,1,0:T(8,128)(2,1)}), bf16[8,144,128]{2,1,0:T(8,128)(2,1)}, u32[]{:S(2)}, u32[]{:S(2)}) async-start(bf16[8,144,128]{2,1,0:T(8,128)(2,1)} %get-tuple-element.29), calls=%async_computation | async-start | bytes 589824 | tf_op jit(solution)/shard_map/all_to_all | solution.py:453
  37.0 7.3 %own_attention.1.own_ref = f32[1024,1024]{1,0:T(8,128)} custom-call(bf16[1024,512]{1,0:T(8,128)(2,1)} %q_ref.5, bf16[1024,512]{1,0:T(8,128)(2,1)} %ko_ref.1, bf16[1024,512]{1,0:T(8,128)(2,1)} %v_ref.1), custom_call_target="tpu_custom_call" | custom-call | flops 99999997952 | bytes 1000000 | tf_op jit(solution)/shard_map/own_attention/pallas_call | solution.py:231
  44.4 0.0 collective-permute-done.1.vp_ref
  44.4 0.0 copy-start
  44.4 10.8 %collective-permute-done.kp_ref = bf16[1024,512]{1,0:T(8,128)(2,1)S(1)} collective-permute-done((bf16[1024,512]{1,0:T(8,128)(2,1)}, bf16[1024,512]{1,0:T(8,128)(2,1)S(1)}, u32[]{:S(2)}, u32[]{:S(2)}) %collective-permute-start) | collective-permute-done | bytes 1048608 | tf_op jit(solution)/shard_map/ppermute | solution.py:447
  55.2 0.0 copy-start.1
  55.2 0.0 copy-done
  55.2 1.0 copy-done.1
  56.2 14.9 %window_attention.1 = (f32[1024,512]{1,0:T(8,128)}, bf16[4,128,128]{2,1,0:T(8,128)(2,1)}) custom-call(s32[1]{0:T(128)} %bitcast.first_ref, bf16[1024,512]{1,0:T(8,128)(2,1)} %q_ref.5, bf16[1024,512]{1,0:T(8,128)(2,1)} %copy-done.1, bf16[1024,512]{1,0:T(8,128)(2,1)} %ko_ref.1, bf16[1024,512]{1,0:T(8,128)(2,1)} %copy-done, f32[1024,1024]{1,0:T(8,128)} %own_attention.1.own_ref, ...), custom_call_target="tpu_custom_call" | custom-call | flops 99999997952 | bytes 1000000 | tf_op jit(solution)/shard_map/window_attention/pallas_call | solution.py:311
  71.1 0.0 all-to-all-done.d_ref
  71.1 1.9 %decay_prefix.1 = (bf16[8,144,128]{2,1,0:T(8,128)(2,1)S(1)}, bf16[144,128]{1,0:T(8,128)(2,1)S(1)}) custom-call(bf16[8,144,128]{2,1,0:T(8,128)(2,1)} %all-to-all-done.d_ref), custom_call_target="tpu_custom_call" | custom-call | flops 1000000 | bytes 1000000 | tf_op jit(solution)/shard_map/decay_prefix/pallas_call | solution.py:341
  73.0 9.0 %all-to-all-start.1 = ((bf16[8,64,128]{2,1,0:T(8,128)(2,1)}), bf16[8,64,128]{2,1,0:T(8,128)(2,1)S(1)}, u32[]{:S(2)}, u32[]{:S(2)}) async-start(bf16[8,64,128]{2,1,0:T(8,128)(2,1)} %bitcast.5), calls=%async_computation.1 | async-start | bytes 262144 | tf_op jit(solution)/shard_map/all_to_all | solution.py:468
  82.1 4.0 %collective-permute-start.6 = (bf16[144,128]{1,0:T(8,128)(2,1)S(1)}, bf16[144,128]{1,0:T(8,128)(2,1)S(1)}, u32[]{:S(2)}, u32[]{:S(2)}) collective-permute-start(bf16[144,128]{1,0:T(8,128)(2,1)S(1)} %get-tuple-element.36), channel_id=1, source_target_pairs={{0,64},{4,68},{8,72},{12,76},{16,80},{20,84},{24,88},{28,92},{32,9... | collective-permute-start | bytes 110600 | tf_op jit(solution)/shard_map/ppermute | solution.py:463
  86.1 1.9 %collective-permute-start.5 = (bf16[144,128]{1,0:T(8,128)(2,1)S(1)}, bf16[144,128]{1,0:T(8,128)(2,1)S(1)}, u32[]{:S(2)}, u32[]{:S(2)}) collective-permute-start(bf16[144,128]{1,0:T(8,128)(2,1)S(1)} %get-tuple-element.36), channel_id=1, source_target_pairs={{0,32},{4,36},{8,40},{12,44},{16,48},{20,52},{24,56},{28,60},{32,6... | collective-permute-start | bytes 110600 | tf_op jit(solution)/shard_map/ppermute | solution.py:463
  88.0 3.1 %all-to-all-done.1.b_ref = bf16[8,64,128]{2,1,0:T(8,128)(2,1)S(1)} async-done(((bf16[8,64,128]{2,1,0:T(8,128)(2,1)}), bf16[8,64,128]{2,1,0:T(8,128)(2,1)S(1)}, u32[]{:S(2)}, u32[]{:S(2)}) %all-to-all-start.1) | async-done | bytes 131104 | tf_op jit(solution)/shard_map/all_to_all | solution.py:468
  91.2 1.8 %line_states.1 = (f32[8,64,128]{2,1,0:T(8,128)S(1)}, f32[64,128]{1,0:T(8,128)S(1)}) custom-call(bf16[8,144,128]{2,1,0:T(8,128)(2,1)} %all-to-all-done.d_ref, bf16[8,64,128]{2,1,0:T(8,128)(2,1)S(1)} %all-to-all-done.1.b_ref), custom_call_target="tpu_custom_call" | custom-call | flops 1000000 | bytes 1000000 | tf_op jit(solution)/shard_map/line_states/pallas_call | solution.py:341
  93.0 0.7 collective-permute-start.4
  93.6 4.7 %collective-permute-start.3 = (f32[64,128]{1,0:T(8,128)S(1)}, f32[64,128]{1,0:T(8,128)S(1)}, u32[]{:S(2)}, u32[]{:S(2)}) collective-permute-start(f32[64,128]{1,0:T(8,128)S(1)} %get-tuple-element.35), channel_id=1, source_target_pairs={{0,64},{4,68},{8,72},{12,76},{16,80},{20,84},{24,88},{28,92},{32,9... | collective-permute-start | bytes 98312 | tf_op jit(solution)/shard_map/ppermute | solution.py:463
  98.3 1.9 %collective-permute-start.2 = (f32[64,128]{1,0:T(8,128)S(1)}, f32[64,128]{1,0:T(8,128)S(1)}, u32[]{:S(2)}, u32[]{:S(2)}) collective-permute-start(f32[64,128]{1,0:T(8,128)S(1)} %get-tuple-element.35), channel_id=1, source_target_pairs={{0,32},{4,36},{8,40},{12,44},{16,48},{20,52},{24,56},{28,60},{32,6... | collective-permute-start | bytes 98312 | tf_op jit(solution)/shard_map/ppermute | solution.py:463
  100.2 0.0 collective-permute-done.6.refs_4_
  100.2 0.0 collective-permute-done.5.refs_3_
  100.2 0.0 collective-permute-done.4.refs_2_
  100.3 0.0 collective-permute-done.3.refs_1_
  100.3 3.8 %collective-permute-done.2.refs_0_ = f32[64,128]{1,0:T(8,128)S(1)} collective-permute-done((f32[64,128]{1,0:T(8,128)S(1)}, f32[64,128]{1,0:T(8,128)S(1)}, u32[]{:S(2)}, u32[]{:S(2)}) %collective-permute-start.2) | collective-permute-done | bytes 32800 | tf_op jit(solution)/shard_map/ppermute | solution.py:463
  104.1 0.5 block_states.1
  104.6 12.1 %all_to_all.15 = bf16[8,64,128]{2,1,0:T(8,128)(2,1)} all-to-all(bf16[8,64,128]{2,1,0:T(8,128)(2,1)S(1)} %block_states.1), channel_id=1, replica_groups={{0,4,8,12,16,20,24,28},{32,36,40,44,48,52,56,60},{64,68,72,76,80,84,88,..., dimensions={0} | all-to-all | bytes 262144 | tf_op jit(solution)/shard_map/all_to_all | solution.py:476
  116.7 4.7 %gated_readout.1 = bf16[1024,512]{1,0:T(8,128)(2,1)} custom-call(f32[1024,512]{1,0:T(8,128)} %get-tuple-element.27.r_ref, bf16[8,4,128,256]{3,2,1,0:T(8,128)(2,1)} %get-tuple-element.28.qf_ref, bf16[4,128,128]{2,1,0:T(8,128)(2,1)} %bitcast.4, bf16[1024,512]{1,0:T(8,128)(2,1)} %gate_ref.1, f32[1,128]{1,0:T(1,128)} %bitcast.6), custom_call_target="tpu_custom_call" | custom-call | flops 140000000 | bytes 6000000 | tf_op jit(solution)/shard_map/gated_readout/pallas_call | solution.py:422
Async XLA Ops:
  0.0 44.4 %collective-permute-start.1 = (bf16[1024,512]{1,0:T(8,128)(2,1)}, bf16[1024,512]{1,0:T(8,128)(2,1)S(1)}, u32[]{:S(2)}, u32[]{:S(2)}) collective-permute-start(bf16[1024,512]{1,0:T(8,128)(2,1)} %v_ref.1), channel_id=1, source_target_pairs={{0,4},{4,8},{8,12},{12,16},{16,20},{20,24},{24,28},{28,32},{32,36}... | collective-permute-start | bytes 3145736 | tf_op jit(solution)/shard_map/ppermute | solution.py:448
  3.8 51.4 %collective-permute-start = (bf16[1024,512]{1,0:T(8,128)(2,1)}, bf16[1024,512]{1,0:T(8,128)(2,1)S(1)}, u32[]{:S(2)}, u32[]{:S(2)}) collective-permute-start(bf16[1024,512]{1,0:T(8,128)(2,1)} %ko_ref.1), channel_id=1, source_target_pairs={{0,4},{4,8},{8,12},{12,16},{16,20},{20,24},{24,28},{28,32},{32,36}... | collective-permute-start | bytes 3145736 | tf_op jit(solution)/shard_map/ppermute | solution.py:447
  30.3 40.7 %all-to-all-start = ((bf16[8,144,128]{2,1,0:T(8,128)(2,1)}), bf16[8,144,128]{2,1,0:T(8,128)(2,1)}, u32[]{:S(2)}, u32[]{:S(2)}) async-start(bf16[8,144,128]{2,1,0:T(8,128)(2,1)} %get-tuple-element.29), calls=%async_computation | async-start | bytes 589824 | tf_op jit(solution)/shard_map/all_to_all | solution.py:453
  44.4 10.8 %copy-start = (bf16[1024,512]{1,0:T(8,128)(2,1)}, bf16[1024,512]{1,0:T(8,128)(2,1)S(1)}, u32[]{:S(2)}) copy-start(bf16[1024,512]{1,0:T(8,128)(2,1)S(1)} %collective-permute-done.1.vp_ref) | copy-start | bytes 3145732
  55.2 1.0 copy-start.1
  73.0 18.1 %all-to-all-start.1 = ((bf16[8,64,128]{2,1,0:T(8,128)(2,1)}), bf16[8,64,128]{2,1,0:T(8,128)(2,1)S(1)}, u32[]{:S(2)}, u32[]{:S(2)}) async-start(bf16[8,64,128]{2,1,0:T(8,128)(2,1)} %bitcast.5), calls=%async_computation.1 | async-start | bytes 262144 | tf_op jit(solution)/shard_map/all_to_all | solution.py:468
  82.1 18.1 %collective-permute-start.6 = (bf16[144,128]{1,0:T(8,128)(2,1)S(1)}, bf16[144,128]{1,0:T(8,128)(2,1)S(1)}, u32[]{:S(2)}, u32[]{:S(2)}) collective-permute-start(bf16[144,128]{1,0:T(8,128)(2,1)S(1)} %get-tuple-element.36), channel_id=1, source_target_pairs={{0,64},{4,68},{8,72},{12,76},{16,80},{20,84},{24,88},{28,92},{32,9... | collective-permute-start | bytes 110600 | tf_op jit(solution)/shard_map/ppermute | solution.py:463
  86.1 14.1 %collective-permute-start.5 = (bf16[144,128]{1,0:T(8,128)(2,1)S(1)}, bf16[144,128]{1,0:T(8,128)(2,1)S(1)}, u32[]{:S(2)}, u32[]{:S(2)}) collective-permute-start(bf16[144,128]{1,0:T(8,128)(2,1)S(1)} %get-tuple-element.36), channel_id=1, source_target_pairs={{0,32},{4,36},{8,40},{12,44},{16,48},{20,52},{24,56},{28,60},{32,6... | collective-permute-start | bytes 110600 | tf_op jit(solution)/shard_map/ppermute | solution.py:463
  93.0 7.3 %collective-permute-start.4 = (f32[64,128]{1,0:T(8,128)S(1)}, f32[64,128]{1,0:T(8,128)S(1)}, u32[]{:S(2)}, u32[]{:S(2)}) collective-permute-start(f32[64,128]{1,0:T(8,128)S(1)} %get-tuple-element.35), channel_id=1, source_target_pairs={{0,96},{4,100},{8,104},{12,108},{16,112},{20,116},{24,120},{28,124... | collective-permute-start | bytes 98312 | tf_op jit(solution)/shard_map/ppermute | solution.py:463
  93.6 6.6 %collective-permute-start.3 = (f32[64,128]{1,0:T(8,128)S(1)}, f32[64,128]{1,0:T(8,128)S(1)}, u32[]{:S(2)}, u32[]{:S(2)}) collective-permute-start(f32[64,128]{1,0:T(8,128)S(1)} %get-tuple-element.35), channel_id=1, source_target_pairs={{0,64},{4,68},{8,72},{12,76},{16,80},{20,84},{24,88},{28,92},{32,9... | collective-permute-start | bytes 98312 | tf_op jit(solution)/shard_map/ppermute | solution.py:463
  98.3 5.8 %collective-permute-start.2 = (f32[64,128]{1,0:T(8,128)S(1)}, f32[64,128]{1,0:T(8,128)S(1)}, u32[]{:S(2)}, u32[]{:S(2)}) collective-permute-start(f32[64,128]{1,0:T(8,128)S(1)} %get-tuple-element.35), channel_id=1, source_target_pairs={{0,32},{4,36},{8,40},{12,44},{16,48},{20,52},{24,56},{28,60},{32,6... | collective-permute-start | bytes 98312 | tf_op jit(solution)/shard_map/ppermute | solution.py:463

commit v3 on v2

--- a/solution.py
+++ b/solution.py
@@ -43,6 +43,21 @@
     return jnp.concatenate(parts, axis=0)
 
 
+def diagonal(one, two):
+    return below(beside(one, jnp.zeros_like(two)), beside(jnp.zeros_like(one), two))
+
+
+def odd_rows(value, size):
+    return below(*[value[i : i + size] for i in range(size, value.shape[0], 2 * size)])
+
+
+def less_odd_rows(value, change, size):
+    parts = []
+    for n, i in enumerate(range(0, value.shape[0], 2 * size)):
+        parts += [value[i : i + size], value[i + size : i + 2 * size] - change[n * size : (n + 1) * size]]
+    return below(*parts)
+
+
 def split_three(g):
     high = g.astype(BF16)
     rest = g - high.astype(F32)
@@ -91,6 +106,8 @@
     eye = jnp.where(ti == tj, 1.0, 0.0)
     state = []
     ts = []
+    products = []
+    diags = []
     for c in range(per):
         part = slice(c * CHUNK, (c + 1) * CHUNK)
         rows = gate_rows(heads, ld_ref[:, part], be_ref[:, part])
@@ -104,58 +121,85 @@
             keys.append((k, kf, rk))
             colmat = jnp.where(tj == h, rk, colmat)
         rowmat = jnp.transpose(colmat)
+        for h in range(0, heads, 2):
+            two = slice(h * DH, (h + 2) * DH)
+            kd = diagonal(keys[h][0], keys[h + 1][0])
+            diags.append(kd)
+            kk2 = dot(k_ref[part, two], kd, NT)
+            qk2 = dot(q_ref[part, two], kd, NT)
+            products.append((kk2[:, :CHUNK], qk2[:, :CHUNK]))
+            products.append((kk2[:, CHUNK:], qk2[:, CHUNK:]))
         for h in range(heads):
             k, kf, rk_c = keys[h]
+            kk, qk = products[c * heads + h]
             rk_r = rowmat[h : h + 1]
-            q = q_ref[part, h * DH : (h + 1) * DH]
-            qf = q.astype(F32)
+            qf = q_ref[part, h * DH : (h + 1) * DH].astype(F32)
             rq_c = lax.rsqrt(jnp.sum(qf * qf, axis=1, keepdims=True) + 1e-6)
             g_c = cols[:, h : h + 1]
             g_r = rows[h : h + 1]
             b_c = cols[:, heads + h : heads + h + 1]
             b_r = rows[heads + h : heads + h + 1]
             decay = jnp.exp(jnp.where(ti >= tj, g_c - g_r, NEG)) * rk_r
-            kk = dot(k, k, NT)
-            qk = dot(q, k, NT)
             a = beside(*halves(decay * rq_c * qk))
             low = jnp.where(ti > tj, decay * (b_c * rk_c) * kk, 0.0)
             ts.append(eye - jnp.where((ti >> 1) == (tj >> 1), low, 0.0))
-            state.append((k, kf, rk_c, rk_r, qf, rq_c, g_c, g_r, b_r, a, low))
+            state.append((kf, rk_c, rk_r, qf, rq_c, g_c, g_r, b_r, a, low))
+    count = per * heads
     for shift in range(1, 7):
         pair = (ti >> (shift + 1)) == (tj >> (shift + 1))
         cross = pair & (((ti >> shift) & 1) == 1) & (((tj >> shift) & 1) == 0)
+        size = 1 << shift
         tb = [t.astype(BF16) for t in ts]
+        lead = [odd_rows(t, size).astype(BF16) for t in ts] if size >= 8 else tb
         lm = [below(*halves(jnp.where(cross, s[-1], 0.0))) for s in state]
-        mid = [dot(beside(x, x), y).astype(BF16) for x, y in zip(tb, lm)]
-        ts = [t - dot(x, y) for t, x, y in zip(ts, mid, tb)]
+        mid = [dot(beside(x, x), y).astype(BF16) for x, y in zip(lead, lm)]
+        change = []
+        for n in range(0, count, 2):
+            both = dot(beside(mid[n], mid[n + 1]), diagonal(tb[n], tb[n + 1]))
+            change += [both[:, :CHUNK], both[:, CHUNK:]]
+        if size >= 8:
+            ts = [less_odd_rows(t, x, size) for t, x in zip(ts, change)]
+        else:
+            ts = [t - x for t, x in zip(ts, change)]
+    ws = []
+    for n in range(0, count, 2):
+        lead = []
+        for s, t in zip(state[n : n + 2], ts[n : n + 2]):
+            lead.append((t * (s[7] * jnp.exp(s[6]) * s[2])).astype(BF16))
+        both = dot(beside(*lead), diags[n // 2])
+        ws += [both[:, :DH], both[:, DH:]]
+    starts = []
+    for n in range(count):
+        c, h = n // heads, n % heads
+        kf, rk_c, rk_r, qf, rq_c, g_c, g_r, b_r, a, low = state[n]
+        t, w = ts[n], ws[n]
+        tail_c = jnp.exp(g_r[:, CHUNK - 1 : CHUNK] - g_c) * rk_c
+        tw = beside(t.astype(BF16), w.astype(BF16))
+        both = dot(a, below(tw, tw))
+        m_ref[c, h] = (both[:, :CHUNK] * b_r).astype(BF16)
+        qe = (jnp.exp(g_c) * rq_c) * qf - both[:, CHUNK:]
+        kt = jnp.transpose(kf).astype(BF16)
+        th, tl = halves(tail_c * t * b_r)
+        wh, wl = halves(tail_c * w)
+        both = dot(beside(kt, kt), below(beside(th, wh), beside(tl, wl)))
+        ke_ref[c, h] = beside(*halves(both[:, :CHUNK]))
+        e = -both[:, CHUNK:]
+        qeb, eb = qe.astype(BF16), e.astype(BF16)
+        qe_ref[c, h] = qeb
+        e_ref[c, h] = eb
+        starts.append((qe, e, below(qeb, eb), jnp.broadcast_to(jnp.exp(g_r[:, CHUNK - 1 : CHUNK]), (1, DH))))
     for c in range(per):
-        for h in range(heads):
-            k, kf, rk_c, rk_r, qf, rq_c, g_c, g_r, b_r, a, low = state[c * heads + h]
-            t = ts[c * heads + h]
-            g_end = g_r[:, CHUNK - 1 : CHUNK]
-            tail_c = jnp.exp(g_end - g_c) * rk_c
-            w = dot((t * (b_r * jnp.exp(g_r) * rk_r)).astype(BF16), k)
-            wb = w.astype(BF16)
-            tw = beside(t.astype(BF16), wb)
-            both = dot(a, below(tw, tw))
-            m_ref[c, h] = (both[:, :CHUNK] * b_r).astype(BF16)
-            qe = (jnp.exp(g_c) * rq_c) * qf - both[:, CHUNK:]
-            qeb = qe.astype(BF16)
-            kt = jnp.transpose(kf).astype(BF16)
-            ke = dot(beside(kt, kt), below(*halves(tail_c * t * b_r)))
-            ke_ref[c, h] = beside(*halves(ke))
-            e = -dot(kt, (tail_c * w).astype(BF16))
-            eb = e.astype(BF16)
-            gc = jnp.broadcast_to(jnp.exp(g_end), (1, DH))
-            gp = gp_scr[h : h + 1]
-            f = f_scr[h]
-            fb = f.astype(BF16)
-            qe_ref[c, h] = qeb
-            qf_ref[c, h] = beside(*halves(gp * qe + dot(qeb, fb)))
-            e_ref[c, h] = eb
-            f_scr[h] = gc * f + gp * e + dot(eb, fb)
-            gp_scr[h : h + 1] = gp * gc
-            g_ref[c, h : h + 1] = gc
+        for h in range(0, heads, 2):
+            ones = starts[c * heads + h : c * heads + h + 2]
+            fs = [f_scr[h], f_scr[h + 1]]
+            both = dot(beside(ones[0][2], ones[1][2]), diagonal(fs[0].astype(BF16), fs[1].astype(BF16)))
+            for n, (qe, e, _, gc) in enumerate(ones):
+                part = both[:, n * DH : (n + 1) * DH]
+                gp = gp_scr[h + n : h + n + 1]
+                qf_ref[c, h + n] = beside(*halves(gp * qe + part[:CHUNK]))
+                f_scr[h + n] = gc * fs[n] + gp * e + part[CHUNK:]
+                gp_scr[h + n : h + n + 1] = gp * gc
+                g_ref[c, h + n : h + n + 1] = gc
 
     @pl.when(step == pl.num_programs(0) - 1)
     def _():
@@ -242,9 +286,10 @@
 
 
 def attend_kernel(
-    first_ref, q_ref, kp_ref, ko_ref, vp_ref, own_ref, m_ref, ke_ref, qe_ref, e_ref, g_ref, r_ref, b_ref, kx, vx
+    base, first_ref, q_ref, kp_ref, ko_ref, vp_ref, own_ref, m_ref, ke_ref, qe_ref, e_ref, g_ref, *rest
 ):
-    h = pl.program_id(0)
+    r_ref, b_ref, kx, vx = rest[-4:]
+    h = pl.program_id(0) + base
     first = first_ref[0]
     window = kp_ref.shape[0]
     vx[:, :DH] = vp_ref[...]
@@ -301,39 +346,42 @@
     b_ref[0] = jnp.transpose(x).astype(BF16)
 
 
-def attend(first, att_query, k_prev, k_own, v_prev, own, m, ke, qe, e, g):
+def attend(base, first, att_query, k_prev, k_own, v_prev, own, m, ke, qe, e, g, *earlier):
     rows, width = att_query.shape
     heads = width // DH
-    window = k_prev.shape[0]
+    window, held = k_prev.shape
     chunks = rows // CHUNK
-    big = pl.BlockSpec((chunks, 1, CHUNK, DH), lambda h: (0, h, 0, 0))
-    tok = pl.BlockSpec((rows, DH), lambda h: (0, h))
+    big = pl.BlockSpec((chunks, 1, CHUNK, DH), lambda h: (0, h + base, 0, 0))
+    tok = pl.BlockSpec((rows, DH), lambda h: (0, h + base))
+    prev = pl.BlockSpec((window, DH), lambda h: (0, h))
     return pl.pallas_call(
-        attend_kernel,
-        grid=(heads,),
+        functools.partial(attend_kernel, base),
+        grid=(held // DH,),
         in_specs=[
             pl.BlockSpec(memory_space=pltpu.SMEM),
             tok,
-            pl.BlockSpec((window, DH), lambda h: (0, h)),
-            pl.BlockSpec((16, DH), lambda h: (0, h)),
-            pl.BlockSpec((window, DH), lambda h: (0, h)),
-            pl.BlockSpec((rows, 2 * DH), lambda h: (0, h)),
+            prev,
+            pl.BlockSpec((16, DH), lambda h: (0, h + base)),
+            prev,
+            pl.BlockSpec((rows, 2 * DH), lambda h: (0, h + base)),
             big,
-            pl.BlockSpec((chunks, 1, CHUNK, 2 * DH), lambda h: (0, h, 0, 0)),
+            pl.BlockSpec((chunks, 1, CHUNK, 2 * DH), lambda h: (0, h + base, 0, 0)),
             big,
             big,
             pl.BlockSpec((chunks, heads, DH), lambda h: (0, 0, 0)),
-        ],
-        out_specs=[tok, pl.BlockSpec((1, DH, DH), lambda h: (h, 0, 0))],
+        ]
+        + [pl.BlockSpec(memory_space=pl.ANY)] * len(earlier),
+        out_specs=[tok, pl.BlockSpec((1, DH, DH), lambda h: (h + base, 0, 0))],
         out_shape=[
             jax.ShapeDtypeStruct((rows, width), F32),
             jax.ShapeDtypeStruct((heads, DH, DH), BF16),
         ],
+        input_output_aliases={11 + n: n for n in range(len(earlier))},
         scratch_shapes=[pltpu.VMEM((window, DH), BF16), pltpu.VMEM((window, 2 * DH), BF16)],
         compiler_params=pltpu.CompilerParams(vmem_limit_bytes=MIDDLE),
         cost_estimate=pl.CostEstimate(flops=100_000_000_000, bytes_accessed=1_000_000, transcendentals=0),
         name="window_attention",
-    )(first, att_query, k_prev, k_own, v_prev, own, m, ke, qe, e, g)
+    )(first, att_query, k_prev, k_own, v_prev, own, m, ke, qe, e, g, *earlier)
 
 
 def vmem_call(kernel, outs, name, *args):
@@ -444,16 +492,18 @@
     majors = count // minor
     place = lax.axis_index("seq")
     onward = [(s, s + 1) for s in range(count - 1)]
-    k_prev = lax.ppermute(att_key, "seq", onward)
-    v_prev = lax.ppermute(att_value, "seq", onward)
+    half = heads // 2 * DH
+    k_first = lax.ppermute(att_key[:, :half], "seq", onward)
+    v_first = lax.ppermute(att_value[:, :half], "seq", onward)
     copies = minor // heads
     m, ke, qe, qf, e, g, wire = prep(log_decay, beta, delta_key, delta_query, copies)
-    own = own_part(att_query, att_key, att_value)
+    wire, k_rest, v_rest = lax.optimization_barrier((wire, att_key[:, half:], att_value[:, half:]))
     lines = [[x * minor + z for z in range(minor)] for x in range(majors)]
     d_line = lax.all_to_all(wire, "seq", 0, 0, axis_index_groups=lines)
-    first = jnp.reshape((place == 0).astype(jnp.int32), (1,))
-    readout, b = attend(first, att_query, k_prev, att_key, v_prev, own, m, ke, qe, e, g)
-    d_line, b = lax.optimization_barrier((d_line, b))
+    k_rest = lax.ppermute(k_rest, "seq", onward)
+    v_rest = lax.ppermute(v_rest, "seq", onward)
+    own = own_part(att_query, att_key, att_value)
+    d_line, own = lax.optimization_barrier((d_line, own))
     p_line, d_total = vmem_call(
         prefix_kernel, [(d_line.shape, BF16), (d_line.shape[1:], BF16)], "decay_prefix", d_line
     )
@@ -463,7 +513,12 @@
         return lax.ppermute(value, "seq", [(s, s + hops) for s in range(count - hops)])
 
     fades = [from_lines(d_total, k) for k in range(1, majors - 1)]
-    b, p_line = lax.optimization_barrier((b, p_line))
+    own, p_line = lax.optimization_barrier((own, p_line))
+    first = jnp.reshape((place == 0).astype(jnp.int32), (1,))
+    coefs = (own, m, ke, qe, e, g)
+    early = attend(0, first, att_query, k_first, att_key, v_first, *coefs)
+    early, fades = lax.optimization_barrier((early, fades))
+    readout, b = attend(half // DH, first, att_query, k_rest, att_key, v_rest, *coefs, *early)
     size = DH // copies
     b_line = lax.all_to_all(b.reshape(minor, size, DH), "seq", 0, 0, axis_index_groups=lines)
     q_line, b_total = vmem_call(

time: 122 us -> 118 us (0.967)
  blocking collectives: 12.1 us -> 24.9 us
  waiting for transfers between devices: 17.8 us -> 5.84 us
  Pallas kernels: 53.9 us -> 48.1 us
  local copies, waits for them, and re-layouts: 0.97 us -> 3.46 us
  starting transfers between devices: 36.5 us -> 34.5 us
    all_to_all x0 -> x1, blocking collectives: none -> 12.8 us  [body(): lax.all_to_all(b.reshape(minor, size, DH), 'seq', 0, 0, axis_index_groups...]
    ppermute x2 -> x4, waiting for transfers between devices: 10.8 us -> 0.01 us  [the longest x1 0.01 us: body(): k_first = lax.ppermute(att_key[:, :half], 'seq', onward)]
    all_to_all x1 -> x0, starting transfers between devices: 9.04 us -> none  [body(): lax.all_to_all(b.reshape(minor, size, DH), 'seq', 0, 0, axis_index_groups...]
    ppermute x2 -> x4, starting transfers between devices: 7.64 us -> 14.9 us  [the longest x1 3.92 us: body(): k_rest = lax.ppermute(k_rest, 'seq', onward)]
    pallas_call x1, Pallas kernels: 22.7 us -> 16.2 us  [prep(): pl.pallas_call(functools.partial(prep_kernel, heads, PER), grid=(chunks /...]
    all_to_all x1 -> x0, waiting for transfers between devices: 3.12 us -> none  [body(): lax.all_to_all(b.reshape(minor, size, DH), 'seq', 0, 0, axis_index_groups...]
    slice x0 -> x1, local copies, waits for them, and re-layouts: none -> 2.68 us  [body(): v_first = lax.ppermute(att_value[:, :half], 'seq', onward)]
    pallas_call x1 -> x2, Pallas kernels: 14.9 us -> 17.5 us  [attend(): pl.pallas_call(functools.partial(attend_kernel, base), grid=(held // DH,)...]
  transfers between devices with their start and end apart: 9 -> 10, of which waited for: 3 -> 2; matrix products, arithmetic and copies ran while one was open for 0% -> 0% of each run, Pallas kernels for 38% -> 28%
where the time goes in v3:
time: 118 us; the launch traced here: 117 us
  Pallas kernels  48.1 us (41%)
  starting transfers between devices  34.5 us (29%)
  blocking collectives  24.9 us (21%)
  waiting for transfers between devices  5.84 us (5%)
  local copies, waits for them, and re-layouts  3.46 us (3%)
    pallas_call x2, Pallas kernels, attend(): pl.pallas_call(functools.partial(attend_kernel, base), grid=(held // DH,)...  17.5 us
    pallas_call x1, Pallas kernels, prep(): pl.pallas_call(functools.partial(prep_kernel, heads, PER), grid=(chunks /...  16.2 us
    ppermute x5, starting transfers between devices, from_lines(): lax.ppermute(value, 'seq', [(s, s + hops) for s in range(count - hops)])  12.9 us
    all_to_all x1, blocking collectives, body(): lax.all_to_all(b.reshape(minor, size, DH), 'seq', 0, 0, axis_index_groups...  12.8 us
    all_to_all x1, blocking collectives, body(): lax.all_to_all(s_line, 'seq', 0, 0, axis_index_groups=lines)  12.1 us
    pallas_call x1, Pallas kernels, own_part(): pl.pallas_call(own_kernel, grid=(heads,), in_specs=[tok, tok, tok], out_s...  7.35 us
    all_to_all x1, starting transfers between devices, body(): d_line = lax.all_to_all(wire, 'seq', 0, 0, axis_index_groups=lines)  6.68 us
    ppermute x5, waiting for transfers between devices, from_lines(): lax.ppermute(value, 'seq', [(s, s + hops) for s in range(count - hops)])  5.83 us
  transfers between devices with their start and end apart: 10, of which 2 were waited for; matrix products, arithmetic and copies ran while one was open for 0% of the time, Pallas kernels for 28%

profile of v3, /device:TPU:18, one launch (start us, length us, event | category | flops | bytes accessed | tf_op | source)
XLA Modules:
  0.0 117.1 jit_solution(11649142942162613176)
XLA Ops:
  0.0 2.7 %fusion = (bf16[1024,256]{1,0:T(8,128)(2,1)S(1)}, bf16[1024,256]{1,0:T(8,128)(2,1)}, bf16[1024,256]{1,0:T(8,128)(2,1)}, bf16[1024,256]{1,0:T(8,128)(2,1)S(1)}) fusion(bf16[1024,512]{1,0:T(8,128)(2,1)} %v_ref.1, bf16[1024,512]{1,0:T(8,128)(2,1)} %ko_ref.3), kind=kLoop, calls=%fused_computation | loop fusion | bytes 4194304 | tf_op jit(solution)/shard_map/slice | solution.py:497
  2.7 3.8 %collective-permute-start.3 = (bf16[1024,256]{1,0:T(8,128)(2,1)S(1)}, bf16[1024,256]{1,0:T(8,128)(2,1)S(1)}, u32[]{:S(2)}, u32[]{:S(2)}) collective-permute-start(bf16[1024,256]{1,0:T(8,128)(2,1)S(1)} %get-tuple-element.57), channel_id=1, source_target_pairs={{0,4},{4,8},{8,12},{12,16},{16,20},{20,24},{24,28},{28,32},{32,36}... | collective-permute-start | bytes 1572872 | tf_op jit(solution)/shard_map/ppermute | solution.py:497
  6.5 3.8 %collective-permute-start.2 = (bf16[1024,256]{1,0:T(8,128)(2,1)S(1)}, bf16[1024,256]{1,0:T(8,128)(2,1)S(1)}, u32[]{:S(2)}, u32[]{:S(2)}) collective-permute-start(bf16[1024,256]{1,0:T(8,128)(2,1)S(1)} %get-tuple-element.62), channel_id=1, source_target_pairs={{0,4},{4,8},{8,12},{12,16},{16,20},{20,24},{24,28},{28,32},{32,36}... | collective-permute-start | bytes 1572872 | tf_op jit(solution)/shard_map/ppermute | solution.py:496
  10.3 16.2 %delta_prep.1 = (bf16[8,4,128,128]{3,2,1,0:T(8,128)(2,1)}, bf16[8,4,128,256]{3,2,1,0:T(8,128)(2,1)}, bf16[8,4,128,128]{3,2,1,0:T(8,128)(2,1)}, bf16[8,4,128,256]...) custom-call(f32[4,1024]{1,0:T(4,128)} %ld_ref.1, ...), custom_call_target="tpu_custom_call" | custom-call | flops 1000000 | bytes 1000000 | tf_op jit(solution)/shard_map/delta_prep/pallas_call | solution.py:226
  26.6 6.7 %all-to-all-start = ((bf16[8,144,128]{2,1,0:T(8,128)(2,1)}), bf16[8,144,128]{2,1,0:T(8,128)(2,1)S(1)}, u32[]{:S(2)}, u32[]{:S(2)}) async-start(bf16[8,144,128]{2,1,0:T(8,128)(2,1)} %get-tuple-element.34), calls=%async_computation | async-start | bytes 589824 | tf_op jit(solution)/shard_map/all_to_all | solution.py:502
  33.3 3.9 %collective-permute-start = (bf16[1024,256]{1,0:T(8,128)(2,1)}, bf16[1024,256]{1,0:T(8,128)(2,1)}, u32[]{:S(2)}, u32[]{:S(2)}) collective-permute-start(bf16[1024,256]{1,0:T(8,128)(2,1)} %get-tuple-element.32), channel_id=1, source_target_pairs={{0,4},{4,8},{8,12},{12,16},{16,20},{20,24},{24,28},{28,32},{32,36}... | collective-permute-start | bytes 1572872 | tf_op jit(solution)/shard_map/ppermute | solution.py:503
  37.2 3.4 %collective-permute-start.1 = (bf16[1024,256]{1,0:T(8,128)(2,1)}, bf16[1024,256]{1,0:T(8,128)(2,1)}, u32[]{:S(2)}, u32[]{:S(2)}) collective-permute-start(bf16[1024,256]{1,0:T(8,128)(2,1)} %get-tuple-element.33), channel_id=1, source_target_pairs={{0,4},{4,8},{8,12},{12,16},{16,20},{20,24},{24,28},{28,32},{32,36}... | collective-permute-start | bytes 1572872 | tf_op jit(solution)/shard_map/ppermute | solution.py:504
  40.6 7.4 %own_attention.1.own_ref = f32[1024,1024]{1,0:T(8,128)} custom-call(bf16[1024,512]{1,0:T(8,128)(2,1)} %q_ref.7, bf16[1024,512]{1,0:T(8,128)(2,1)} %ko_ref.3, bf16[1024,512]{1,0:T(8,128)(2,1)} %v_ref.1), custom_call_target="tpu_custom_call" | custom-call | flops 99999997952 | bytes 1000000 | tf_op jit(solution)/shard_map/own_attention/pallas_call | solution.py:275
  47.9 0.0 all-to-all-done.d_ref
  47.9 1.0 decay_prefix.1
  48.9 4.0 %collective-permute-start.5 = (bf16[144,128]{1,0:T(8,128)(2,1)S(1)}, bf16[144,128]{1,0:T(8,128)(2,1)S(1)}, u32[]{:S(2)}, u32[]{:S(2)}) collective-permute-start(bf16[144,128]{1,0:T(8,128)(2,1)S(1)} %get-tuple-element.46), channel_id=1, source_target_pairs={{0,64},{4,68},{8,72},{12,76},{16,80},{20,84},{24,88},{28,92},{32,9... | collective-permute-start | bytes 110600 | tf_op jit(solution)/shard_map/ppermute | solution.py:513
  52.9 0.0 collective-permute-done.3.vp_ref
  53.0 2.1 %collective-permute-start.4 = (bf16[144,128]{1,0:T(8,128)(2,1)S(1)}, bf16[144,128]{1,0:T(8,128)(2,1)S(1)}, u32[]{:S(2)}, u32[]{:S(2)}) collective-permute-start(bf16[144,128]{1,0:T(8,128)(2,1)S(1)} %get-tuple-element.46), channel_id=1, source_target_pairs={{0,32},{4,36},{8,40},{12,44},{16,48},{20,52},{24,56},{28,60},{32,6... | collective-permute-start | bytes 110600 | tf_op jit(solution)/shard_map/ppermute | solution.py:513
  55.1 0.0 collective-permute-done.2.kp_ref
  55.1 0.8 copy-done.1
  55.9 8.8 %window_attention.2 = (f32[1024,512]{1,0:T(8,128)}, bf16[4,128,128]{2,1,0:T(8,128)(2,1)}) custom-call(s32[1]{0:T(128)} %bitcast.first_ref, bf16[1024,512]{1,0:T(8,128)(2,1)} %q_ref.7, bf16[1024,256]{1,0:T(8,128)(2,1)} %copy-done.1, bf16[1024,512]{1,0:T(8,128)(2,1)} %ko_ref.3, bf16[1024,256]{1,0:T(8,128)(2,1)} %copy-done, f32[1024,1024]{1,0:T(8,128)} %own_attention.1.own_ref, ...), custom_call_target="tpu_custom_call" | custom-call | flops 99999997952 | bytes 1000000 | tf_op jit(solution)/shard_map/window_attention/pallas_call | solution.py:357
  64.6 0.0 collective-permute-done.5.refs_4_
  64.6 2.0 %collective-permute-done.4.refs_3_ = bf16[144,128]{1,0:T(8,128)(2,1)S(1)} collective-permute-done((bf16[144,128]{1,0:T(8,128)(2,1)S(1)}, bf16[144,128]{1,0:T(8,128)(2,1)S(1)}, u32[]{:S(2)}, u32[]{:S(2)}) %collective-permute-start.4) | collective-permute-done | bytes 36896 | tf_op jit(solution)/shard_map/ppermute | solution.py:513
  66.6 0.0 collective-permute-done.kp_ref
  66.6 0.0 collective-permute-done.1.vp_ref
  66.6 8.8 %window_attention.3 = (f32[1024,512]{1,0:T(8,128)}, bf16[4,128,128]{2,1,0:T(8,128)(2,1)}) custom-call(s32[1]{0:T(128)} %bitcast.first_ref, bf16[1024,512]{1,0:T(8,128)(2,1)} %q_ref.7, bf16[1024,256]{1,0:T(8,128)(2,1)} %collective-permute-done.kp_ref, bf16[1024,512]{1,0:T(8,128)(2,1)} %ko_ref.3, ...), custom_call_target="tpu_custom_call", output_to_operand_aliasing={{0}: (11, {}), {1}: (12, {})} | custom-call | flops 99999997952 | bytes 1000000 | tf_op jit(solution)/shard_map/window_attention/pallas_call | solution.py:357
  75.4 12.8 %all_to_all.15.b_ref = bf16[8,64,128]{2,1,0:T(8,128)(2,1)S(1)} all-to-all(bf16[8,64,128]{2,1,0:T(8,128)(2,1)} %bitcast.5), channel_id=1, replica_groups={{0,4,8,12,16,20,24,28},{32,36,40,44,48,52,56,60},{64,68,72,76,80,84,88,..., dimensions={0} | all-to-all | bytes 262144 | tf_op jit(solution)/shard_map/all_to_all | solution.py:523
  88.2 0.8 line_states.1
  89.0 0.7 collective-permute-start.8
  89.7 4.2 %collective-permute-start.7 = (f32[64,128]{1,0:T(8,128)S(1)}, f32[64,128]{1,0:T(8,128)S(1)}, u32[]{:S(2)}, u32[]{:S(2)}) collective-permute-start(f32[64,128]{1,0:T(8,128)S(1)} %get-tuple-element.52), channel_id=1, source_target_pairs={{0,64},{4,68},{8,72},{12,76},{16,80},{20,84},{24,88},{28,92},{32,9... | collective-permute-start | bytes 98312 | tf_op jit(solution)/shard_map/ppermute | solution.py:513
  93.9 1.9 %collective-permute-start.6 = (f32[64,128]{1,0:T(8,128)S(1)}, f32[64,128]{1,0:T(8,128)S(1)}, u32[]{:S(2)}, u32[]{:S(2)}) collective-permute-start(f32[64,128]{1,0:T(8,128)S(1)} %get-tuple-element.52), channel_id=1, source_target_pairs={{0,32},{4,36},{8,40},{12,44},{16,48},{20,52},{24,56},{28,60},{32,6... | collective-permute-start | bytes 98312 | tf_op jit(solution)/shard_map/ppermute | solution.py:513
  95.8 0.0 collective-permute-done.8.refs_2_
  95.8 0.0 collective-permute-done.7.refs_1_
  95.9 3.9 %collective-permute-done.6.refs_0_ = f32[64,128]{1,0:T(8,128)S(1)} collective-permute-done((f32[64,128]{1,0:T(8,128)S(1)}, f32[64,128]{1,0:T(8,128)S(1)}, u32[]{:S(2)}, u32[]{:S(2)}) %collective-permute-start.6) | collective-permute-done | bytes 32800 | tf_op jit(solution)/shard_map/ppermute | solution.py:513
  99.7 0.5 block_states.1
  100.2 12.1 %all_to_all.16 = bf16[8,64,128]{2,1,0:T(8,128)(2,1)} all-to-all(bf16[8,64,128]{2,1,0:T(8,128)(2,1)S(1)} %block_states.1), channel_id=1, replica_groups={{0,4,8,12,16,20,24,28},{32,36,40,44,48,52,56,60},{64,68,72,76,80,84,88,..., dimensions={0} | all-to-all | bytes 262144 | tf_op jit(solution)/shard_map/all_to_all | solution.py:531
  112.3 4.7 %gated_readout.1 = bf16[1024,512]{1,0:T(8,128)(2,1)} custom-call(f32[1024,512]{1,0:T(8,128)} %get-tuple-element.49.r_ref, bf16[8,4,128,256]{3,2,1,0:T(8,128)(2,1)} %get-tuple-element.50.qf_ref, bf16[4,128,128]{2,1,0:T(8,128)(2,1)} %bitcast.4, bf16[1024,512]{1,0:T(8,128)(2,1)} %gate_ref.1, f32[1,128]{1,0:T(1,128)} %bitcast.6), custom_call_target="tpu_custom_call" | custom-call | flops 140000000 | bytes 6000000 | tf_op jit(solution)/shard_map/gated_readout/pallas_call | solution.py:470
  (3 shorter events, 0.0 us)
Async XLA Ops:
  2.7 50.3 %collective-permute-start.3 = (bf16[1024,256]{1,0:T(8,128)(2,1)S(1)}, bf16[1024,256]{1,0:T(8,128)(2,1)S(1)}, u32[]{:S(2)}, u32[]{:S(2)}) collective-permute-start(bf16[1024,256]{1,0:T(8,128)(2,1)S(1)} %get-tuple-element.57), channel_id=1, source_target_pairs={{0,4},{4,8},{8,12},{12,16},{16,20},{20,24},{24,28},{28,32},{32,36}... | collective-permute-start | bytes 1572872 | tf_op jit(solution)/shard_map/ppermute | solution.py:497
  6.5 48.6 %collective-permute-start.2 = (bf16[1024,256]{1,0:T(8,128)(2,1)S(1)}, bf16[1024,256]{1,0:T(8,128)(2,1)S(1)}, u32[]{:S(2)}, u32[]{:S(2)}) collective-permute-start(bf16[1024,256]{1,0:T(8,128)(2,1)S(1)} %get-tuple-element.62), channel_id=1, source_target_pairs={{0,4},{4,8},{8,12},{12,16},{16,20},{20,24},{24,28},{28,32},{32,36}... | collective-permute-start | bytes 1572872 | tf_op jit(solution)/shard_map/ppermute | solution.py:496
  26.6 21.3 %all-to-all-start = ((bf16[8,144,128]{2,1,0:T(8,128)(2,1)}), bf16[8,144,128]{2,1,0:T(8,128)(2,1)S(1)}, u32[]{:S(2)}, u32[]{:S(2)}) async-start(bf16[8,144,128]{2,1,0:T(8,128)(2,1)} %get-tuple-element.34), calls=%async_computation | async-start | bytes 589824 | tf_op jit(solution)/shard_map/all_to_all | solution.py:502
  33.3 33.3 %collective-permute-start = (bf16[1024,256]{1,0:T(8,128)(2,1)}, bf16[1024,256]{1,0:T(8,128)(2,1)}, u32[]{:S(2)}, u32[]{:S(2)}) collective-permute-start(bf16[1024,256]{1,0:T(8,128)(2,1)} %get-tuple-element.32), channel_id=1, source_target_pairs={{0,4},{4,8},{8,12},{12,16},{16,20},{20,24},{24,28},{28,32},{32,36}... | collective-permute-start | bytes 1572872 | tf_op jit(solution)/shard_map/ppermute | solution.py:503
  37.2 29.4 %collective-permute-start.1 = (bf16[1024,256]{1,0:T(8,128)(2,1)}, bf16[1024,256]{1,0:T(8,128)(2,1)}, u32[]{:S(2)}, u32[]{:S(2)}) collective-permute-start(bf16[1024,256]{1,0:T(8,128)(2,1)} %get-tuple-element.33), channel_id=1, source_target_pairs={{0,4},{4,8},{8,12},{12,16},{16,20},{20,24},{24,28},{28,32},{32,36}... | collective-permute-start | bytes 1572872 | tf_op jit(solution)/shard_map/ppermute | solution.py:504
  48.9 15.7 %collective-permute-start.5 = (bf16[144,128]{1,0:T(8,128)(2,1)S(1)}, bf16[144,128]{1,0:T(8,128)(2,1)S(1)}, u32[]{:S(2)}, u32[]{:S(2)}) collective-permute-start(bf16[144,128]{1,0:T(8,128)(2,1)S(1)} %get-tuple-element.46), channel_id=1, source_target_pairs={{0,64},{4,68},{8,72},{12,76},{16,80},{20,84},{24,88},{28,92},{32,9... | collective-permute-start | bytes 110600 | tf_op jit(solution)/shard_map/ppermute | solution.py:513
  52.9 2.1 %copy-start = (bf16[1024,256]{1,0:T(8,128)(2,1)}, bf16[1024,256]{1,0:T(8,128)(2,1)S(1)}, u32[]{:S(2)}) copy-start(bf16[1024,256]{1,0:T(8,128)(2,1)S(1)} %collective-permute-done.3.vp_ref) | copy-start | bytes 1572868
  53.0 13.7 %collective-permute-start.4 = (bf16[144,128]{1,0:T(8,128)(2,1)S(1)}, bf16[144,128]{1,0:T(8,128)(2,1)S(1)}, u32[]{:S(2)}, u32[]{:S(2)}) collective-permute-start(bf16[144,128]{1,0:T(8,128)(2,1)S(1)} %get-tuple-element.46), channel_id=1, source_target_pairs={{0,32},{4,36},{8,40},{12,44},{16,48},{20,52},{24,56},{28,60},{32,6... | collective-permute-start | bytes 110600 | tf_op jit(solution)/shard_map/ppermute | solution.py:513
  55.1 0.8 copy-start.1
  89.0 6.8 %collective-permute-start.8 = (f32[64,128]{1,0:T(8,128)S(1)}, f32[64,128]{1,0:T(8,128)S(1)}, u32[]{:S(2)}, u32[]{:S(2)}) collective-permute-start(f32[64,128]{1,0:T(8,128)S(1)} %get-tuple-element.52), channel_id=1, source_target_pairs={{0,96},{4,100},{8,104},{12,108},{16,112},{20,116},{24,120},{28,124... | collective-permute-start | bytes 98312 | tf_op jit(solution)/shard_map/ppermute | solution.py:513
  89.7 6.1 %collective-permute-start.7 = (f32[64,128]{1,0:T(8,128)S(1)}, f32[64,128]{1,0:T(8,128)S(1)}, u32[]{:S(2)}, u32[]{:S(2)}) collective-permute-start(f32[64,128]{1,0:T(8,128)S(1)} %get-tuple-element.52), channel_id=1, source_target_pairs={{0,64},{4,68},{8,72},{12,76},{16,80},{20,84},{24,88},{28,92},{32,9... | collective-permute-start | bytes 98312 | tf_op jit(solution)/shard_map/ppermute | solution.py:513
  93.9 5.8 %collective-permute-start.6 = (f32[64,128]{1,0:T(8,128)S(1)}, f32[64,128]{1,0:T(8,128)S(1)}, u32[]{:S(2)}, u32[]{:S(2)}) collective-permute-start(f32[64,128]{1,0:T(8,128)S(1)} %get-tuple-element.52), channel_id=1, source_target_pairs={{0,32},{4,36},{8,40},{12,44},{16,48},{20,52},{24,56},{28,60},{32,6... | collective-permute-start | bytes 98312 | tf_op jit(solution)/shard_map/ppermute | solution.py:513

commit v4 on v3

--- a/solution.py
+++ b/solution.py
@@ -346,23 +346,23 @@
     b_ref[0] = jnp.transpose(x).astype(BF16)
 
 
-def attend(base, first, att_query, k_prev, k_own, v_prev, own, m, ke, qe, e, g, *earlier):
+def attend(base, first, att_query, kv_prev, k_own, own, m, ke, qe, e, g, *earlier):
     rows, width = att_query.shape
     heads = width // DH
-    window, held = k_prev.shape
+    window, held = kv_prev.shape
+    held = held // (2 * DH)
     chunks = rows // CHUNK
     big = pl.BlockSpec((chunks, 1, CHUNK, DH), lambda h: (0, h + base, 0, 0))
     tok = pl.BlockSpec((rows, DH), lambda h: (0, h + base))
-    prev = pl.BlockSpec((window, DH), lambda h: (0, h))
     return pl.pallas_call(
         functools.partial(attend_kernel, base),
-        grid=(held // DH,),
+        grid=(held,),
         in_specs=[
             pl.BlockSpec(memory_space=pltpu.SMEM),
             tok,
-            prev,
+            pl.BlockSpec((window, DH), lambda h: (0, h)),
             pl.BlockSpec((16, DH), lambda h: (0, h + base)),
-            prev,
+            pl.BlockSpec((window, DH), lambda h: (0, h + held)),
             pl.BlockSpec((rows, 2 * DH), lambda h: (0, h + base)),
             big,
             pl.BlockSpec((chunks, 1, CHUNK, 2 * DH), lambda h: (0, h + base, 0, 0)),
@@ -381,7 +381,7 @@
         compiler_params=pltpu.CompilerParams(vmem_limit_bytes=MIDDLE),
         cost_estimate=pl.CostEstimate(flops=100_000_000_000, bytes_accessed=1_000_000, transcendentals=0),
         name="window_attention",
-    )(first, att_query, k_prev, k_own, v_prev, own, m, ke, qe, e, g, *earlier)
+    )(first, att_query, kv_prev, k_own, kv_prev, own, m, ke, qe, e, g, *earlier)
 
 
 def vmem_call(kernel, outs, name, *args):
@@ -415,31 +415,35 @@
     t_ref[DH:] = pack_gain(g)
 
 
-def line_kernel(d_ref, b_ref, q_ref, t_ref):
+def line_kernel(d_ref, t_ref, b_ref, q_ref, w_ref):
     acc = b_ref[0].astype(F32)
     q_ref[0] = jnp.zeros_like(acc)
     for z in range(1, d_ref.shape[0]):
         q_ref[z] = acc
         g = unpack_gain(d_ref[z, DH:])
         acc = g * acc + b_ref[z].astype(F32) + dot(acc.astype(BF16), d_ref[z, :DH])
-    t_ref[...] = acc
+    size = acc.shape[0]
+    w_ref[: 2 * size] = below(*halves(acc))
+    w_ref[2 * size :] = t_ref[...]
 
 
 def place_kernel(majors, *refs):
-    sums, fades = refs[: majors - 1], refs[majors - 1 : 2 * majors - 3]
-    p_ref, q_ref, s_ref = refs[2 * majors - 3 :]
-    base = sums[0][...]
-    g = jnp.ones((1, DH), F32)
-    f = jnp.zeros((DH, DH), F32)
+    wires = refs[: majors - 1]
+    p_ref, q_ref, s_ref = refs[majors - 1 :]
+    size = q_ref.shape[1]
+
+    def added(wire):
+        return wire[:size].astype(F32) + wire[size : 2 * size].astype(F32)
+
+    base = added(wires[0])
     for k in range(1, majors - 1):
-        d = fades[k - 1]
-        step = unpack_gain(d[DH:])
+        old = wires[k - 1][2 * size : 2 * size + DH]
+        step = unpack_gain(wires[k - 1][2 * size + DH :])
         if k == 1:
-            g, f = step, d[:DH].astype(F32)
+            g, f = step, old.astype(F32)
         else:
-            old = d[:DH]
             f, g = step * f + g * old.astype(F32) + dot(old, f.astype(BF16)), g * step
-        value = sums[k][...]
+        value = added(wires[k])
         base = base + g * value + dot(value.astype(BF16), f.astype(BF16))
     high = base.astype(BF16)
     for z in range(p_ref.shape[0]):
@@ -492,41 +496,42 @@
     majors = count // minor
     place = lax.axis_index("seq")
     onward = [(s, s + 1) for s in range(count - 1)]
-    half = heads // 2 * DH
-    k_first = lax.ppermute(att_key[:, :half], "seq", onward)
-    v_first = lax.ppermute(att_value[:, :half], "seq", onward)
     copies = minor // heads
+    last = heads - 1
+
+    def both(begin, end):
+        part = slice(begin * DH, end * DH)
+        return beside(att_key[:, part], att_value[:, part])
+
+    kv_first = lax.ppermute(both(0, last), "seq", onward)
     m, ke, qe, qf, e, g, wire = prep(log_decay, beta, delta_key, delta_query, copies)
-    wire, k_rest, v_rest = lax.optimization_barrier((wire, att_key[:, half:], att_value[:, half:]))
+    wire, kv_last = lax.optimization_barrier((wire, both(last, heads)))
+    kv_last = lax.ppermute(kv_last, "seq", onward)
     lines = [[x * minor + z for z in range(minor)] for x in range(majors)]
     d_line = lax.all_to_all(wire, "seq", 0, 0, axis_index_groups=lines)
-    k_rest = lax.ppermute(k_rest, "seq", onward)
-    v_rest = lax.ppermute(v_rest, "seq", onward)
     own = own_part(att_query, att_key, att_value)
-    d_line, own = lax.optimization_barrier((d_line, own))
+    first = jnp.reshape((place == 0).astype(jnp.int32), (1,))
+    coefs = (own, m, ke, qe, e, g)
+    early = attend(0, first, att_query, kv_first, att_key, *coefs)
+    d_line, early = lax.optimization_barrier((d_line, early))
     p_line, d_total = vmem_call(
         prefix_kernel, [(d_line.shape, BF16), (d_line.shape[1:], BF16)], "decay_prefix", d_line
     )
+    early, p_line, d_total = lax.optimization_barrier((early, p_line, d_total))
+    readout, b = attend(last, first, att_query, kv_last, att_key, *coefs, *early)
+    size = DH // copies
+    b_line = lax.all_to_all(b.reshape(minor, size, DH), "seq", 0, 0, axis_index_groups=lines)
+    q_line, added = vmem_call(
+        line_kernel, [(b_line.shape, F32), ((2 * size + WIRE, DH), BF16)], "line_states", d_line, d_total, b_line
+    )
 
     def from_lines(value, back):
         hops = back * minor
         return lax.ppermute(value, "seq", [(s, s + hops) for s in range(count - hops)])
 
-    fades = [from_lines(d_total, k) for k in range(1, majors - 1)]
-    own, p_line = lax.optimization_barrier((own, p_line))
-    first = jnp.reshape((place == 0).astype(jnp.int32), (1,))
-    coefs = (own, m, ke, qe, e, g)
-    early = attend(0, first, att_query, k_first, att_key, v_first, *coefs)
-    early, fades = lax.optimization_barrier((early, fades))
-    readout, b = attend(half // DH, first, att_query, k_rest, att_key, v_rest, *coefs, *early)
-    size = DH // copies
-    b_line = lax.all_to_all(b.reshape(minor, size, DH), "seq", 0, 0, axis_index_groups=lines)
-    q_line, b_total = vmem_call(
-        line_kernel, [(b_line.shape, F32), ((size, DH), F32)], "line_states", d_line, b_line
-    )
-    sums = [from_lines(b_total, k) for k in range(1, majors)]
+    wires = [from_lines(added, k) for k in range(1, majors)]
     (s_line,) = vmem_call(
-        functools.partial(place_kernel, majors), [(b_line.shape, BF16)], "block_states", *sums, *fades, p_line, q_line
+        functools.partial(place_kernel, majors), [(b_line.shape, BF16)], "block_states", *wires, p_line, q_line
     )
     state = lax.all_to_all(s_line, "seq", 0, 0, axis_index_groups=lines).reshape(heads, DH, DH)
     return finish(readout, qf, state, out_gate, norm_gain.reshape(1, DH))

time: 118 us -> 116 us (0.983)
  starting transfers between devices: 34.5 us -> 22.6 us
  waiting for transfers between devices: 5.84 us -> 10.7 us
  blocking collectives: 24.9 us -> 27.8 us
  other arithmetic: 0 us -> 2.21 us
  Pallas kernels: 48.1 us -> 50.2 us
  local copies, waits for them, and re-layouts: 3.46 us -> 1.38 us
    ppermute x4 -> x2, starting transfers between devices: 14.9 us -> 7.73 us  [the longest x1 3.92 us: body(): kv_last = lax.ppermute(kv_last, 'seq', onward)]
    ppermute x4 -> x2, waiting for transfers between devices: 0.01 us -> 6.41 us  [the longest x1 4.33 us: body(): kv_first = lax.ppermute(both(0, last), 'seq', onward)]
    ppermute x5 -> x3, starting transfers between devices: 12.9 us -> 7.24 us  [from_lines(): lax.ppermute(value, 'seq', [(s, s + hops) for s in range(count - hops)])]
    all_to_all x1, blocking collectives: 12.8 us -> 15.6 us  [body(): lax.all_to_all(b.reshape(minor, size, DH), 'seq', 0, 0, axis_index_groups...]
    concatenate x0 -> x2, other arithmetic: none -> 2.21 us  [beside(): return jnp.concatenate(parts, axis=1)]
    pallas_call x3, Pallas kernels: 2.28 us -> 4.22 us  [vmem_call(): pl.pallas_call(kernel, in_specs=[vm] * len(args), out_specs=[vm] * len(ou...]
    ppermute x5 -> x3, waiting for transfers between devices: 5.83 us -> 4.26 us  [from_lines(): lax.ppermute(value, 'seq', [(s, s + hops) for s in range(count - hops)])]
    slice x1 -> x8, local copies, waits for them, and re-layouts: 2.68 us -> 1.38 us  [both(): return beside(att_key[:, part], att_value[:, part])]
  transfers between devices with their start and end apart: 10 -> 6, of which waited for: 2 -> 3; matrix products, arithmetic and copies ran while one was open for 0% -> 1% of each run, Pallas kernels for 28% -> 32%
where the time goes in v4:
time: 116 us; the launch traced here: 115 us
  Pallas kernels  50.2 us (43%)
  blocking collectives  27.8 us (24%)
  starting transfers between devices  22.6 us (19%)
  waiting for transfers between devices  10.7 us (9%)
  other arithmetic  2.21 us (2%)
  local copies, waits for them, and re-layouts  1.38 us (1%)
    pallas_call x2, Pallas kernels, attend(): pl.pallas_call(functools.partial(attend_kernel, base), grid=(held,), in_s...  17.8 us
    pallas_call x1, Pallas kernels, prep(): pl.pallas_call(functools.partial(prep_kernel, heads, PER), grid=(chunks /...  16.2 us
    all_to_all x1, blocking collectives, body(): lax.all_to_all(b.reshape(minor, size, DH), 'seq', 0, 0, axis_index_groups...  15.6 us
    all_to_all x1, blocking collectives, body(): lax.all_to_all(s_line, 'seq', 0, 0, axis_index_groups=lines)  12.1 us
    all_to_all x1, starting transfers between devices, body(): d_line = lax.all_to_all(wire, 'seq', 0, 0, axis_index_groups=lines)  7.58 us
    pallas_call x1, Pallas kernels, own_part(): pl.pallas_call(own_kernel, grid=(heads,), in_specs=[tok, tok, tok], out_s...  7.32 us
    ppermute x3, starting transfers between devices, from_lines(): lax.ppermute(value, 'seq', [(s, s + hops) for s in range(count - hops)])  7.24 us
    pallas_call x1, Pallas kernels, finish(): pl.pallas_call(functools.partial(finish_kernel, heads), grid=(rows // (PE...  4.74 us
  transfers between devices with their start and end apart: 6, of which 3 were waited for; matrix products, arithmetic and copies ran while one was open for 1% of the time, Pallas kernels for 32%

profile of v4, /device:TPU:18, one launch (start us, length us, event | category | flops | bytes accessed | tf_op | source)
XLA Modules:
  0.0 114.9 jit_solution(7714715536040017441)
XLA Ops:
  0.0 0.0 slice-start
  0.0 0.0 slice-start.2
  0.0 1.1 slice-done
  1.1 0.2 slice-done.2
  1.4 0.0 slice-start.1
  1.4 0.0 slice-start.3
  1.4 1.3 %pad_maximum_fusion = bf16[1024,768]{1,0:T(8,128)(2,1)} fusion(bf16[1024,384]{1,0:T(8,128)(2,1)S(1)} %slice-done, bf16[1024,384]{1,0:T(8,128)(2,1)S(1)} %slice-done.2), kind=kLoop, calls=%fused_computation | loop fusion | flops 3145728 | bytes 3145728 | tf_op jit(solution)/shard_map/concatenate | solution.py:39
  2.7 3.8 %collective-permute-start.1 = (bf16[1024,768]{1,0:T(8,128)(2,1)}, bf16[1024,768]{1,0:T(8,128)(2,1)}, u32[]{:S(2)}, u32[]{:S(2)}) collective-permute-start(bf16[1024,768]{1,0:T(8,128)(2,1)} %pad_maximum_fusion), channel_id=1, source_target_pairs={{0,4},{4,8},{8,12},{12,16},{16,20},{20,24},{24,28},{28,32},{32,36}... | collective-permute-start | bytes 4718600 | tf_op jit(solution)/shard_map/ppermute | solution.py:506
  6.5 0.0 slice-done.1
  6.6 0.0 slice-done.3
  6.6 0.9 pad_maximum_fusion.1
  7.4 16.2 %delta_prep.1 = (bf16[8,4,128,128]{3,2,1,0:T(8,128)(2,1)}, bf16[8,4,128,256]{3,2,1,0:T(8,128)(2,1)}, bf16[8,4,128,128]{3,2,1,0:T(8,128)(2,1)}, bf16[8,4,128,256]...) custom-call(f32[4,1024]{1,0:T(4,128)} %ld_ref.1, ...), custom_call_target="tpu_custom_call" | custom-call | flops 1000000 | bytes 1000000 | tf_op jit(solution)/shard_map/delta_prep/pallas_call | solution.py:226
  23.6 7.6 %all-to-all-start = ((bf16[8,144,128]{2,1,0:T(8,128)(2,1)}), bf16[8,144,128]{2,1,0:T(8,128)(2,1)}, u32[]{:S(2)}, u32[]{:S(2)}) async-start(bf16[8,144,128]{2,1,0:T(8,128)(2,1)} %get-tuple-element.36), calls=%async_computation | async-start | bytes 589824 | tf_op jit(solution)/shard_map/all_to_all | solution.py:511
  31.2 3.9 %collective-permute-start = (bf16[1024,256]{1,0:T(8,128)(2,1)}, bf16[1024,256]{1,0:T(8,128)(2,1)}, u32[]{:S(2)}, u32[]{:S(2)}) collective-permute-start(bf16[1024,256]{1,0:T(8,128)(2,1)} %pad_maximum_fusion.1), channel_id=1, source_target_pairs={{0,4},{4,8},{8,12},{12,16},{16,20},{20,24},{24,28},{28,32},{32,36}... | collective-permute-start | bytes 1572872 | tf_op jit(solution)/shard_map/ppermute | solution.py:509
  35.2 7.3 %own_attention.1.own_ref = f32[1024,1024]{1,0:T(8,128)} custom-call(bf16[1024,512]{1,0:T(8,128)(2,1)} %q_ref.7, bf16[1024,512]{1,0:T(8,128)(2,1)} %ko_ref.3, bf16[1024,512]{1,0:T(8,128)(2,1)} %v_ref.1), custom_call_target="tpu_custom_call" | custom-call | flops 99999997952 | bytes 1000000 | tf_op jit(solution)/shard_map/own_attention/pallas_call | solution.py:275
  42.5 4.3 %collective-permute-done.1.kp_ref.vp_ref = bf16[1024,768]{1,0:T(8,128)(2,1)} collective-permute-done((bf16[1024,768]{1,0:T(8,128)(2,1)}, bf16[1024,768]{1,0:T(8,128)(2,1)}, u32[]{:S(2)}, u32[]{:S(2)}) %collective-permute-start.1) | collective-permute-done | bytes 1572896 | tf_op jit(solution)/shard_map/ppermute | solution.py:506
  46.8 11.9 %window_attention.2 = (f32[1024,512]{1,0:T(8,128)}, bf16[4,128,128]{2,1,0:T(8,128)(2,1)}) custom-call(s32[1]{0:T(128)} %bitcast.first_ref, bf16[1024,512]{1,0:T(8,128)(2,1)} %q_ref.7, bf16[1024,768]{1,0:T(8,128)(2,1)} %collective-permute-done.1.kp_ref.vp_ref, bf16[1024,512]{1,0:T(8,128)(2,1)} %ko_ref.3, ...), custom_call_target="tpu_custom_call" | custom-call | flops 99999997952 | bytes 1000000 | tf_op jit(solution)/shard_map/window_attention/pallas_call | solution.py:357
  58.7 0.0 all-to-all-done.d_ref
  58.7 1.9 %decay_prefix.1 = (bf16[8,144,128]{2,1,0:T(8,128)(2,1)S(1)}, bf16[144,128]{1,0:T(8,128)(2,1)S(1)}) custom-call(bf16[8,144,128]{2,1,0:T(8,128)(2,1)} %all-to-all-done.d_ref), custom_call_target="tpu_custom_call" | custom-call | flops 1000000 | bytes 1000000 | tf_op jit(solution)/shard_map/decay_prefix/pallas_call | solution.py:389
  60.6 2.1 %collective-permute-done.kp_ref.vp_ref = bf16[1024,256]{1,0:T(8,128)(2,1)} collective-permute-done((bf16[1024,256]{1,0:T(8,128)(2,1)}, bf16[1024,256]{1,0:T(8,128)(2,1)}, u32[]{:S(2)}, u32[]{:S(2)}) %collective-permute-start) | collective-permute-done | bytes 524320 | tf_op jit(solution)/shard_map/ppermute | solution.py:509
  62.7 5.9 %window_attention.3 = (f32[1024,512]{1,0:T(8,128)}, bf16[4,128,128]{2,1,0:T(8,128)(2,1)}) custom-call(s32[1]{0:T(128)} %bitcast.first_ref, bf16[1024,512]{1,0:T(8,128)(2,1)} %q_ref.7, bf16[1024,256]{1,0:T(8,128)(2,1)} %collective-permute-done.kp_ref.vp_ref, bf16[1024,512]{1,0:T(8,128)(2,1)} %ko_ref.3, ...), custom_call_target="tpu_custom_call", output_to_operand_aliasing={{0}: (11, {}), {1}: (12, {})} | custom-call | flops 99999997952 | bytes 1000000 | tf_op jit(solution)/shard_map/window_attention/pallas_call | solution.py:357
  68.6 15.6 %all_to_all.15.b_ref = bf16[8,64,128]{2,1,0:T(8,128)(2,1)S(1)} all-to-all(bf16[8,64,128]{2,1,0:T(8,128)(2,1)} %bitcast.5), channel_id=1, replica_groups={{0,4,8,12,16,20,24,28},{32,36,40,44,48,52,56,60},{64,68,72,76,80,84,88,..., dimensions={0} | all-to-all | bytes 262144 | tf_op jit(solution)/shard_map/all_to_all | solution.py:523
  84.2 1.8 %line_states.1 = (f32[8,64,128]{2,1,0:T(8,128)S(1)}, bf16[272,128]{1,0:T(8,128)(2,1)S(1)}) custom-call(bf16[8,144,128]{2,1,0:T(8,128)(2,1)} %all-to-all-done.d_ref, bf16[144,128]{1,0:T(8,128)(2,1)S(1)} %get-tuple-element.48.t_ref, bf16[8,64,128]{2,1,0:T(8,128)(2,1)S(1)} %all_to_all.15.b_ref), custom_call_target="tpu_custom_call" | custom-call | flops 1000000 | bytes 1000000 | tf_op jit(solution)/shard_map/line_states/pallas_call | solution.py:389
  86.1 0.7 collective-permute-start.4
  86.7 4.7 %collective-permute-start.3 = (bf16[272,128]{1,0:T(8,128)(2,1)S(1)}, bf16[272,128]{1,0:T(8,128)(2,1)S(1)}, u32[]{:S(2)}, u32[]{:S(2)}) collective-permute-start(bf16[272,128]{1,0:T(8,128)(2,1)S(1)} %get-tuple-element.50), channel_id=1, source_target_pairs={{0,64},{4,68},{8,72},{12,76},{16,80},{20,84},{24,88},{28,92},{32,9... | collective-permute-start | bytes 208904 | tf_op jit(solution)/shard_map/ppermute | solution.py:530
  91.4 1.9 %collective-permute-start.2 = (bf16[272,128]{1,0:T(8,128)(2,1)S(1)}, bf16[272,128]{1,0:T(8,128)(2,1)S(1)}, u32[]{:S(2)}, u32[]{:S(2)}) collective-permute-start(bf16[272,128]{1,0:T(8,128)(2,1)S(1)} %get-tuple-element.50), channel_id=1, source_target_pairs={{0,32},{4,36},{8,40},{12,44},{16,48},{20,52},{24,56},{28,60},{32,6... | collective-permute-start | bytes 208904 | tf_op jit(solution)/shard_map/ppermute | solution.py:530
  93.3 0.0 collective-permute-done.4.refs_2_
  93.3 0.0 collective-permute-done.3.refs_1_
  93.3 4.3 %collective-permute-done.2.refs_0_ = bf16[272,128]{1,0:T(8,128)(2,1)S(1)} collective-permute-done((bf16[272,128]{1,0:T(8,128)(2,1)S(1)}, bf16[272,128]{1,0:T(8,128)(2,1)S(1)}, u32[]{:S(2)}, u32[]{:S(2)}) %collective-permute-start.2) | collective-permute-done | bytes 69664 | tf_op jit(solution)/shard_map/ppermute | solution.py:530
  97.6 0.5 block_states.1
  98.1 12.1 %all_to_all.16 = bf16[8,64,128]{2,1,0:T(8,128)(2,1)} all-to-all(bf16[8,64,128]{2,1,0:T(8,128)(2,1)S(1)} %block_states.1), channel_id=1, replica_groups={{0,4,8,12,16,20,24,28},{32,36,40,44,48,52,56,60},{64,68,72,76,80,84,88,..., dimensions={0} | all-to-all | bytes 262144 | tf_op jit(solution)/shard_map/all_to_all | solution.py:536
  110.2 4.7 %gated_readout.1 = bf16[1024,512]{1,0:T(8,128)(2,1)} custom-call(f32[1024,512]{1,0:T(8,128)} %get-tuple-element.46.r_ref, bf16[8,4,128,256]{3,2,1,0:T(8,128)(2,1)} %get-tuple-element.47.qf_ref, bf16[4,128,128]{2,1,0:T(8,128)(2,1)} %bitcast.4, bf16[1024,512]{1,0:T(8,128)(2,1)} %gate_ref.1, f32[1,128]{1,0:T(1,128)} %bitcast.6), custom_call_target="tpu_custom_call" | custom-call | flops 140000000 | bytes 6000000 | tf_op jit(solution)/shard_map/gated_readout/pallas_call | solution.py:474
Async XLA Ops:
  0.0 1.1 slice-start
  0.0 1.4 %slice-start.2 = ((bf16[1024,512]{1,0:T(8,128)(2,1)}), bf16[1024,384]{1,0:T(8,128)(2,1)S(1)}, s32[]{:S(2)}) async-start(bf16[1024,512]{1,0:T(8,128)(2,1)} %ko_ref.3), calls=%async_computation.5 | async-start | bytes 1572864 | tf_op jit(solution)/shard_map/slice | solution.py:504
  1.4 5.2 %slice-start.1 = ((bf16[1024,512]{1,0:T(8,128)(2,1)}), bf16[1024,128]{1,0:T(8,128)(2,1)S(1)}, s32[]{:S(2)}) async-start(bf16[1024,512]{1,0:T(8,128)(2,1)} %v_ref.1), calls=%async_computation.4 | async-start | bytes 524288 | tf_op jit(solution)/shard_map/slice | solution.py:504
  1.4 5.2 %slice-start.3 = ((bf16[1024,512]{1,0:T(8,128)(2,1)}), bf16[1024,128]{1,0:T(8,128)(2,1)S(1)}, s32[]{:S(2)}) async-start(bf16[1024,512]{1,0:T(8,128)(2,1)} %ko_ref.3), calls=%async_computation.6 | async-start | bytes 524288 | tf_op jit(solution)/shard_map/slice | solution.py:504
  2.7 44.1 %collective-permute-start.1 = (bf16[1024,768]{1,0:T(8,128)(2,1)}, bf16[1024,768]{1,0:T(8,128)(2,1)}, u32[]{:S(2)}, u32[]{:S(2)}) collective-permute-start(bf16[1024,768]{1,0:T(8,128)(2,1)} %pad_maximum_fusion), channel_id=1, source_target_pairs={{0,4},{4,8},{8,12},{12,16},{16,20},{20,24},{24,28},{28,32},{32,36}... | collective-permute-start | bytes 4718600 | tf_op jit(solution)/shard_map/ppermute | solution.py:506
  23.6 35.0 %all-to-all-start = ((bf16[8,144,128]{2,1,0:T(8,128)(2,1)}), bf16[8,144,128]{2,1,0:T(8,128)(2,1)}, u32[]{:S(2)}, u32[]{:S(2)}) async-start(bf16[8,144,128]{2,1,0:T(8,128)(2,1)} %get-tuple-element.36), calls=%async_computation | async-start | bytes 589824 | tf_op jit(solution)/shard_map/all_to_all | solution.py:511
  31.2 31.5 %collective-permute-start = (bf16[1024,256]{1,0:T(8,128)(2,1)}, bf16[1024,256]{1,0:T(8,128)(2,1)}, u32[]{:S(2)}, u32[]{:S(2)}) collective-permute-start(bf16[1024,256]{1,0:T(8,128)(2,1)} %pad_maximum_fusion.1), channel_id=1, source_target_pairs={{0,4},{4,8},{8,12},{12,16},{16,20},{20,24},{24,28},{28,32},{32,36}... | collective-permute-start | bytes 1572872 | tf_op jit(solution)/shard_map/ppermute | solution.py:509
  86.1 7.3 %collective-permute-start.4 = (bf16[272,128]{1,0:T(8,128)(2,1)S(1)}, bf16[272,128]{1,0:T(8,128)(2,1)S(1)}, u32[]{:S(2)}, u32[]{:S(2)}) collective-permute-start(bf16[272,128]{1,0:T(8,128)(2,1)S(1)} %get-tuple-element.50), channel_id=1, source_target_pairs={{0,96},{4,100},{8,104},{12,108},{16,112},{20,116},{24,120},{28,124... | collective-permute-start | bytes 208904 | tf_op jit(solution)/shard_map/ppermute | solution.py:530
  86.7 6.6 %collective-permute-start.3 = (bf16[272,128]{1,0:T(8,128)(2,1)S(1)}, bf16[272,128]{1,0:T(8,128)(2,1)S(1)}, u32[]{:S(2)}, u32[]{:S(2)}) collective-permute-start(bf16[272,128]{1,0:T(8,128)(2,1)S(1)} %get-tuple-element.50), channel_id=1, source_target_pairs={{0,64},{4,68},{8,72},{12,76},{16,80},{20,84},{24,88},{28,92},{32,9... | collective-permute-start | bytes 208904 | tf_op jit(solution)/shard_map/ppermute | solution.py:530
  91.4 6.2 %collective-permute-start.2 = (bf16[272,128]{1,0:T(8,128)(2,1)S(1)}, bf16[272,128]{1,0:T(8,128)(2,1)S(1)}, u32[]{:S(2)}, u32[]{:S(2)}) collective-permute-start(bf16[272,128]{1,0:T(8,128)(2,1)S(1)} %get-tuple-element.50), channel_id=1, source_target_pairs={{0,32},{4,36},{8,40},{12,44},{16,48},{20,52},{24,56},{28,60},{32,6... | collective-permute-start | bytes 208904 | tf_op jit(solution)/shard_map/ppermute | solution.py:530

commit v5 on v4

--- a/solution.py
+++ b/solution.py
@@ -45,6 +45,16 @@
 
 def diagonal(one, two):
     return below(beside(one, jnp.zeros_like(two)), beside(jnp.zeros_like(one), two))
+
+
+def mean_squares(tiles):
+    mean = jnp.full((DH, DH), 1.0 / DH, BF16)
+    means = diagonal(mean, mean)
+    out = []
+    for one, two in zip(tiles[::2], tiles[1::2]):
+        both = dot(beside((one * one).astype(BF16), (two * two).astype(BF16)), means)
+        out += [both[:, :DH], both[:, DH:]]
+    return out
 
 
 def odd_rows(value, size):
@@ -306,7 +316,6 @@
 
     ri = lax.broadcasted_iota(jnp.int32, (QB, QB), 0)
     rj = lax.broadcasted_iota(jnp.int32, (QB, QB), 1)
-    mean = jnp.full((DH, DH), 1.0 / DH, BF16)
     blocks = [slice(i * QB, (i + 1) * QB) for i in range(q_ref.shape[0] // QB)]
     scores = []
     for i, here in enumerate(blocks):
@@ -323,7 +332,7 @@
     for here, (pv, fade) in zip(blocks, sums):
         total = pv[:, DH:] + fade * own_ref[here, DH : DH + 1]
         outs.append(((pv[:, :DH] + fade * own_ref[here, :DH]) / total).astype(BF16).astype(F32))
-    squares = [dot(beside(*halves(o * o)), below(mean, mean)) for o in outs]
+    squares = mean_squares(outs)
     values = [halves(o * lax.rsqrt(square + 1e-6)) for o, square in zip(outs, squares)]
     per = QB // CHUNK
     chunks = []
@@ -423,28 +432,20 @@
         g = unpack_gain(d_ref[z, DH:])
         acc = g * acc + b_ref[z].astype(F32) + dot(acc.astype(BF16), d_ref[z, :DH])
     size = acc.shape[0]
-    w_ref[: 2 * size] = below(*halves(acc))
-    w_ref[2 * size :] = t_ref[...]
-
-
-def place_kernel(majors, *refs):
-    wires = refs[: majors - 1]
-    p_ref, q_ref, s_ref = refs[majors - 1 :]
+    wire = below(*halves(acc), t_ref[...])
+    for x in range(w_ref.shape[0]):
+        w_ref[x] = wire
+
+
+def place_kernel(w_ref, earlier_ref, p_ref, q_ref, s_ref):
     size = q_ref.shape[1]
-
-    def added(wire):
-        return wire[:size].astype(F32) + wire[size : 2 * size].astype(F32)
-
-    base = added(wires[0])
-    for k in range(1, majors - 1):
-        old = wires[k - 1][2 * size : 2 * size + DH]
-        step = unpack_gain(wires[k - 1][2 * size + DH :])
-        if k == 1:
-            g, f = step, old.astype(F32)
-        else:
-            f, g = step * f + g * old.astype(F32) + dot(old, f.astype(BF16)), g * step
-        value = added(wires[k])
-        base = base + g * value + dot(value.astype(BF16), f.astype(BF16))
+    base = jnp.zeros((size, DH), F32)
+    for x in range(w_ref.shape[0] - 1):
+        added = w_ref[x, :size].astype(F32) + w_ref[x, size : 2 * size].astype(F32)
+        if x:
+            step = unpack_gain(w_ref[x, 2 * size + DH :])
+            added = added + step * base + dot(base.astype(BF16), w_ref[x, 2 * size : 2 * size + DH])
+        base = jnp.where(earlier_ref[x : x + 1] > 0.0, added, base)
     high = base.astype(BF16)
     for z in range(p_ref.shape[0]):
         out = unpack_gain(p_ref[z, DH:]) * base + q_ref[z] + dot(high, p_ref[z, :DH])
@@ -453,14 +454,13 @@
 
 def finish_kernel(heads, r_ref, qf_ref, s_ref, gate_ref, gain_ref, o_ref):
     gain = gain_ref[...]
-    mean = jnp.full((DH, DH), 1.0 / DH, BF16)
     tiles = [
         (slice(c * CHUNK, (c + 1) * CHUNK), slice(h * DH, (h + 1) * DH), c, h)
         for c in range(qf_ref.shape[0])
         for h in range(heads)
     ]
     reads = [r_ref[rows, cols] + dot(qf_ref[c, h], beside(s_ref[h], s_ref[h]), NT) for rows, cols, c, h in tiles]
-    squares = [dot(beside(*halves(r * r)), below(mean, mean)) for r in reads]
+    squares = mean_squares(reads)
     for (rows, cols, c, h), r, square in zip(tiles, reads, squares):
         gate = gate_ref[rows, cols].astype(F32)
         r = r * lax.rsqrt(square + 1e-6) * gain
@@ -499,13 +499,16 @@
     copies = minor // heads
     last = heads - 1
 
+
     def both(begin, end):
         part = slice(begin * DH, end * DH)
         return beside(att_key[:, part], att_value[:, part])
 
     kv_first = lax.ppermute(both(0, last), "seq", onward)
     m, ke, qe, qf, e, g, wire = prep(log_decay, beta, delta_key, delta_query, copies)
-    wire, kv_last = lax.optimization_barrier((wire, both(last, heads)))
+    earlier = (jnp.arange(majors) < place // minor).astype(F32)
+    earlier = jnp.broadcast_to(earlier[:, None], (majors, DH))
+    wire, kv_last, earlier = lax.optimization_barrier((wire, both(last, heads), earlier))
     kv_last = lax.ppermute(kv_last, "seq", onward)
     lines = [[x * minor + z for z in range(minor)] for x in range(majors)]
     d_line = lax.all_to_all(wire, "seq", 0, 0, axis_index_groups=lines)
@@ -522,17 +525,12 @@
     size = DH // copies
     b_line = lax.all_to_all(b.reshape(minor, size, DH), "seq", 0, 0, axis_index_groups=lines)
     q_line, added = vmem_call(
-        line_kernel, [(b_line.shape, F32), ((2 * size + WIRE, DH), BF16)], "line_states", d_line, d_total, b_line
+        line_kernel, [(b_line.shape, F32), ((majors, 2 * size + WIRE, DH), BF16)], "line_states", d_line, d_total, b_line
     )
 
-    def from_lines(value, back):
-        hops = back * minor
-        return lax.ppermute(value, "seq", [(s, s + hops) for s in range(count - hops)])
-
-    wires = [from_lines(added, k) for k in range(1, majors)]
-    (s_line,) = vmem_call(
-        functools.partial(place_kernel, majors), [(b_line.shape, BF16)], "block_states", *wires, p_line, q_line
-    )
+    columns = [[x * minor + z for x in range(majors)] for z in range(minor)]
+    wires = lax.all_to_all(added, "seq", 0, 0, axis_index_groups=columns)
+    (s_line,) = vmem_call(place_kernel, [(b_line.shape, BF16)], "block_states", wires, earlier, p_line, q_line)
     state = lax.all_to_all(s_line, "seq", 0, 0, axis_index_groups=lines).reshape(heads, DH, DH)
     return finish(readout, qf, state, out_gate, norm_gain.reshape(1, DH))
 

time: 116 us -> 115 us (level)
  blocking collectives: 27.8 us -> 37.7 us
  starting transfers between devices: 22.6 us -> 15.3 us
  waiting for transfers between devices: 10.7 us -> 6.35 us
    all_to_all x0 -> x1, blocking collectives: none -> 9.94 us  [body(): wires = lax.all_to_all(added, 'seq', 0, 0, axis_index_groups=columns)]
    ppermute x3 -> x0, starting transfers between devices: 7.24 us -> none  [from_lines(): lax.ppermute(value, 'seq', [(s, s + hops) for s in range(count - hops)])]
    ppermute x3 -> x0, waiting for transfers between devices: 4.26 us -> none  [from_lines(): lax.ppermute(value, 'seq', [(s, s + hops) for s in range(count - hops)])]
  transfers between devices with their start and end apart: 6 -> 3, of which waited for: 3 -> 2; matrix products, arithmetic and copies ran while one was open for 1% -> 1% of each run, Pallas kernels for 32% -> 33%
where the time goes in v5:
time: 115 us; the launch traced here: 113 us
  Pallas kernels  50.2 us (44%)
  blocking collectives  37.7 us (33%)
  starting transfers between devices  15.3 us (13%)
  waiting for transfers between devices  6.35 us (6%)
  other arithmetic  2.18 us (2%)
  local copies, waits for them, and re-layouts  1.45 us (1%)
    pallas_call x2, Pallas kernels, attend(): pl.pallas_call(functools.partial(attend_kernel, base), grid=(held,), in_s...  17.8 us
    pallas_call x1, Pallas kernels, prep(): pl.pallas_call(functools.partial(prep_kernel, heads, PER), grid=(chunks /...  16.2 us
    all_to_all x1, blocking collectives, body(): lax.all_to_all(b.reshape(minor, size, DH), 'seq', 0, 0, axis_index_groups...  15.6 us
    all_to_all x1, blocking collectives, body(): lax.all_to_all(s_line, 'seq', 0, 0, axis_index_groups=lines)  12.1 us
    all_to_all x1, blocking collectives, body(): wires = lax.all_to_all(added, 'seq', 0, 0, axis_index_groups=columns)  9.94 us
    all_to_all x1, starting transfers between devices, body(): d_line = lax.all_to_all(wire, 'seq', 0, 0, axis_index_groups=lines)  7.56 us
    pallas_call x1, Pallas kernels, own_part(): pl.pallas_call(own_kernel, grid=(heads,), in_specs=[tok, tok, tok], out_s...  7.33 us
    pallas_call x1, Pallas kernels, finish(): pl.pallas_call(functools.partial(finish_kernel, heads), grid=(rows // (PE...  4.69 us
  transfers between devices with their start and end apart: 3, of which 2 were waited for; matrix products, arithmetic and copies ran while one was open for 1% of the time, Pallas kernels for 33%

profile of v5, /device:TPU:18, one launch (start us, length us, event | category | flops | bytes accessed | tf_op | source)
XLA Modules:
  0.0 113.2 jit_solution(5688186683154026854)
XLA Ops:
  0.0 0.0 slice-start
  0.0 0.0 slice-start.2
  0.0 1.1 slice-done
  1.1 0.2 slice-done.2
  1.4 0.0 slice-start.1
  1.4 0.0 slice-start.3
  1.4 1.3 %pad_maximum_fusion = bf16[1024,768]{1,0:T(8,128)(2,1)} fusion(bf16[1024,384]{1,0:T(8,128)(2,1)S(1)} %slice-done, bf16[1024,384]{1,0:T(8,128)(2,1)S(1)} %slice-done.2), kind=kLoop, calls=%fused_computation | loop fusion | flops 3145728 | bytes 3145728 | tf_op jit(solution)/shard_map/concatenate | solution.py:39
  2.7 3.8 %collective-permute-start.1 = (bf16[1024,768]{1,0:T(8,128)(2,1)}, bf16[1024,768]{1,0:T(8,128)(2,1)}, u32[]{:S(2)}, u32[]{:S(2)}) collective-permute-start(bf16[1024,768]{1,0:T(8,128)(2,1)} %pad_maximum_fusion), channel_id=1, source_target_pairs={{0,4},{4,8},{8,12},{12,16},{16,20},{20,24},{24,28},{28,32},{32,36}... | collective-permute-start | bytes 4718600 | tf_op jit(solution)/shard_map/ppermute | solution.py:507
  6.6 0.0 slice-done.1
  6.6 0.0 slice-done.3
  6.6 0.8 pad_maximum_fusion.1
  7.4 16.2 %delta_prep.1 = (bf16[8,4,128,128]{3,2,1,0:T(8,128)(2,1)}, bf16[8,4,128,256]{3,2,1,0:T(8,128)(2,1)}, bf16[8,4,128,128]{3,2,1,0:T(8,128)(2,1)}, bf16[8,4,128,256]...) custom-call(f32[4,1024]{1,0:T(4,128)} %ld_ref.1, ...), custom_call_target="tpu_custom_call" | custom-call | flops 1000000 | bytes 1000000 | tf_op jit(solution)/shard_map/delta_prep/pallas_call | solution.py:236
  23.6 0.1 broadcast_in_dim.2.earlier_ref
  23.7 7.6 %all-to-all-start = ((bf16[8,144,128]{2,1,0:T(8,128)(2,1)}), bf16[8,144,128]{2,1,0:T(8,128)(2,1)}, u32[]{:S(2)}, u32[]{:S(2)}) async-start(bf16[8,144,128]{2,1,0:T(8,128)(2,1)} %get-tuple-element.37), calls=%async_computation | async-start | bytes 589824 | tf_op jit(solution)/shard_map/all_to_all | solution.py:514
  31.3 3.9 %collective-permute-start = (bf16[1024,256]{1,0:T(8,128)(2,1)}, bf16[1024,256]{1,0:T(8,128)(2,1)}, u32[]{:S(2)}, u32[]{:S(2)}) collective-permute-start(bf16[1024,256]{1,0:T(8,128)(2,1)} %pad_maximum_fusion.1), channel_id=1, source_target_pairs={{0,4},{4,8},{8,12},{12,16},{16,20},{20,24},{24,28},{28,32},{32,36}... | collective-permute-start | bytes 1572872 | tf_op jit(solution)/shard_map/ppermute | solution.py:512
  35.2 7.3 %own_attention.1.own_ref = f32[1024,1024]{1,0:T(8,128)} custom-call(bf16[1024,512]{1,0:T(8,128)(2,1)} %q_ref.7, bf16[1024,512]{1,0:T(8,128)(2,1)} %ko_ref.3, bf16[1024,512]{1,0:T(8,128)(2,1)} %v_ref.1), custom_call_target="tpu_custom_call" | custom-call | flops 99999997952 | bytes 1000000 | tf_op jit(solution)/shard_map/own_attention/pallas_call | solution.py:285
  42.5 4.3 %collective-permute-done.1.kp_ref.vp_ref = bf16[1024,768]{1,0:T(8,128)(2,1)} collective-permute-done((bf16[1024,768]{1,0:T(8,128)(2,1)}, bf16[1024,768]{1,0:T(8,128)(2,1)}, u32[]{:S(2)}, u32[]{:S(2)}) %collective-permute-start.1) | collective-permute-done | bytes 1572896 | tf_op jit(solution)/shard_map/ppermute | solution.py:507
  46.8 11.9 %window_attention.2 = (f32[1024,512]{1,0:T(8,128)}, bf16[4,128,128]{2,1,0:T(8,128)(2,1)}) custom-call(s32[1]{0:T(128)} %bitcast.first_ref, bf16[1024,512]{1,0:T(8,128)(2,1)} %q_ref.7, bf16[1024,768]{1,0:T(8,128)(2,1)} %collective-permute-done.1.kp_ref.vp_ref, bf16[1024,512]{1,0:T(8,128)(2,1)} %ko_ref.3, ...), custom_call_target="tpu_custom_call" | custom-call | flops 99999997952 | bytes 1000000 | tf_op jit(solution)/shard_map/window_attention/pallas_call | solution.py:366
  58.7 0.0 all-to-all-done.d_ref
  58.7 1.9 %decay_prefix.1 = (bf16[8,144,128]{2,1,0:T(8,128)(2,1)S(1)}, bf16[144,128]{1,0:T(8,128)(2,1)S(1)}) custom-call(bf16[8,144,128]{2,1,0:T(8,128)(2,1)} %all-to-all-done.d_ref), custom_call_target="tpu_custom_call" | custom-call | flops 1000000 | bytes 1000000 | tf_op jit(solution)/shard_map/decay_prefix/pallas_call | solution.py:398
  60.6 2.1 %collective-permute-done.kp_ref.vp_ref = bf16[1024,256]{1,0:T(8,128)(2,1)} collective-permute-done((bf16[1024,256]{1,0:T(8,128)(2,1)}, bf16[1024,256]{1,0:T(8,128)(2,1)}, u32[]{:S(2)}, u32[]{:S(2)}) %collective-permute-start) | collective-permute-done | bytes 524320 | tf_op jit(solution)/shard_map/ppermute | solution.py:512
  62.7 5.9 %window_attention.3 = (f32[1024,512]{1,0:T(8,128)}, bf16[4,128,128]{2,1,0:T(8,128)(2,1)}) custom-call(s32[1]{0:T(128)} %bitcast.first_ref, bf16[1024,512]{1,0:T(8,128)(2,1)} %q_ref.7, bf16[1024,256]{1,0:T(8,128)(2,1)} %collective-permute-done.kp_ref.vp_ref, bf16[1024,512]{1,0:T(8,128)(2,1)} %ko_ref.3, ...), custom_call_target="tpu_custom_call", output_to_operand_aliasing={{0}: (11, {}), {1}: (12, {})} | custom-call | flops 99999997952 | bytes 1000000 | tf_op jit(solution)/shard_map/window_attention/pallas_call | solution.py:366
  68.6 15.6 %all_to_all.20.b_ref = bf16[8,64,128]{2,1,0:T(8,128)(2,1)S(1)} all-to-all(bf16[8,64,128]{2,1,0:T(8,128)(2,1)} %bitcast.5), channel_id=1, replica_groups={{0,4,8,12,16,20,24,28},{32,36,40,44,48,52,56,60},{64,68,72,76,80,84,88,..., dimensions={0} | all-to-all | bytes 262144 | tf_op jit(solution)/shard_map/all_to_all | solution.py:526
  84.2 1.8 %line_states.1 = (f32[8,64,128]{2,1,0:T(8,128)S(1)}, bf16[4,272,128]{2,1,0:T(8,128)(2,1)S(1)}) custom-call(bf16[8,144,128]{2,1,0:T(8,128)(2,1)} %all-to-all-done.d_ref, bf16[144,128]{1,0:T(8,128)(2,1)S(1)} %get-tuple-element.49.t_ref, bf16[8,64,128]{2,1,0:T(8,128)(2,1)S(1)} %all_to_all.20.b_ref), custom_call_target="tpu_custom_call" | custom-call | flops 1000000 | bytes 1000000 | tf_op jit(solution)/shard_map/line_states/pallas_call | solution.py:398
  86.0 9.9 %all_to_all.21.w_ref = bf16[4,272,128]{2,1,0:T(8,128)(2,1)S(1)} all-to-all(bf16[4,272,128]{2,1,0:T(8,128)(2,1)S(1)} %get-tuple-element.51), channel_id=1, replica_groups={{0,32,64,96},{4,36,68,100},{8,40,72,104},{12,44,76,108},{16,48,80,112},..., dimensions={0} | all-to-all | bytes 557056 | tf_op jit(solution)/shard_map/all_to_all | solution.py:532
  96.0 0.4 block_states.1
  96.4 12.1 %all_to_all.22 = bf16[8,64,128]{2,1,0:T(8,128)(2,1)} all-to-all(bf16[8,64,128]{2,1,0:T(8,128)(2,1)S(1)} %block_states.1), channel_id=1, replica_groups={{0,4,8,12,16,20,24,28},{32,36,40,44,48,52,56,60},{64,68,72,76,80,84,88,..., dimensions={0} | all-to-all | bytes 262144 | tf_op jit(solution)/shard_map/all_to_all | solution.py:534
  108.6 4.7 %gated_readout.1 = bf16[1024,512]{1,0:T(8,128)(2,1)} custom-call(f32[1024,512]{1,0:T(8,128)} %get-tuple-element.47.r_ref, bf16[8,4,128,256]{3,2,1,0:T(8,128)(2,1)} %get-tuple-element.48.qf_ref, bf16[4,128,128]{2,1,0:T(8,128)(2,1)} %bitcast.4, bf16[1024,512]{1,0:T(8,128)(2,1)} %gate_ref.1, f32[1,128]{1,0:T(1,128)} %bitcast.6), custom_call_target="tpu_custom_call" | custom-call | flops 140000000 | bytes 6000000 | tf_op jit(solution)/shard_map/gated_readout/pallas_call | solution.py:474
  (1 shorter events, 0.0 us)
Async XLA Ops:
  0.0 1.1 %slice-start = ((bf16[1024,512]{1,0:T(8,128)(2,1)}), bf16[1024,384]{1,0:T(8,128)(2,1)S(1)}, s32[]{:S(2)}) async-start(bf16[1024,512]{1,0:T(8,128)(2,1)} %v_ref.1), calls=%async_computation.4 | async-start | bytes 1572864 | tf_op jit(solution)/shard_map/slice | solution.py:505
  0.0 1.4 %slice-start.2 = ((bf16[1024,512]{1,0:T(8,128)(2,1)}), bf16[1024,384]{1,0:T(8,128)(2,1)S(1)}, s32[]{:S(2)}) async-start(bf16[1024,512]{1,0:T(8,128)(2,1)} %ko_ref.3), calls=%async_computation.6 | async-start | bytes 1572864 | tf_op jit(solution)/shard_map/slice | solution.py:505
  1.4 5.2 %slice-start.1 = ((bf16[1024,512]{1,0:T(8,128)(2,1)}), bf16[1024,128]{1,0:T(8,128)(2,1)S(1)}, s32[]{:S(2)}) async-start(bf16[1024,512]{1,0:T(8,128)(2,1)} %v_ref.1), calls=%async_computation.5 | async-start | bytes 524288 | tf_op jit(solution)/shard_map/slice | solution.py:505
  1.4 5.2 %slice-start.3 = ((bf16[1024,512]{1,0:T(8,128)(2,1)}), bf16[1024,128]{1,0:T(8,128)(2,1)S(1)}, s32[]{:S(2)}) async-start(bf16[1024,512]{1,0:T(8,128)(2,1)} %ko_ref.3), calls=%async_computation.7 | async-start | bytes 524288 | tf_op jit(solution)/shard_map/slice | solution.py:505
  2.7 44.1 %collective-permute-start.1 = (bf16[1024,768]{1,0:T(8,128)(2,1)}, bf16[1024,768]{1,0:T(8,128)(2,1)}, u32[]{:S(2)}, u32[]{:S(2)}) collective-permute-start(bf16[1024,768]{1,0:T(8,128)(2,1)} %pad_maximum_fusion), channel_id=1, source_target_pairs={{0,4},{4,8},{8,12},{12,16},{16,20},{20,24},{24,28},{28,32},{32,36}... | collective-permute-start | bytes 4718600 | tf_op jit(solution)/shard_map/ppermute | solution.py:507
  23.7 35.0 %all-to-all-start = ((bf16[8,144,128]{2,1,0:T(8,128)(2,1)}), bf16[8,144,128]{2,1,0:T(8,128)(2,1)}, u32[]{:S(2)}, u32[]{:S(2)}) async-start(bf16[8,144,128]{2,1,0:T(8,128)(2,1)} %get-tuple-element.37), calls=%async_computation | async-start | bytes 589824 | tf_op jit(solution)/shard_map/all_to_all | solution.py:514
  31.3 31.4 %collective-permute-start = (bf16[1024,256]{1,0:T(8,128)(2,1)}, bf16[1024,256]{1,0:T(8,128)(2,1)}, u32[]{:S(2)}, u32[]{:S(2)}) collective-permute-start(bf16[1024,256]{1,0:T(8,128)(2,1)} %pad_maximum_fusion.1), channel_id=1, source_target_pairs={{0,4},{4,8},{8,12},{12,16},{16,20},{20,24},{24,28},{28,32},{32,36}... | collective-permute-start | bytes 1572872 | tf_op jit(solution)/shard_map/ppermute | solution.py:512

commit v6 on v5

--- a/solution.py
+++ b/solution.py
@@ -388,7 +388,7 @@
         input_output_aliases={11 + n: n for n in range(len(earlier))},
         scratch_shapes=[pltpu.VMEM((window, DH), BF16), pltpu.VMEM((window, 2 * DH), BF16)],
         compiler_params=pltpu.CompilerParams(vmem_limit_bytes=MIDDLE),
-        cost_estimate=pl.CostEstimate(flops=100_000_000_000, bytes_accessed=1_000_000, transcendentals=0),
+        cost_estimate=pl.CostEstimate(flops=1_000_000 if earlier else 100_000_000_000, bytes_accessed=1_000_000, transcendentals=0),
         name="window_attention",
     )(first, att_query, kv_prev, k_own, kv_prev, own, m, ke, qe, e, g, *earlier)
 
@@ -505,23 +505,23 @@
         return beside(att_key[:, part], att_value[:, part])
 
     kv_first = lax.ppermute(both(0, last), "seq", onward)
-    m, ke, qe, qf, e, g, wire = prep(log_decay, beta, delta_key, delta_query, copies)
+    own = own_part(att_query, att_key, att_value)
     earlier = (jnp.arange(majors) < place // minor).astype(F32)
     earlier = jnp.broadcast_to(earlier[:, None], (majors, DH))
-    wire, kv_last, earlier = lax.optimization_barrier((wire, both(last, heads), earlier))
+    own, kv_last, delta_key, earlier = lax.optimization_barrier((own, both(last, heads), delta_key, earlier))
     kv_last = lax.ppermute(kv_last, "seq", onward)
+    m, ke, qe, qf, e, g, wire = prep(log_decay, beta, delta_key, delta_query, copies)
     lines = [[x * minor + z for z in range(minor)] for x in range(majors)]
     d_line = lax.all_to_all(wire, "seq", 0, 0, axis_index_groups=lines)
-    own = own_part(att_query, att_key, att_value)
     first = jnp.reshape((place == 0).astype(jnp.int32), (1,))
     coefs = (own, m, ke, qe, e, g)
     early = attend(0, first, att_query, kv_first, att_key, *coefs)
-    d_line, early = lax.optimization_barrier((d_line, early))
+    readout, b = attend(last, first, att_query, kv_last, att_key, *coefs, *early)
+    d_line, b = lax.optimization_barrier((d_line, b))
     p_line, d_total = vmem_call(
         prefix_kernel, [(d_line.shape, BF16), (d_line.shape[1:], BF16)], "decay_prefix", d_line
     )
-    early, p_line, d_total = lax.optimization_barrier((early, p_line, d_total))
-    readout, b = attend(last, first, att_query, kv_last, att_key, *coefs, *early)
+    b, p_line, d_total = lax.optimization_barrier((b, p_line, d_total))
     size = DH // copies
     b_line = lax.all_to_all(b.reshape(minor, size, DH), "seq", 0, 0, axis_index_groups=lines)
     q_line, added = vmem_call(

time: 115 us -> 112 us (0.974)
  blocking collectives: 37.7 us -> 40.2 us
  Pallas kernels: 50.2 us -> 48.2 us
  other arithmetic: 2.18 us -> 0.19 us
  waiting for transfers between devices: 6.35 us -> 5.09 us
    all_to_all x1, blocking collectives: 15.6 us -> 18.1 us  [body(): lax.all_to_all(b.reshape(minor, size, DH), 'seq', 0, 0, axis_index_groups...]
    ppermute x1, waiting for transfers between devices: 2.08 us -> 0.08 us  [body(): kv_last = lax.ppermute(kv_last, 'seq', onward)]
    concatenate x2, other arithmetic: 2.17 us -> 0.18 us  [beside(): return jnp.concatenate(parts, axis=1)]
    pallas_call x3, Pallas kernels: 4.18 us -> 2.25 us  [vmem_call(): pl.pallas_call(kernel, in_specs=[vm] * len(args), out_specs=[vm] * len(ou...]
  transfers between devices with their start and end apart: 3 -> 3, of which waited for: 2 -> 2; matrix products, arithmetic and copies ran while one was open for 1% -> 0% of each run, Pallas kernels for 33% -> 37%
where the time goes in v6:
time: 112 us; the launch traced here: 110 us
  Pallas kernels  48.2 us (43%)
  blocking collectives  40.2 us (36%)
  starting transfers between devices  14.5 us (13%)
  waiting for transfers between devices  5.09 us (5%)
  local copies, waits for them, and re-layouts  2.25 us (2%)
    all_to_all x1, blocking collectives, body(): lax.all_to_all(b.reshape(minor, size, DH), 'seq', 0, 0, axis_index_groups...  18.1 us
    pallas_call x2, Pallas kernels, attend(): pl.pallas_call(functools.partial(attend_kernel, base), grid=(held,), in_s...  17.8 us
    pallas_call x1, Pallas kernels, prep(): pl.pallas_call(functools.partial(prep_kernel, heads, PER), grid=(chunks /...  16.2 us
    all_to_all x1, blocking collectives, body(): lax.all_to_all(s_line, 'seq', 0, 0, axis_index_groups=lines)  12.1 us
    all_to_all x1, blocking collectives, body(): wires = lax.all_to_all(added, 'seq', 0, 0, axis_index_groups=columns)  9.94 us
    pallas_call x1, Pallas kernels, own_part(): pl.pallas_call(own_kernel, grid=(heads,), in_specs=[tok, tok, tok], out_s...  7.33 us
    all_to_all x1, starting transfers between devices, body(): d_line = lax.all_to_all(wire, 'seq', 0, 0, axis_index_groups=lines)  6.69 us
    ppermute x1, waiting for transfers between devices, body(): kv_first = lax.ppermute(both(0, last), 'seq', onward)  5.01 us
  transfers between devices with their start and end apart: 3, of which 2 were waited for; matrix products, arithmetic and copies ran while one was open for 0% of the time, Pallas kernels for 37%

profile of v6, /device:TPU:18, one launch (start us, length us, event | category | flops | bytes accessed | tf_op | source)
XLA Modules:
  0.0 110.5 jit_solution(6225914090900105194)
XLA Ops:
  0.0 0.0 slice-start.2
  0.0 0.0 slice-start
  0.0 1.1 %slice-done.2 = bf16[1024,384]{1,0:T(8,128)(2,1)S(1)} async-done(((bf16[1024,512]{1,0:T(8,128)(2,1)}), bf16[1024,384]{1,0:T(8,128)(2,1)S(1)}, s32[]{:S(2)}) %slice-start.2) | async-done | bytes 786456 | tf_op jit(solution)/shard_map/slice | solution.py:505
  1.1 0.2 slice-done
  1.4 0.1 pad_maximum_fusion
  1.5 0.0 slice-start.1
  1.5 0.0 slice-start.3
  1.5 4.0 %collective-permute-start.1 = (bf16[1024,768]{1,0:T(8,128)(2,1)S(1)}, bf16[1024,768]{1,0:T(8,128)(2,1)}, u32[]{:S(2)}, u32[]{:S(2)}) collective-permute-start(bf16[1024,768]{1,0:T(8,128)(2,1)S(1)} %pad_maximum_fusion), channel_id=1, source_target_pairs={{0,4},{4,8},{8,12},{12,16},{16,20},{20,24},{24,28},{28,32},{32,36}... | collective-permute-start | bytes 4718600 | tf_op jit(solution)/shard_map/ppermute | solution.py:507
  5.5 7.3 %own_attention.1.own_ref = f32[1024,1024]{1,0:T(8,128)} custom-call(bf16[1024,512]{1,0:T(8,128)(2,1)} %q_ref.7, bf16[1024,512]{1,0:T(8,128)(2,1)} %ko_ref.3, bf16[1024,512]{1,0:T(8,128)(2,1)} %v_ref.1), custom_call_target="tpu_custom_call" | custom-call | flops 99999997952 | bytes 1000000 | tf_op jit(solution)/shard_map/own_attention/pallas_call | solution.py:285
  12.8 0.0 slice-done.1
  12.8 0.0 slice-done.3
  12.8 0.1 pad_maximum_fusion.1
  12.9 0.1 broadcast_in_dim.2.earlier_ref
  13.0 3.8 %collective-permute-start = (bf16[1024,256]{1,0:T(8,128)(2,1)S(1)}, bf16[1024,256]{1,0:T(8,128)(2,1)S(1)}, u32[]{:S(2)}, u32[]{:S(2)}) collective-permute-start(bf16[1024,256]{1,0:T(8,128)(2,1)S(1)} %pad_maximum_fusion.1), channel_id=1, source_target_pairs={{0,4},{4,8},{8,12},{12,16},{16,20},{20,24},{24,28},{28,32},{32,36}... | collective-permute-start | bytes 1572872 | tf_op jit(solution)/shard_map/ppermute | solution.py:512
  16.8 16.2 %delta_prep.1 = (bf16[8,4,128,128]{3,2,1,0:T(8,128)(2,1)}, bf16[8,4,128,256]{3,2,1,0:T(8,128)(2,1)}, bf16[8,4,128,128]{3,2,1,0:T(8,128)(2,1)}, bf16[8,4,128,256]...) custom-call(f32[4,1024]{1,0:T(4,128)} %ld_ref.1, ...), custom_call_target="tpu_custom_call" | custom-call | flops 1000000 | bytes 1000000 | tf_op jit(solution)/shard_map/delta_prep/pallas_call | solution.py:236
  33.0 6.7 %all-to-all-start = ((bf16[8,144,128]{2,1,0:T(8,128)(2,1)}), bf16[8,144,128]{2,1,0:T(8,128)(2,1)S(1)}, u32[]{:S(2)}, u32[]{:S(2)}) async-start(bf16[8,144,128]{2,1,0:T(8,128)(2,1)} %get-tuple-element.41), calls=%async_computation | async-start | bytes 589824 | tf_op jit(solution)/shard_map/all_to_all | solution.py:515
  39.7 5.0 %collective-permute-done.1.kp_ref.vp_ref = bf16[1024,768]{1,0:T(8,128)(2,1)} collective-permute-done((bf16[1024,768]{1,0:T(8,128)(2,1)S(1)}, bf16[1024,768]{1,0:T(8,128)(2,1)}, u32[]{:S(2)}, u32[]{:S(2)}) %collective-permute-start.1) | collective-permute-done | bytes 1572896 | tf_op jit(solution)/shard_map/ppermute | solution.py:507
  44.7 11.9 %window_attention.2 = (f32[1024,512]{1,0:T(8,128)}, bf16[4,128,128]{2,1,0:T(8,128)(2,1)}) custom-call(s32[1]{0:T(128)} %bitcast.first_ref, bf16[1024,512]{1,0:T(8,128)(2,1)} %q_ref.7, bf16[1024,768]{1,0:T(8,128)(2,1)} %collective-permute-done.1.kp_ref.vp_ref, bf16[1024,512]{1,0:T(8,128)(2,1)} %ko_ref.3, ...), custom_call_target="tpu_custom_call" | custom-call | flops 99999997952 | bytes 1000000 | tf_op jit(solution)/shard_map/window_attention/pallas_call | solution.py:366
  56.6 0.1 collective-permute-done.kp_ref.vp_ref
  56.7 0.0 copy-start
  56.7 0.8 copy-done
  57.5 5.9 %window_attention.3 = (f32[1024,512]{1,0:T(8,128)}, bf16[4,128,128]{2,1,0:T(8,128)(2,1)}) custom-call(s32[1]{0:T(128)} %bitcast.first_ref, bf16[1024,512]{1,0:T(8,128)(2,1)} %q_ref.7, bf16[1024,256]{1,0:T(8,128)(2,1)} %copy-done, bf16[1024,512]{1,0:T(8,128)(2,1)} %ko_ref.3, ...), custom_call_target="tpu_custom_call", output_to_operand_aliasing={{0}: (11, {}), {1}: (12, {})} | custom-call | flops 1000000 | bytes 1000000 | tf_op jit(solution)/shard_map/window_attention/pallas_call | solution.py:366
  63.4 0.0 all-to-all-done.d_ref
  63.4 1.0 decay_prefix.1
  64.3 18.1 %all_to_all.20.b_ref = bf16[8,64,128]{2,1,0:T(8,128)(2,1)S(1)} all-to-all(bf16[8,64,128]{2,1,0:T(8,128)(2,1)} %bitcast.4), channel_id=1, replica_groups={{0,4,8,12,16,20,24,28},{32,36,40,44,48,52,56,60},{64,68,72,76,80,84,88,..., dimensions={0} | all-to-all | bytes 262144 | tf_op jit(solution)/shard_map/all_to_all | solution.py:526
  82.4 0.8 line_states.1
  83.3 9.9 %all_to_all.21.w_ref = bf16[4,272,128]{2,1,0:T(8,128)(2,1)S(1)} all-to-all(bf16[4,272,128]{2,1,0:T(8,128)(2,1)S(1)} %get-tuple-element.49), channel_id=1, replica_groups={{0,32,64,96},{4,36,68,100},{8,40,72,104},{12,44,76,108},{16,48,80,112},..., dimensions={0} | all-to-all | bytes 557056 | tf_op jit(solution)/shard_map/all_to_all | solution.py:532
  93.2 0.4 block_states.1
  93.7 12.1 %all_to_all.22 = bf16[8,64,128]{2,1,0:T(8,128)(2,1)} all-to-all(bf16[8,64,128]{2,1,0:T(8,128)(2,1)S(1)} %block_states.1), channel_id=1, replica_groups={{0,4,8,12,16,20,24,28},{32,36,40,44,48,52,56,60},{64,68,72,76,80,84,88,..., dimensions={0} | all-to-all | bytes 262144 | tf_op jit(solution)/shard_map/all_to_all | solution.py:534
  105.8 4.7 %gated_readout.1 = bf16[1024,512]{1,0:T(8,128)(2,1)} custom-call(f32[1024,512]{1,0:T(8,128)} %get-tuple-element.39.r_ref, bf16[8,4,128,256]{3,2,1,0:T(8,128)(2,1)} %get-tuple-element.40.qf_ref, bf16[4,128,128]{2,1,0:T(8,128)(2,1)} %bitcast.5, bf16[1024,512]{1,0:T(8,128)(2,1)} %gate_ref.1, f32[1,128]{1,0:T(1,128)} %bitcast.6), custom_call_target="tpu_custom_call" | custom-call | flops 140000000 | bytes 6000000 | tf_op jit(solution)/shard_map/gated_readout/pallas_call | solution.py:474
  (1 shorter events, 0.0 us)
Async XLA Ops:
  0.0 1.1 %slice-start.2 = ((bf16[1024,512]{1,0:T(8,128)(2,1)}), bf16[1024,384]{1,0:T(8,128)(2,1)S(1)}, s32[]{:S(2)}) async-start(bf16[1024,512]{1,0:T(8,128)(2,1)} %v_ref.1), calls=%async_computation.6 | async-start | bytes 1572864 | tf_op jit(solution)/shard_map/slice | solution.py:505
  0.0 1.4 %slice-start = ((bf16[1024,512]{1,0:T(8,128)(2,1)}), bf16[1024,384]{1,0:T(8,128)(2,1)S(1)}, s32[]{:S(2)}) async-start(bf16[1024,512]{1,0:T(8,128)(2,1)} %ko_ref.3), calls=%async_computation.4 | async-start | bytes 1572864 | tf_op jit(solution)/shard_map/slice | solution.py:505
  1.5 11.3 %slice-start.1 = ((bf16[1024,512]{1,0:T(8,128)(2,1)}), bf16[1024,128]{1,0:T(8,128)(2,1)S(1)}, s32[]{:S(2)}) async-start(bf16[1024,512]{1,0:T(8,128)(2,1)} %ko_ref.3), calls=%async_computation.5 | async-start | bytes 524288 | tf_op jit(solution)/shard_map/slice | solution.py:505
  1.5 11.3 %slice-start.3 = ((bf16[1024,512]{1,0:T(8,128)(2,1)}), bf16[1024,128]{1,0:T(8,128)(2,1)S(1)}, s32[]{:S(2)}) async-start(bf16[1024,512]{1,0:T(8,128)(2,1)} %v_ref.1), calls=%async_computation.7 | async-start | bytes 524288 | tf_op jit(solution)/shard_map/slice | solution.py:505
  1.5 43.2 %collective-permute-start.1 = (bf16[1024,768]{1,0:T(8,128)(2,1)S(1)}, bf16[1024,768]{1,0:T(8,128)(2,1)}, u32[]{:S(2)}, u32[]{:S(2)}) collective-permute-start(bf16[1024,768]{1,0:T(8,128)(2,1)S(1)} %pad_maximum_fusion), channel_id=1, source_target_pairs={{0,4},{4,8},{8,12},{12,16},{16,20},{20,24},{24,28},{28,32},{32,36}... | collective-permute-start | bytes 4718600 | tf_op jit(solution)/shard_map/ppermute | solution.py:507
  13.0 43.7 %collective-permute-start = (bf16[1024,256]{1,0:T(8,128)(2,1)S(1)}, bf16[1024,256]{1,0:T(8,128)(2,1)S(1)}, u32[]{:S(2)}, u32[]{:S(2)}) collective-permute-start(bf16[1024,256]{1,0:T(8,128)(2,1)S(1)} %pad_maximum_fusion.1), channel_id=1, source_target_pairs={{0,4},{4,8},{8,12},{12,16},{16,20},{20,24},{24,28},{28,32},{32,36}... | collective-permute-start | bytes 1572872 | tf_op jit(solution)/shard_map/ppermute | solution.py:512
  33.0 30.3 %all-to-all-start = ((bf16[8,144,128]{2,1,0:T(8,128)(2,1)}), bf16[8,144,128]{2,1,0:T(8,128)(2,1)S(1)}, u32[]{:S(2)}, u32[]{:S(2)}) async-start(bf16[8,144,128]{2,1,0:T(8,128)(2,1)} %get-tuple-element.41), calls=%async_computation | async-start | bytes 589824 | tf_op jit(solution)/shard_map/all_to_all | solution.py:515
  56.7 0.8 copy-start

commit v7 on v6

--- a/solution.py
+++ b/solution.py
@@ -14,6 +14,7 @@
 VMEM = 60 * 2**20
 MIDDLE = 58 * 2**20
 SMALL = 8 * 2**20
+LATER = 50 * 2**20
 NEG = -1e30
 F32 = jnp.float32
 BF16 = jnp.bfloat16
@@ -387,7 +388,7 @@
         ],
         input_output_aliases={11 + n: n for n in range(len(earlier))},
         scratch_shapes=[pltpu.VMEM((window, DH), BF16), pltpu.VMEM((window, 2 * DH), BF16)],
-        compiler_params=pltpu.CompilerParams(vmem_limit_bytes=MIDDLE),
+        compiler_params=pltpu.CompilerParams(vmem_limit_bytes=LATER if earlier else MIDDLE),
         cost_estimate=pl.CostEstimate(flops=1_000_000 if earlier else 100_000_000_000, bytes_accessed=1_000_000, transcendentals=0),
         name="window_attention",
     )(first, att_query, kv_prev, k_own, kv_prev, own, m, ke, qe, e, g, *earlier)

time: 112 us -> 113 us (level)
  transfers between devices with their start and end apart: 3 -> 3, of which waited for: 2 -> 1; matrix products, arithmetic and copies ran while one was open for 0% -> 1% of each run, Pallas kernels for 37% -> 37%
where the time goes in v7:
time: 113 us; the launch traced here: 111 us
  Pallas kernels  48.1 us (43%)
  blocking collectives  40.1 us (35%)
  starting transfers between devices  14.5 us (13%)
  waiting for transfers between devices  4.21 us (4%)
  local copies, waits for them, and re-layouts  3.02 us (3%)
    all_to_all x1, blocking collectives, body(): lax.all_to_all(b.reshape(minor, size, DH), 'seq', 0, 0, axis_index_groups...  18 us
    pallas_call x2, Pallas kernels, attend(): pl.pallas_call(functools.partial(attend_kernel, base), grid=(held,), in_s...  17.7 us
    pallas_call x1, Pallas kernels, prep(): pl.pallas_call(functools.partial(prep_kernel, heads, PER), grid=(chunks /...  16.2 us
    all_to_all x1, blocking collectives, body(): lax.all_to_all(s_line, 'seq', 0, 0, axis_index_groups=lines)  12.1 us
    all_to_all x1, blocking collectives, body(): wires = lax.all_to_all(added, 'seq', 0, 0, axis_index_groups=columns)  9.93 us
    pallas_call x1, Pallas kernels, own_part(): pl.pallas_call(own_kernel, grid=(heads,), in_specs=[tok, tok, tok], out_s...  7.33 us
    all_to_all x1, starting transfers between devices, body(): d_line = lax.all_to_all(wire, 'seq', 0, 0, axis_index_groups=lines)  6.69 us
    pallas_call x1, Pallas kernels, finish(): pl.pallas_call(functools.partial(finish_kernel, heads), grid=(rows // (PE...  4.66 us
  transfers between devices with their start and end apart: 3, of which 1 were waited for; matrix products, arithmetic and copies ran while one was open for 1% of the time, Pallas kernels for 37%

profile of v7, /device:TPU:18, one launch (start us, length us, event | category | flops | bytes accessed | tf_op | source)
XLA Modules:
  0.0 111.0 jit_solution(6637066931588399015)
XLA Ops:
  0.0 1.1 %slice-done.2 = bf16[1024,384]{1,0:T(8,128)(2,1)S(1)} async-done(((bf16[1024,512]{1,0:T(8,128)(2,1)}), bf16[1024,384]{1,0:T(8,128)(2,1)S(1)}, s32[]{:S(2)}) %slice-start.2) | async-done | bytes 786456 | tf_op jit(solution)/shard_map/slice | solution.py:506
  1.1 0.2 slice-done
  1.4 0.1 pad_maximum_fusion
  1.5 0.0 slice-start.1
  1.5 0.0 slice-start.3
  1.5 4.0 %collective-permute-start.1 = (bf16[1024,768]{1,0:T(8,128)(2,1)S(1)}, bf16[1024,768]{1,0:T(8,128)(2,1)}, u32[]{:S(2)}, u32[]{:S(2)}) collective-permute-start(bf16[1024,768]{1,0:T(8,128)(2,1)S(1)} %pad_maximum_fusion), channel_id=1, source_target_pairs={{0,4},{4,8},{8,12},{12,16},{16,20},{20,24},{24,28},{28,32},{32,36}... | collective-permute-start | bytes 4718600 | tf_op jit(solution)/shard_map/ppermute | solution.py:508
  5.5 7.3 %own_attention.1.own_ref = f32[1024,1024]{1,0:T(8,128)} custom-call(bf16[1024,512]{1,0:T(8,128)(2,1)} %q_ref.7, bf16[1024,512]{1,0:T(8,128)(2,1)} %ko_ref.3, bf16[1024,512]{1,0:T(8,128)(2,1)} %v_ref.1), custom_call_target="tpu_custom_call" | custom-call | flops 99999997952 | bytes 1000000 | tf_op jit(solution)/shard_map/own_attention/pallas_call | solution.py:286
  12.8 0.0 slice-done.1
  12.8 0.0 slice-done.3
  12.8 0.9 pad_maximum_fusion.1
  13.7 0.1 broadcast_in_dim.2.earlier_ref
  13.8 3.8 %collective-permute-start = (bf16[1024,256]{1,0:T(8,128)(2,1)}, bf16[1024,256]{1,0:T(8,128)(2,1)S(1)}, u32[]{:S(2)}, u32[]{:S(2)}) collective-permute-start(bf16[1024,256]{1,0:T(8,128)(2,1)} %pad_maximum_fusion.1), channel_id=1, source_target_pairs={{0,4},{4,8},{8,12},{12,16},{16,20},{20,24},{24,28},{28,32},{32,36}... | collective-permute-start | bytes 1572872 | tf_op jit(solution)/shard_map/ppermute | solution.py:513
  17.6 16.2 %delta_prep.1 = (bf16[8,4,128,128]{3,2,1,0:T(8,128)(2,1)}, bf16[8,4,128,256]{3,2,1,0:T(8,128)(2,1)}, bf16[8,4,128,128]{3,2,1,0:T(8,128)(2,1)}, bf16[8,4,128,256]...) custom-call(f32[4,1024]{1,0:T(4,128)} %ld_ref.1, ...), custom_call_target="tpu_custom_call" | custom-call | flops 1000000 | bytes 1000000 | tf_op jit(solution)/shard_map/delta_prep/pallas_call | solution.py:237
  33.8 6.7 %all-to-all-start = ((bf16[8,144,128]{2,1,0:T(8,128)(2,1)}), bf16[8,144,128]{2,1,0:T(8,128)(2,1)S(1)}, u32[]{:S(2)}, u32[]{:S(2)}) async-start(bf16[8,144,128]{2,1,0:T(8,128)(2,1)} %get-tuple-element.41), calls=%async_computation | async-start | bytes 589824 | tf_op jit(solution)/shard_map/all_to_all | solution.py:516
  40.5 4.2 %collective-permute-done.1.kp_ref.vp_ref = bf16[1024,768]{1,0:T(8,128)(2,1)} collective-permute-done((bf16[1024,768]{1,0:T(8,128)(2,1)S(1)}, bf16[1024,768]{1,0:T(8,128)(2,1)}, u32[]{:S(2)}, u32[]{:S(2)}) %collective-permute-start.1) | collective-permute-done | bytes 1572896 | tf_op jit(solution)/shard_map/ppermute | solution.py:508
  44.7 12.0 %window_attention.2 = (f32[1024,512]{1,0:T(8,128)}, bf16[4,128,128]{2,1,0:T(8,128)(2,1)}) custom-call(s32[1]{0:T(128)} %bitcast.first_ref, bf16[1024,512]{1,0:T(8,128)(2,1)} %q_ref.7, bf16[1024,768]{1,0:T(8,128)(2,1)} %collective-permute-done.1.kp_ref.vp_ref, bf16[1024,512]{1,0:T(8,128)(2,1)} %ko_ref.3, ...), custom_call_target="tpu_custom_call" | custom-call | flops 99999997952 | bytes 1000000 | tf_op jit(solution)/shard_map/window_attention/pallas_call | solution.py:367
  56.7 0.0 collective-permute-done.kp_ref.vp_ref
  56.8 0.0 copy-done
  56.8 0.0 copy-done.1
  56.8 0.0 copy-done.2
  56.8 0.0 copy-done.5
  56.8 0.9 copy-done.3
  57.7 5.7 %window_attention.3 = (f32[1024,512]{1,0:T(8,128)}, bf16[4,128,128]{2,1,0:T(8,128)(2,1)S(1)}) custom-call(s32[1]{0:T(128)} %bitcast.first_ref, bf16[1024,512]{1,0:T(8,128)(2,1)S(1)} %copy-done.1, bf16[1024,256]{1,0:T(8,128)(2,1)S(1)} %collective-permute-done.kp_ref.vp_ref, ...), custom_call_target="tpu_custom_call", output_to_operand_aliasing={{0}: (11, {}), {1}: (12, {})} | custom-call | flops 1000000 | bytes 1000000 | tf_op jit(solution)/shard_map/window_attention/pallas_call | solution.py:367
  63.4 0.7 copy-done.4
  64.0 0.0 all-to-all-done.d_ref
  64.0 1.0 decay_prefix.1
  65.0 18.0 %all_to_all.20.b_ref = bf16[8,64,128]{2,1,0:T(8,128)(2,1)S(1)} all-to-all(bf16[8,64,128]{2,1,0:T(8,128)(2,1)} %bitcast.4), channel_id=1, replica_groups={{0,4,8,12,16,20,24,28},{32,36,40,44,48,52,56,60},{64,68,72,76,80,84,88,..., dimensions={0} | all-to-all | bytes 262144 | tf_op jit(solution)/shard_map/all_to_all | solution.py:527
  83.0 0.8 line_states.1
  83.9 9.9 %all_to_all.21.w_ref = bf16[4,272,128]{2,1,0:T(8,128)(2,1)S(1)} all-to-all(bf16[4,272,128]{2,1,0:T(8,128)(2,1)S(1)} %get-tuple-element.49), channel_id=1, replica_groups={{0,32,64,96},{4,36,68,100},{8,40,72,104},{12,44,76,108},{16,48,80,112},..., dimensions={0} | all-to-all | bytes 557056 | tf_op jit(solution)/shard_map/all_to_all | solution.py:533
  93.8 0.4 block_states.1
  94.2 12.1 %all_to_all.22 = bf16[8,64,128]{2,1,0:T(8,128)(2,1)} all-to-all(bf16[8,64,128]{2,1,0:T(8,128)(2,1)S(1)} %block_states.1), channel_id=1, replica_groups={{0,4,8,12,16,20,24,28},{32,36,40,44,48,52,56,60},{64,68,72,76,80,84,88,..., dimensions={0} | all-to-all | bytes 262144 | tf_op jit(solution)/shard_map/all_to_all | solution.py:535
  106.4 4.7 %gated_readout.1 = bf16[1024,512]{1,0:T(8,128)(2,1)} custom-call(f32[1024,512]{1,0:T(8,128)} %get-tuple-element.39.r_ref, bf16[8,4,128,256]{3,2,1,0:T(8,128)(2,1)} %get-tuple-element.40.qf_ref, bf16[4,128,128]{2,1,0:T(8,128)(2,1)} %bitcast.5, bf16[1024,512]{1,0:T(8,128)(2,1)} %gate_ref.1, f32[1,128]{1,0:T(1,128)} %bitcast.6), custom_call_target="tpu_custom_call" | custom-call | flops 140000000 | bytes 6000000 | tf_op jit(solution)/shard_map/gated_readout/pallas_call | solution.py:475
  (9 shorter events, 0.0 us)
Async XLA Ops:
  0.0 1.1 %slice-start.2 = ((bf16[1024,512]{1,0:T(8,128)(2,1)}), bf16[1024,384]{1,0:T(8,128)(2,1)S(1)}, s32[]{:S(2)}) async-start(bf16[1024,512]{1,0:T(8,128)(2,1)} %v_ref.1), calls=%async_computation.6 | async-start | bytes 1572864 | tf_op jit(solution)/shard_map/slice | solution.py:506
  0.0 1.4 %slice-start = ((bf16[1024,512]{1,0:T(8,128)(2,1)}), bf16[1024,384]{1,0:T(8,128)(2,1)S(1)}, s32[]{:S(2)}) async-start(bf16[1024,512]{1,0:T(8,128)(2,1)} %ko_ref.3), calls=%async_computation.4 | async-start | bytes 1572864 | tf_op jit(solution)/shard_map/slice | solution.py:506
  1.5 11.3 %slice-start.1 = ((bf16[1024,512]{1,0:T(8,128)(2,1)}), bf16[1024,128]{1,0:T(8,128)(2,1)S(1)}, s32[]{:S(2)}) async-start(bf16[1024,512]{1,0:T(8,128)(2,1)} %ko_ref.3), calls=%async_computation.5 | async-start | bytes 524288 | tf_op jit(solution)/shard_map/slice | solution.py:506
  1.5 11.3 %slice-start.3 = ((bf16[1024,512]{1,0:T(8,128)(2,1)}), bf16[1024,128]{1,0:T(8,128)(2,1)S(1)}, s32[]{:S(2)}) async-start(bf16[1024,512]{1,0:T(8,128)(2,1)} %v_ref.1), calls=%async_computation.7 | async-start | bytes 524288 | tf_op jit(solution)/shard_map/slice | solution.py:506
  1.5 43.2 %collective-permute-start.1 = (bf16[1024,768]{1,0:T(8,128)(2,1)S(1)}, bf16[1024,768]{1,0:T(8,128)(2,1)}, u32[]{:S(2)}, u32[]{:S(2)}) collective-permute-start(bf16[1024,768]{1,0:T(8,128)(2,1)S(1)} %pad_maximum_fusion), channel_id=1, source_target_pairs={{0,4},{4,8},{8,12},{12,16},{16,20},{20,24},{24,28},{28,32},{32,36}... | collective-permute-start | bytes 4718600 | tf_op jit(solution)/shard_map/ppermute | solution.py:508
  13.8 43.0 %collective-permute-start = (bf16[1024,256]{1,0:T(8,128)(2,1)}, bf16[1024,256]{1,0:T(8,128)(2,1)S(1)}, u32[]{:S(2)}, u32[]{:S(2)}) collective-permute-start(bf16[1024,256]{1,0:T(8,128)(2,1)} %pad_maximum_fusion.1), channel_id=1, source_target_pairs={{0,4},{4,8},{8,12},{12,16},{16,20},{20,24},{24,28},{28,32},{32,36}... | collective-permute-start | bytes 1572872 | tf_op jit(solution)/shard_map/ppermute | solution.py:513
  33.8 30.2 %all-to-all-start = ((bf16[8,144,128]{2,1,0:T(8,128)(2,1)}), bf16[8,144,128]{2,1,0:T(8,128)(2,1)S(1)}, u32[]{:S(2)}, u32[]{:S(2)}) async-start(bf16[8,144,128]{2,1,0:T(8,128)(2,1)} %get-tuple-element.41), calls=%async_computation | async-start | bytes 589824 | tf_op jit(solution)/shard_map/all_to_all | solution.py:516
  44.7 12.0 %copy-start = (bf16[1024,512]{1,0:T(8,128)(2,1)S(1)}, bf16[1024,512]{1,0:T(8,128)(2,1)}, u32[]{:S(2)}) copy-start(bf16[1024,512]{1,0:T(8,128)(2,1)} %ko_ref.3) | copy-start | bytes 3145732
  44.7 12.0 %copy-start.1 = (bf16[1024,512]{1,0:T(8,128)(2,1)S(1)}, bf16[1024,512]{1,0:T(8,128)(2,1)}, u32[]{:S(2)}) copy-start(bf16[1024,512]{1,0:T(8,128)(2,1)} %q_ref.7) | copy-start | bytes 3145732
  44.7 12.1 %copy-start.2 = (bf16[8,4,128,128]{3,2,1,0:T(8,128)(2,1)S(1)}, bf16[8,4,128,128]{3,2,1,0:T(8,128)(2,1)}, u32[]{:S(2)}) copy-start(bf16[8,4,128,128]{3,2,1,0:T(8,128)(2,1)} %get-tuple-element.32.m_ref) | copy-start | bytes 3145732
  44.7 12.1 %copy-start.5 = (f32[8,4,128]{2,1,0:T(4,128)S(1)}, f32[8,4,128]{2,1,0:T(4,128)}, u32[]{:S(2)}) copy-start(f32[8,4,128]{2,1,0:T(4,128)} %get-tuple-element.36.g_ref) | copy-start | bytes 49156
  56.8 0.9 copy-start.3
  63.4 0.7 copy-start.4
